TPU v7x, 32 devices: a whole 2x2x4 slice. The times are simulated.
32 devices in a mesh: along: 8 (over y, x, core), cross: 4 (over z).
Axes of the slice: x: 2, y: 2, z: 4, core: 2. Of those that a mesh axis runs over, the one named last changes fastest.
Arguments:
- nadir_view: bfloat16 [2048, 6144], P('along', 'cross'), may hold values from -36 to 36
- forward: bfloat16 [2048, 6144], P('along', 'cross'), may hold values from -36 to 36
- backward: bfloat16 [2048, 6144], P('along', 'cross'), may hold values from -36 to 36
- along_weights: bfloat16 [2, 4, 2048], replicated, may hold values from 0.049804688 to 0.5
- cross_weights: bfloat16 [2, 4, 6144], P(None, None, 'cross'), may hold values from 0.049804688 to 0.5
- band_offsets: int32 [2, 2048], replicated, may hold values from -6 to 6, as said below
- col_offsets: int32 [2, 6144], P(None, 'cross'), may hold values from -6 to 6, as said below
- lag_lines: int32 [2048], replicated, may hold values from 21504 to 21519, as said below
- window_start: int32 [1], replicated, may hold values from 0 to 2095104
Outputs:
- parallax: bfloat16 [2, 2048, 6144], P(None, 'along', 'cross')
- normal_gram: float32 [8, 256, 256], P('along', 'cross')
- normal_rhs: float32 [8, 256], P('along', 'cross')
Inputs may be any that keep to these rules, and one draw needn't show every extreme that they name: `lag_lines`: every value in the range occurs in each draw. `band_offsets`: both ends of the range occur in each draw. `col_offsets`: both ends of the range occur in each draw.
All inputs are finite; a program needn't handle non-finite values.
Results may differ from a plain program's by a relative error of at most 0.0065.
Values may be sent and summed in bfloat16 or wider, within the bound.
No kernel may reach another device: no remote copies, remote signals or barrier semaphores. Data moves between devices by JAX's collectives and lax.ppermute only.
A program may use at most 64 MiB of HBM per device.

v0:
```python
import jax
import jax.numpy as jnp
from jax import lax
from jax.sharding import PartitionSpec as P

TAPS = 4
CAMERA_LAG = 20480
BOX = 4
MODES = 64
LINE_RIM = 32
COL_RIM = 9


def shifted(value, axis, steps):
    count = lax.axis_size(axis)
    pairs = [(source, (source + steps) % count) for source in range(count)]
    return lax.ppermute(value, axis, pairs)


def extended(cells, sides, width):
    for axis, dim in sides:
        count = lax.axis_size(axis)
        ends = count - 1
        head = lax.slice_in_dim(cells, 0, width, axis=dim)
        tail = lax.slice_in_dim(cells, cells.shape[dim] - width, cells.shape[dim], axis=dim)
        cells = jnp.concatenate(
            [
                lax.ppermute(tail, axis, [(i, (i + 1) % count) for i in range(ends)]),
                cells,
                lax.ppermute(head, axis, [((i + 1) % count, i) for i in range(ends)]),
            ],
            axis=dim,
        )
    return cells


def harmonics(absolute):
    period = 4 * MODES
    factor = 2 * jnp.arange(MODES, dtype=jnp.int32) + 1
    phases = (absolute % period)[:, None] * factor[None, :] % period
    angles = phases.astype(jnp.float32) * (2.0 * jnp.pi / period)
    return jnp.concatenate([jnp.cos(angles), jnp.sin(angles)], axis=1)


def box_mean(values, count):
    running = values[0:count]
    for offset in range(1, 2 * BOX + 1):
        running = running + values[offset : offset + count]
    return running / (2 * BOX + 1)


def shift_slabs(lead_part, trail_part, distance):
    lead_moved = shifted(lead_part, "along", distance)
    trail_moved = shifted(trail_part, "along", -distance)
    return (lead_moved, trail_moved)


def line_margin(stacked):
    height = stacked.shape[1]
    from_below = shifted(stacked[:, height - LINE_RIM :], "along", 1)
    from_above = shifted(stacked[:, :LINE_RIM], "along", -1)
    return jnp.concatenate([from_below, stacked, from_above], axis=1)


def column_margin(stacked):
    return extended(stacked, (("cross", 2),), COL_RIM)


def margins(stacked):
    return column_margin(line_margin(stacked))


def along_resample(slab_ext, tap_weights, row_start):
    positions = jnp.arange(slab_ext.shape[0], dtype=jnp.int32)
    distance = positions[None, :] - row_start[:, None]
    banded = jnp.zeros(distance.shape, jnp.bfloat16)
    for tap_index in range(TAPS):
        banded = jnp.where(distance == tap_index, tap_weights[tap_index][:, None], banded)
    return jnp.dot(banded, slab_ext, preferred_element_type=jnp.float32).astype(jnp.bfloat16)


def cross_resample(along_ext, tap_weights, col_shift):
    out_width = col_shift.shape[0]
    tile_count = out_width // 128
    window = 128 + 2 * COL_RIM
    positions = jnp.arange(window, dtype=jnp.int32)
    starts = (
        COL_RIM + jnp.arange(128, dtype=jnp.int32)[None, :] + col_shift.reshape(tile_count, 128)
    )
    distance = positions[None, :, None] - starts[:, None, :]
    banded = jnp.zeros(distance.shape, jnp.bfloat16)
    for tap_index in range(TAPS):
        banded = jnp.where(
            distance == tap_index, tap_weights[tap_index].reshape(tile_count, 1, 128), banded
        )
    pieces = jnp.stack(
        [
            along_ext[:, tile_index * 128 : tile_index * 128 + window]
            for tile_index in range(tile_count)
        ]
    )
    product = jnp.einsum("qla,qaj->lqj", pieces, banded, preferred_element_type=jnp.float32)
    return product.reshape(along_ext.shape[0], out_width).astype(jnp.bfloat16)


def local(
    nadir_view,
    forward,
    backward,
    along_weights,
    cross_weights,
    band_offsets,
    col_offsets,
    lag_lines,
    window_start,
):
    lines_dev, cols_dev = nadir_view.shape
    along_count = lax.axis_size("along")
    cross_count = lax.axis_size("cross")
    along_index = lax.axis_index("along")
    cross_index = lax.axis_index("cross")
    total_lines = lines_dev * along_count
    total_cols = cols_dev * cross_count
    lag_blocks = along_count // 2
    lag_floor = CAMERA_LAG // total_lines * total_lines + lag_blocks * lines_dev
    lead_moved, trail_moved = shift_slabs(forward, backward, lag_blocks)
    widened = margins(jnp.stack([nadir_view, lead_moved, trail_moved]))
    nadir_full, lead_full, trail_full = (widened[0], widened[1], widened[2])
    local_lines = jnp.arange(-BOX, lines_dev + BOX, dtype=jnp.int32)
    wrapped = (along_index * lines_dev + local_lines) % total_lines
    lag_excess = jnp.take(lag_lines, wrapped) - lag_floor
    lead_start = LINE_RIM + local_lines - lag_excess + jnp.take(band_offsets[0], wrapped)
    trail_start = LINE_RIM + local_lines + lag_excess + jnp.take(band_offsets[1], wrapped)
    lead_along = along_resample(lead_full, jnp.take(along_weights[0], wrapped, axis=1), lead_start)
    trail_along = along_resample(
        trail_full, jnp.take(along_weights[1], wrapped, axis=1), trail_start
    )
    lead_res = cross_resample(lead_along, cross_weights[0], col_offsets[0])
    trail_res = cross_resample(trail_along, cross_weights[1], col_offsets[1])
    framed = nadir_full[
        LINE_RIM - BOX - 1 : LINE_RIM + lines_dev + BOX + 1, COL_RIM - 1 : COL_RIM + cols_dev + 1
    ].astype(jnp.float32)
    slopes = (
        framed[2:, :-2]
        + 2.0 * framed[2:, 1:-1]
        + framed[2:, 2:]
        - framed[:-2, :-2]
        - 2.0 * framed[:-2, 1:-1]
        - framed[:-2, 2:]
    ) / 4.0
    center = framed[1:-1, 1:-1]
    texture = box_mean(slopes * slopes, lines_dev)
    divisor = jnp.maximum(texture, 0.4)
    lead_est = -box_mean(slopes * (lead_res.astype(jnp.float32) - center), lines_dev) / divisor
    trail_est = -box_mean(slopes * (trail_res.astype(jnp.float32) - center), lines_dev) / divisor
    parallax = jnp.stack([lead_est, trail_est]).astype(jnp.bfloat16)
    disagree = lead_est + trail_est
    columns = cross_index * cols_dev + jnp.arange(cols_dev, dtype=jnp.int32)
    position = (columns.astype(jnp.float32) + 0.5) / total_cols + 0.25
    lever_two = position * position
    lever_three = lever_two * position
    lever_four = lever_two * lever_two
    scale_sum = 1.0 / (lines_dev * total_cols)
    scale_pull = 1.0 / (lines_dev * total_cols) ** 0.5
    line_terms = jnp.stack(
        [
            jnp.sum(texture * lever_two[None, :], axis=1) * scale_sum,
            jnp.sum(texture * lever_three[None, :], axis=1) * scale_sum,
            jnp.sum(texture * lever_four[None, :], axis=1) * scale_sum,
            jnp.sum(texture * disagree * position[None, :], axis=1) * scale_pull,
            jnp.sum(texture * disagree * lever_two[None, :], axis=1) * scale_pull,
        ]
    )
    basis_lines = harmonics(
        window_start[0] + along_index * lines_dev + jnp.arange(lines_dev, dtype=jnp.int32)
    )
    summed = lax.psum(line_terms, "cross")
    row_count = 4 * MODES // cross_count
    row_first = cross_index * row_count
    upper_rows = row_first + jnp.arange(row_count, dtype=jnp.int32) >= 2 * MODES
    doubled = jnp.concatenate([basis_lines, basis_lines], axis=1)
    basis_rows = lax.dynamic_slice_in_dim(doubled, row_first, row_count, 1)
    left_coef = jnp.where(upper_rows[None, :], summed[1][:, None], summed[0][:, None])
    right_coef = jnp.where(upper_rows[None, :], summed[2][:, None], summed[1][:, None])
    pull_coef = jnp.where(upper_rows[None, :], summed[4][:, None], summed[3][:, None])
    gram_rows = jnp.concatenate(
        [
            jnp.dot((basis_rows * left_coef).T, basis_lines, precision=lax.Precision.HIGHEST),
            jnp.dot((basis_rows * right_coef).T, basis_lines, precision=lax.Precision.HIGHEST),
        ],
        axis=1,
    )
    rhs_rows = jnp.sum(basis_rows * pull_coef, axis=0)
    normal_gram = gram_rows[None]
    normal_rhs = rhs_rows[None]
    return (parallax, normal_gram, normal_rhs)


def solution(mesh):
    placed = (
        P("along", "cross"),
        P("along", "cross"),
        P("along", "cross"),
        P(),
        P(None, None, "cross"),
        P(),
        P(None, "cross"),
        P(),
        P(),
    )
    return jax.shard_map(
        local,
        mesh=mesh,
        in_specs=placed,
        out_specs=(P(None, "along", "cross"), P("along", "cross", None), P("along", "cross")),
        check_vma=False,
    )
```

profile of v0, /device:TPU:0, one launch (start us, length us, event | category | flops | bytes accessed | tf_op | source)
XLA Modules:
  0.0 97.9 jit_solution(17160775110576314804)
XLA Ops:
  0.6 0.0 copy-start
  0.6 3.0 %collective-permute-start = (bf16[256,1536]{1,0:T(8,128)(2,1)}, bf16[256,1536]{1,0:T(8,128)(2,1)S(1)}, u32[]{:S(2)}, u32[]{:S(2)}) collective-permute-start(bf16[256,1536]{1,0:T(8,128)(2,1)} %param.14), channel_id=1, source_target_pairs={{0,16},{4,20},{8,24},{12,28},{16,0},{20,4},{24,8},{28,12},{1,17},{... | collective-permute-start | bytes 2359304 | tf_op jit(solution)/shard_map/ppermute | solution.py:17
  3.7 0.1 collective-permute-start.1
  3.9 0.8 fusion.162
  4.6 0.3 copy.30
  4.9 0.3 copy.31
  5.3 1.4 %gather_fusion.2 = bf16[264,4]{1,0:T(8,128)(2,1)S(1)} fusion(bf16[4,2048]{0,1:T(8,128)(2,1)S(1)} %bitcast.174, s32[1024]{0:T(1024)S(1)} %pad_clamp_fusion), kind=kCustom, calls=%fused_computation.1.clone | custom fusion | bytes 5280 | tf_op jit(solution)/shard_map/jit(_take)/gather | solution.py:134
  6.6 1.4 %gather_fusion.4 = bf16[264,4]{1,0:T(8,128)(2,1)S(1)} fusion(bf16[4,2048]{0,1:T(8,128)(2,1)S(1)} %bitcast.175, s32[1024]{0:T(1024)S(1)} %pad_clamp_fusion), kind=kCustom, calls=%fused_computation.4.clone | custom fusion | bytes 5280 | tf_op jit(solution)/shard_map/jit(_take)/gather | solution.py:136
  8.0 0.8 fusion.163
  8.8 2.2 %gather_fusion.1 = s32[264]{0:T(512)S(1)} fusion(s32[2048]{0:T(1024)S(1)} %bitcast.165, s32[1024]{0:T(1024)S(1)} %pad_clamp_fusion), kind=kCustom, calls=%fused_computation.2.clone | custom fusion | bytes 3168 | tf_op jit(solution)/shard_map/jit(_take)/gather | solution.py:132
  11.1 0.0 copy-start.5
  11.1 0.0 copy-start.6
  11.1 2.2 %gather_fusion.3 = s32[264]{0:T(512)S(1)} fusion(s32[2048]{0:T(1024)S(1)} %bitcast.164, s32[1024]{0:T(1024)S(1)} %pad_clamp_fusion), kind=kCustom, calls=%fused_computation.3.clone | custom fusion | bytes 3168 | tf_op jit(solution)/shard_map/jit(_take)/gather | solution.py:133
  13.3 0.0 copy-start.1
  13.3 2.2 %gather_fusion = s32[264]{0:T(512)S(1)} fusion(s32[2048]{0:T(1024)S(1)} %copy-done, s32[1024]{0:T(1024)S(1)} %pad_clamp_fusion), kind=kCustom, calls=%fused_computation.clone | custom fusion | bytes 3168 | tf_op jit(solution)/shard_map/jit(_take)/gather | solution.py:131
  15.6 0.1 slice_reduce_fusion.16
  16.5 0.1 select_bitcast_fusion
  16.6 0.5 slice_reduce_fusion.3
  17.1 5.2 %collective-permute-done = bf16[256,1536]{1,0:T(8,128)(2,1)S(1)} collective-permute-done((bf16[256,1536]{1,0:T(8,128)(2,1)}, bf16[256,1536]{1,0:T(8,128)(2,1)S(1)}, u32[]{:S(2)}, u32[]{:S(2)}) %collective-permute-start) | collective-permute-done | bytes 786464 | tf_op jit(solution)/shard_map/ppermute | solution.py:17
  22.3 16.0 %collective-permute-done.1 = bf16[256,1536]{1,0:T(8,128)(2,1)S(1)} collective-permute-done((bf16[256,1536]{1,0:T(8,128)(2,1)}, bf16[256,1536]{1,0:T(8,128)(2,1)S(1)}, u32[]{:S(2)}, u32[]{:S(2)}) %collective-permute-start.1) | collective-permute-done | bytes 786464 | tf_op jit(solution)/shard_map/ppermute | solution.py:17
  38.3 0.1 collective-permute-start.2
  38.4 2.6 %collective-permute-start.3 = (bf16[3,32,1536]{2,1,0:T(8,128)(2,1)S(1)}, bf16[3,32,1536]{2,1,0:T(8,128)(2,1)S(1)}, u32[]{:S(2)}, u32[]{:S(2)}) collective-permute-start(bf16[3,32,1536]{2,1,0:T(8,128)(2,1)S(1)} %get-tuple-element.39), channel_id=1, source_target_pairs={{0,28},{4,0},{8,4},{12,8},{16,12},{20,16},{24,20},{28,24},{1,29},{... | collective-permute-start | bytes 884744 | tf_op jit(solution)/shard_map/ppermute | solution.py:17
  41.0 0.3 fusion.128
  41.4 5.1 %collective-permute-done.2 = bf16[3,32,1536]{2,1,0:T(8,128)(2,1)S(1)} collective-permute-done((bf16[3,32,1536]{2,1,0:T(8,128)(2,1)S(1)}, bf16[3,32,1536]{2,1,0:T(8,128)(2,1)S(1)}, u32[]{:S(2)}, u32[]{:S(2)}) %collective-permute-start.2) | collective-permute-done | bytes 294944 | tf_op jit(solution)/shard_map/ppermute | solution.py:17
  46.5 0.0 copy-done.4
  46.5 0.5 collective-permute-done.3
  46.9 1.5 %pad_maximum_fusion = bf16[3,320,1536]{2,1,0:T(8,128)(2,1)S(1)} fusion(bf16[3,32,1536]{2,1,0:T(8,128)(2,1)S(1)} %collective-permute-done.3, bf16[1,256,1536]{2,1,0:T(8,128)(2,1)} %bitcast.171, bf16[1,256,1536]{2,1,0:T(8,128)(2,1)} %bitcast.169, bf16[1,256,1536]{2,1,0:T(8,128)(2,1)S(1)} %bitcast.167, bf16[3,32,1536]{2,1,0:T(8,128)(2,1)S(1)} %collective-permute-done.2), kind=kLoop, calls=%fused_computation.5 | loop fusion | flops 14745600 | bytes 5898240 | tf_op jit(solution)/shard_map/concatenate | solution.py:62
  48.4 0.9 fusion.161
  49.3 3.5 %collective-permute-start.4 = (bf16[3,320,9]{2,1,0:T(8,128)(2,1)}, bf16[3,320,9]{2,1,0:T(8,128)(2,1)S(1)}, u32[]{:S(2)}, u32[]{:S(2)}) collective-permute-start(bf16[3,320,9]{2,1,0:T(8,128)(2,1)} %get-tuple-element.37), channel_id=1, source_target_pairs={{0,1},{1,2},{2,3},{4,5},{5,6},{6,7},{8,9},{9,10},{10,11},{12,13},{... | collective-permute-start | bytes 51848 | tf_op jit(solution)/shard_map/ppermute | solution.py:28
  52.8 1.5 %collective-permute-start.5 = (bf16[3,320,9]{2,1,0:T(8,128)(2,1)}, bf16[3,320,9]{2,1,0:T(8,128)(2,1)}, u32[]{:S(2)}, u32[]{:S(2)}) collective-permute-start(bf16[3,320,9]{2,1,0:T(8,128)(2,1)} %get-tuple-element.36), channel_id=1, source_target_pairs={{1,0},{2,1},{3,2},{5,4},{6,5},{7,6},{9,8},{10,9},{11,10},{13,12},{... | collective-permute-start | bytes 51848 | tf_op jit(solution)/shard_map/ppermute | solution.py:30
  54.3 4.4 %collective-permute-done.4 = bf16[3,320,9]{2,1,0:T(8,128)(2,1)S(1)} collective-permute-done((bf16[3,320,9]{2,1,0:T(8,128)(2,1)}, bf16[3,320,9]{2,1,0:T(8,128)(2,1)S(1)}, u32[]{:S(2)}, u32[]{:S(2)}) %collective-permute-start.4) | collective-permute-done | bytes 17312 | tf_op jit(solution)/shard_map/ppermute | solution.py:28
  58.7 4.7 %collective-permute-done.5 = bf16[3,320,9]{2,1,0:T(8,128)(2,1)} collective-permute-done((bf16[3,320,9]{2,1,0:T(8,128)(2,1)}, bf16[3,320,9]{2,1,0:T(8,128)(2,1)}, u32[]{:S(2)}, u32[]{:S(2)}) %collective-permute-start.5) | collective-permute-done | bytes 17312 | tf_op jit(solution)/shard_map/ppermute | solution.py:30
  63.4 6.0 %concatenate.17 = bf16[3,320,1554]{2,1,0:T(8,128)(2,1)} concatenate(bf16[3,320,9]{2,1,0:T(8,128)(2,1)S(1)} %collective-permute-done.4, bf16[3,320,1536]{2,1,0:T(8,128)(2,1)S(1)} %pad_maximum_fusion, bf16[3,320,9]{2,1,0:T(8,128)(2,1)} %collective-permute-done.5), dimensions={2} | concatenate | bytes 5967360 | tf_op jit(solution)/shard_map/concatenate | solution.py:26
  69.3 1.3 %slice_bitcast_fusion.4 = bf16[320,1554]{1,0:T(8,128)(2,1)S(1)} fusion(bf16[3,320,1554]{2,1,0:T(8,128)(2,1)} %concatenate.17), kind=kLoop, calls=%fused_computation.63 | loop fusion | bytes 1989120 | tf_op jit(solution)/shard_map/squeeze | solution.py:128
  70.7 2.0 %convolution_convert_fusion = bf16[264,1554]{1,0:T(8,128)(2,1)S(1)} fusion(bf16[3,320,1554]{2,1,0:T(8,128)(2,1)} %concatenate.17, s32[264]{0:T(512)S(1)} %get-tuple-element.49, bf16[264]{0:T(512)(128)(2,1)S(1)} %get-tuple-element.15, bf16[264]{0:T(512)(128)(2,1)S(1)} %get-tuple-element.16, bf16[264]{0:T(512)(128)(2,1)S(1)} %get-tuple-element.17, ...), kind=kOutput, calls=%fused_computation.6 | convolution fusion | flops 263734416 | bytes 1888640 | tf_op jit(solution)/shard_map/dot_general | solution.py:79
  72.9 2.0 %convolution_convert_fusion.1 = bf16[264,1554]{1,0:T(8,128)(2,1)S(1)} fusion(bf16[3,320,1554]{2,1,0:T(8,128)(2,1)} %concatenate.17, s32[264]{0:T(512)S(1)} %get-tuple-element.50, bf16[264]{0:T(512)(128)(2,1)S(1)} %get-tuple-element.63, bf16[264]{0:T(512)(128)(2,1)S(1)} %get-tuple-element.62, bf16[264]{0:T(512)(128)(2,1)S(1)} %get-tuple-element.61, ...), kind=kOutput, calls=%fused_computation.7 | convolution fusion | flops 263734416 | bytes 1888640 | tf_op jit(solution)/shard_map/dot_general | solution.py:79
  75.2 0.4 slice_convert_fusion
  75.6 0.6 convert_bitcast_fusion.1
  76.3 2.2 %fusion.1 = (f32[264,1536]{1,0:T(8,128)S(1)}, f32[264,1536]{1,0:T(8,128)S(1)}) fusion(f32[12,33,8,128]{3,2,1,0:T(8,128)S(1)} %convert_bitcast_fusion.1, f32[266,1538]{1,0:T(8,128)S(1)} %slice_convert_fusion), kind=kLoop, calls=%fused_computation.11 | loop fusion | flops 4055040 | bytes 16220160 | tf_op jit(solution)/shard_map/mul | solution.py:154
  78.4 0.6 convert_bitcast_fusion
  79.1 0.7 fusion
  79.7 4.7 %multiply_reduce_fusion = (f32[256]{0:T(256)S(1)}, f32[256]{0:T(256)S(1)}, f32[256]{0:T(256)S(1)}, f32[256]{0:T(256)S(1)}, f32[256]{0:T(256)S(1)}, /*index=5*/bf...) fusion(f32[1536]{0:T(1024)S(1)} %get-tuple-element.60, f32[1536]{0:T(1024)S(1)} %get-tuple-element.59, ...), kind=kLoop, calls=%fused_computation.53 | loop fusion | flops 18086656 | bytes 44076032 | tf_op jit(solution)/shard_map/reduce_sum | solution.py:171
  84.6 10.1 %psum.7 = f32[5,256]{1,0:T(8,128)S(1)} all-reduce(f32[5,256]{1,0:T(8,128)S(1)} %stack.143), channel_id=1, replica_groups=mesh['along'=8,'cross'=4] {'cross'}, use_global_device_ids=true, to_apply=%region_5.8 | all-reduce | flops 1280 | bytes 10240 | tf_op jit(solution)/shard_map/psum | solution.py:177
  94.7 0.7 multiply_reduce_fusion.5
  95.4 0.3 fusion.102
  95.7 0.3 fusion.101
  96.0 0.6 maximum_bitcast_fusion
  96.6 1.3 %pad_maximum_fusion.1 = bf16[2,256,1536]{2,1,0:T(8,128)(2,1)} fusion(bf16[1,256,1536]{2,1,0:T(8,128)(2,1)S(1)} %bitcast.173, bf16[1,256,1536]{2,1,0:T(8,128)(2,1)S(1)} %bitcast.172), kind=kLoop, calls=%fused_computation.52 | loop fusion | flops 786432 | bytes 3145728 | tf_op jit(solution)/shard_map/stack | solution.py:156
  (54 shorter events, 0.5 us)
Async XLA Ops:
  0.6 12.7 %copy-start = (s32[2048]{0:T(1024)S(1)}, s32[2048]{0:T(1024)}, u32[]{:S(2)}) copy-start(s32[2048]{0:T(1024)} %param.20) | copy-start | bytes 24580
  0.6 21.6 %collective-permute-start = (bf16[256,1536]{1,0:T(8,128)(2,1)}, bf16[256,1536]{1,0:T(8,128)(2,1)S(1)}, u32[]{:S(2)}, u32[]{:S(2)}) collective-permute-start(bf16[256,1536]{1,0:T(8,128)(2,1)} %param.14), channel_id=1, source_target_pairs={{0,16},{4,20},{8,24},{12,28},{16,0},{20,4},{24,8},{28,12},{1,17},{... | collective-permute-start | bytes 2359304 | tf_op jit(solution)/shard_map/ppermute | solution.py:17
  3.7 34.6 %collective-permute-start.1 = (bf16[256,1536]{1,0:T(8,128)(2,1)}, bf16[256,1536]{1,0:T(8,128)(2,1)S(1)}, u32[]{:S(2)}, u32[]{:S(2)}) collective-permute-start(bf16[256,1536]{1,0:T(8,128)(2,1)} %param.15), channel_id=1, source_target_pairs={{0,16},{4,20},{8,24},{12,28},{16,0},{20,4},{24,8},{28,12},{1,17},{... | collective-permute-start | bytes 2359304 | tf_op jit(solution)/shard_map/ppermute | solution.py:17
  11.1 4.5 %copy-start.5 = (bf16[2,4,1536]{2,1,0:T(4,128)(2,1)S(1)}, bf16[2,4,1536]{2,1,0:T(4,128)(2,1)}, u32[]{:S(2)}) copy-start(bf16[2,4,1536]{2,1,0:T(4,128)(2,1)} %param.17) | copy-start | bytes 73732
  11.1 4.7 %copy-start.6 = (s32[2,1536]{1,0:T(2,128)S(1)}, s32[2,1536]{1,0:T(2,128)}, u32[]{:S(2)}) copy-start(s32[2,1536]{1,0:T(2,128)} %param.19) | copy-start | bytes 36868
  13.3 25.0 %copy-start.1 = (bf16[256,1536]{1,0:T(8,128)(2,1)S(1)}, bf16[256,1536]{1,0:T(8,128)(2,1)}, u32[]{:S(2)}) copy-start(bf16[256,1536]{1,0:T(8,128)(2,1)} %param.13) | copy-start | bytes 2359300
  17.1 29.9 %copy-start.2 = (bf16[256,1536]{1,0:T(8,128)(2,1)S(1)}, bf16[256,1536]{1,0:T(8,128)(2,1)}, u32[]{:S(2)}) copy-start(bf16[256,1536]{1,0:T(8,128)(2,1)} %param.13) | copy-start | bytes 2359300
  22.3 24.2 %copy-start.3 = (bf16[256,1536]{1,0:T(8,128)(2,1)}, bf16[256,1536]{1,0:T(8,128)(2,1)S(1)}, u32[]{:S(2)}) copy-start(bf16[256,1536]{1,0:T(8,128)(2,1)S(1)} %collective-permute-done) | copy-start | bytes 2359300
  38.3 8.2 %copy-start.4 = (bf16[256,1536]{1,0:T(8,128)(2,1)}, bf16[256,1536]{1,0:T(8,128)(2,1)S(1)}, u32[]{:S(2)}) copy-start(bf16[256,1536]{1,0:T(8,128)(2,1)S(1)} %collective-permute-done.1) | copy-start | bytes 2359300
  38.3 8.1 %collective-permute-start.2 = (bf16[3,32,1536]{2,1,0:T(8,128)(2,1)S(1)}, bf16[3,32,1536]{2,1,0:T(8,128)(2,1)S(1)}, u32[]{:S(2)}, u32[]{:S(2)}) collective-permute-start(bf16[3,32,1536]{2,1,0:T(8,128)(2,1)S(1)} %get-tuple-element.38), channel_id=1, source_target_pairs={{0,4},{4,8},{8,12},{12,16},{16,20},{20,24},{24,28},{28,0},{1,5},{5... | collective-permute-start | bytes 884744 | tf_op jit(solution)/shard_map/ppermute | solution.py:17
  38.4 8.5 %collective-permute-start.3 = (bf16[3,32,1536]{2,1,0:T(8,128)(2,1)S(1)}, bf16[3,32,1536]{2,1,0:T(8,128)(2,1)S(1)}, u32[]{:S(2)}, u32[]{:S(2)}) collective-permute-start(bf16[3,32,1536]{2,1,0:T(8,128)(2,1)S(1)} %get-tuple-element.39), channel_id=1, source_target_pairs={{0,28},{4,0},{8,4},{12,8},{16,12},{20,16},{24,20},{28,24},{1,29},{... | collective-permute-start | bytes 884744 | tf_op jit(solution)/shard_map/ppermute | solution.py:17
  49.3 9.4 %collective-permute-start.4 = (bf16[3,320,9]{2,1,0:T(8,128)(2,1)}, bf16[3,320,9]{2,1,0:T(8,128)(2,1)S(1)}, u32[]{:S(2)}, u32[]{:S(2)}) collective-permute-start(bf16[3,320,9]{2,1,0:T(8,128)(2,1)} %get-tuple-element.37), channel_id=1, source_target_pairs={{0,1},{1,2},{2,3},{4,5},{5,6},{6,7},{8,9},{9,10},{10,11},{12,13},{... | collective-permute-start | bytes 51848 | tf_op jit(solution)/shard_map/ppermute | solution.py:28
  52.8 10.6 %collective-permute-start.5 = (bf16[3,320,9]{2,1,0:T(8,128)(2,1)}, bf16[3,320,9]{2,1,0:T(8,128)(2,1)}, u32[]{:S(2)}, u32[]{:S(2)}) collective-permute-start(bf16[3,320,9]{2,1,0:T(8,128)(2,1)} %get-tuple-element.36), channel_id=1, source_target_pairs={{1,0},{2,1},{3,2},{5,4},{6,5},{7,6},{9,8},{10,9},{11,10},{13,12},{... | collective-permute-start | bytes 51848 | tf_op jit(solution)/shard_map/ppermute | solution.py:30
where the time goes:
time: 98.8 us; the launch traced here: 97.9 us
  waiting for transfers between devices  35.8 us (36%)
  local copies, waits for them, and re-layouts  20.7 us (21%)
  other arithmetic  12.7 us (13%)
  starting transfers between devices  10.8 us (11%)
  blocking collectives  10.1 us (10%)
  matrix products  5.91 us (6%)
  between operations  1.82 us (2%)
    ppermute x4, waiting for transfers between devices, shifted(): return lax.ppermute(value, axis, pairs)  26.7 us
    psum x1, blocking collectives, local(): summed = lax.psum(line_terms, 'cross')  10.1 us
    concatenate x1, local copies, waits for them, and re-layouts, extended(): jnp.concatenate([lax.ppermute(tail, axis, [(i, (i + 1) % count) for i in...  5.96 us
    ppermute x4, starting transfers between devices, shifted(): return lax.ppermute(value, axis, pairs)  5.8 us
    reduce_sum x1, other arithmetic, local(): jnp.sum(texture * disagree * lever_two[None, :], axis=1) * scale_pull  4.75 us
    ppermute x1, waiting for transfers between devices, extended(): lax.ppermute(head, axis, [((i + 1) % count, i) for i in range(ends)])  4.73 us
    ppermute x1, waiting for transfers between devices, extended(): lax.ppermute(tail, axis, [(i, (i + 1) % count) for i in range(ends)])  4.38 us
    dot_general x2, matrix products, along_resample(): jnp.dot(banded, slab_ext, preferred_element_type=jnp.float32)  4.06 us
  transfers between devices with their start and end apart: 6, of which 6 were waited for; matrix products, arithmetic and copies ran while one was open for 13% of the time, Pallas kernels for 0%

commit v1 on v0

v1 whole, which is shorter than its diff:
```python
import functools

import jax
import jax.numpy as jnp
from jax import lax
from jax.experimental import pallas as pl
from jax.experimental.pallas import tpu as pltpu
from jax.sharding import PartitionSpec as P

TAPS = 4
CAMERA_LAG = 20480
BOX = 4
MODES = 64
LINE_RIM = 32
NADIR_RIM = 16
TILE = 128
WIDE = 256


def pairs_of(count, step):
    return [(i, i + step) for i in range(count) if 0 <= i + step < count]


def harmonics(absolute):
    period = 4 * MODES
    factor = 2 * jnp.arange(MODES, dtype=jnp.int32) + 1
    phases = (absolute % period)[:, None] * factor[None, :] % period
    angles = phases.astype(jnp.float32) * (2.0 * jnp.pi / period)
    return jnp.concatenate([jnp.cos(angles), jnp.sin(angles)], axis=1)


def box_sum(x, lines):
    rows = x.shape[0]
    two = x + pltpu.roll(x, rows - 1, 0)
    four = two + pltpu.roll(two, rows - 2, 0)
    eight = four + pltpu.roll(four, rows - 4, 0)
    return eight[:lines] + x[2 * BOX : lines + 2 * BOX]


def lane_fold(x):
    folded = x[:, :TILE]
    for at in range(TILE, x.shape[1], TILE):
        folded = folded + x[:, at : at + TILE]
    return folded


def prep_kernel(
    lines, cols, nadir, left, right, above, below, line_params, pos,
    slopes, center, texture, inverse, sums, bands, framed,
):
    tall = lines + 2 * NADIR_RIM
    rows = lines + 16
    framed[0:NADIR_RIM, :] = above[...]
    framed[NADIR_RIM + lines : tall, :] = below[...]
    framed[NADIR_RIM : NADIR_RIM + lines, 0:TILE] = left[...]
    framed[NADIR_RIM : NADIR_RIM + lines, TILE : TILE + cols] = nadir[...]
    framed[NADIR_RIM : NADIR_RIM + lines, TILE + cols :] = right[...]
    row = lax.broadcasted_iota(jnp.int32, (2 * WIDE, WIDE), 0)
    col = lax.broadcasted_iota(jnp.int32, (2 * WIDE, WIDE), 1)
    gap = jnp.abs(row - TILE - col)
    smear = jnp.where(gap == 0, 2.0, jnp.where(gap == 1, 1.0, 0.0)).astype(jnp.bfloat16)
    totals = [jnp.zeros((lines, TILE), jnp.float32) for _ in range(3)]
    for at in range(0, cols, WIDE):
        across = jnp.dot(
            framed[:, at : at + 2 * WIDE], smear, preferred_element_type=jnp.float32
        )
        change = pltpu.roll(across, tall - 5, 0) - pltpu.roll(across, tall - 3, 0)
        slope = change[8 : 8 + rows] * 0.25
        slopes[:, at : at + WIDE] = slope
        middle = framed[:, TILE + at : TILE + at + WIDE].astype(jnp.float32)
        center[:, at : at + WIDE] = pltpu.roll(middle, tall - 4, 0)[8 : 8 + rows]
        level = box_sum(slope * slope, lines) * (1.0 / (2 * BOX + 1))
        texture[:, at : at + WIDE] = level
        inverse[:, at : at + WIDE] = (-1.0 / (2 * BOX + 1)) / jnp.maximum(level, 0.4)
        for k in range(3):
            totals[k] = totals[k] + lane_fold(level * pos[k + 1 : k + 2, at : at + WIDE])
    lane = lax.broadcasted_iota(jnp.int32, (lines, TILE), 1)
    packed = jnp.zeros((lines, TILE), jnp.float32)
    for k in range(3):
        packed = jnp.where(lane == k, jnp.sum(totals[k], axis=1, keepdims=True), packed)
    sums[...] = packed
    half = lines // 2
    depth = half + 2 * LINE_RIM
    for s in range(2):
        for first, last in ((0, half), (half, rows)):
            at = lax.broadcasted_iota(jnp.int32, (last - first, depth), 1).astype(jnp.float32)
            distance = at + float(first) - line_params[first:last, 5 * s : 5 * s + 1]
            band = jnp.zeros((last - first, depth), jnp.float32)
            for tap in range(TAPS):
                weight = line_params[first:last, 5 * s + 1 + tap : 5 * s + 2 + tap]
                band = jnp.where(distance == float(tap), weight, band)
            bands[s, first:last, :] = band.astype(jnp.bfloat16)


def slab_kernel(
    lines, cols, s, first, width, spans, fresh,
    slopes, center, texture, inverse, bands, col_params, pos, basis, earlier,
    above, below, left, right, edges, ends, *rest,
):
    count = len(spans)
    interiors = rest[:count]
    rest = rest[count + (0 if fresh else 1) :]
    parallax, pulled, ext, along, slope_v, center_v, texture_v, inverse_v, result, sem = rest
    rows = lines + 16
    half = lines // 2
    depth = half + 2 * LINE_RIM
    low, high = first, first + width + 2 * TILE
    copies = []

    def fetch(source, target):
        copy = pltpu.make_async_copy(source, target, sem.at[len(copies)])
        copy.start()
        copies.append(copy)

    def place(ref, lead, row, span, height, begin, end):
        a, b = max(begin, low), min(end, high)
        if a < b:
            fetch(
                ref.at[lead + (pl.ds(row, height), pl.ds(a - begin + span[0], b - a))],
                ext.at[pl.ds(span[1], height), pl.ds(a - low, b - a)],
            )

    whole = cols + 2 * TILE
    place(above, (s,), 0, (0, 0), LINE_RIM, 0, whole)
    place(below, (s,), 0, (0, LINE_RIM + lines), LINE_RIM, 0, whole)
    place(left, (s,), 0, (0, LINE_RIM), lines, 0, TILE)
    place(edges, (s,), 0, (0, LINE_RIM), lines, TILE, 2 * TILE)
    place(ends, (s,), 0, (0, LINE_RIM), LINE_RIM, 2 * TILE, cols)
    place(ends, (s,), LINE_RIM, (0, lines), LINE_RIM, 2 * TILE, cols)
    place(edges, (s,), 0, (TILE, LINE_RIM), lines, cols, cols + TILE)
    place(right, (s,), 0, (0, LINE_RIM), lines, cols + TILE, whole)
    for ref, (begin, end) in zip(interiors, spans):
        place(ref, (), 0, (0, 2 * LINE_RIM), lines - 2 * LINE_RIM, begin, end)
    loaded = len(copies)
    columns = pl.ds(first, width)
    fetch(slopes.at[:, columns], slope_v)
    fetch(center.at[:, columns], center_v)
    fetch(inverse.at[:, columns], inverse_v)
    fetch(texture.at[:, columns], texture_v)
    for copy in copies[:loaded]:
        copy.wait()
    for at in range(0, width + 2 * TILE, WIDE):
        end = min(at + WIDE, width + 2 * TILE)
        for start, stop in ((0, half), (half, rows)):
            along[start:stop, at:end] = jnp.dot(
                bands[s, start:stop, :],
                ext[start : start + depth, at:end],
                preferred_element_type=jnp.float32,
            ).astype(jnp.bfloat16)
    for copy in copies[loaded:]:
        copy.wait()
    pulls = [jnp.zeros((lines, TILE), jnp.float32) for _ in range(2)]
    for at in range(0, width, WIDE):
        span = min(WIDE, width - at)
        place_of = slice(first + at, first + at + span)
        row = lax.broadcasted_iota(jnp.int32, (span + 2 * TILE, span), 0)
        col = lax.broadcasted_iota(jnp.int32, (span + 2 * TILE, span), 1)
        distance = (row - col - TILE).astype(jnp.float32) - col_params[8 * s : 8 * s + 1, place_of]
        band = jnp.zeros((span + 2 * TILE, span), jnp.float32)
        for tap in range(TAPS):
            weight = col_params[8 * s + 1 + tap : 8 * s + 2 + tap, place_of]
            band = jnp.where(distance == float(tap), weight, band)
        resampled = jnp.dot(
            along[:, at : at + span + 2 * TILE],
            band.astype(jnp.bfloat16),
            preferred_element_type=jnp.float32,
        ).astype(jnp.bfloat16)
        here = slice(at, at + span)
        mismatch = resampled.astype(jnp.float32) - center_v[:, here]
        estimate = box_sum(slope_v[:, here] * mismatch, lines) * inverse_v[:, here]
        result[:, here] = estimate.astype(jnp.bfloat16)
        weighted = texture_v[:, here] * estimate
        for k in range(2):
            pulls[k] = pulls[k] + lane_fold(weighted * pos[k : k + 1, place_of])
    out = pltpu.make_async_copy(result, parallax.at[s, :, columns], sem.at[len(copies)])
    out.start()
    pulled[...] = earlier[...]
    for k in range(2):
        per_line = jnp.sum(pulls[k], axis=1, keepdims=True)
        pulled[k : k + 1, :] += jnp.sum(basis[...] * per_line, axis=0, keepdims=True)
    out.wait()


def local(
    nadir_view, forward, backward, along_weights, cross_weights, band_offsets, col_offsets,
    lag_lines, window_start,
):
    lines, cols = nadir_view.shape
    along_count = lax.axis_size("along")
    cross_count = lax.axis_size("cross")
    along_index = lax.axis_index("along")
    cross_index = lax.axis_index("cross")
    total_lines = lines * along_count
    total_cols = cols * cross_count
    half_ring = along_count // 2
    lag_floor = CAMERA_LAG // total_lines * total_lines + half_ring * lines
    rows = lines + 16
    whole = cols + 2 * TILE
    low_z, high_z = pairs_of(cross_count, -1), pairs_of(cross_count, 1)
    ring_down = [(i, (i - 1) % along_count) for i in range(along_count)]
    ring_up = [(i, (i + 1) % along_count) for i in range(along_count)]
    half_down, half_up = [], []
    for i in range(along_count):
        base = i // half_ring * half_ring
        half_down.append((i, base + (i - base - 1) % half_ring))
        half_up.append((i, base + (i - base + 1) % half_ring))
    across = [(i, (i + half_ring) % along_count) for i in range(along_count)]

    def over(value):
        return lax.ppermute(value, "along", across)

    inner = slice(TILE, cols - TILE)
    slabs = (forward, backward)
    edges = over(
        jnp.stack([jnp.concatenate([v[:, :TILE], v[:, cols - TILE :]], axis=1) for v in slabs])
    )
    ends = over(
        jnp.stack(
            [
                jnp.concatenate([v[:LINE_RIM, inner], v[lines - LINE_RIM :, inner]], axis=0)
                for v in slabs
            ]
        )
    )
    tiles = cols // TILE - 2
    cuts = [tiles - 6, tiles - 3, tiles - 1, tiles] if tiles > 6 else [tiles]
    body = slice(LINE_RIM, lines - LINE_RIM)

    def after(value, *others):
        return lax.optimization_barrier((value, *others))[0]

    lead_inner = over(after(forward[body, inner], edges))
    trail_spans, trail_parts, begin = [], [], 0
    for n, cut in enumerate(cuts):
        start, stop = TILE + begin * TILE, TILE + cut * TILE
        piece = backward[body, start:stop]
        if n == 0:
            piece = after(piece, ends)
        elif n < 3:
            piece = after(piece, lead_inner)
        else:
            piece = after(piece, trail_parts[n - 3])
        trail_parts.append(over(piece))
        trail_spans.append((start + TILE, stop + TILE))
        begin = cut

    def rim(v):
        return jnp.concatenate([v[:LINE_RIM], v[lines - LINE_RIM :]], axis=0)

    raw_left = jnp.concatenate([v[:, :TILE] for v in (nadir_view, rim(forward), rim(backward))])
    raw_right = jnp.concatenate(
        [v[:, cols - TILE :] for v in (nadir_view, rim(forward), rim(backward))]
    )
    from_right = lax.ppermute(raw_left, "cross", low_z)
    from_left = lax.ppermute(raw_right, "cross", high_z)
    nadir_left, nadir_right = from_left[:lines], from_right[:lines]

    def widened(v, left, right):
        return jnp.concatenate([left, v, right], axis=-1)

    first_lines = widened(nadir_view[:NADIR_RIM], nadir_left[:NADIR_RIM], nadir_right[:NADIR_RIM])
    last_lines = widened(
        nadir_view[lines - NADIR_RIM :],
        nadir_left[lines - NADIR_RIM :],
        nadir_right[lines - NADIR_RIM :],
    )
    nadir_below = lax.ppermute(first_lines, "along", ring_down)
    nadir_above = lax.ppermute(last_lines, "along", ring_up)

    def window(v):
        padded = jnp.concatenate([v[..., total_lines - BOX :], v, v[..., : rows - lines]], axis=-1)
        return lax.dynamic_slice_in_dim(padded, along_index * lines, rows, v.ndim - 1)

    excess = lag_lines - lag_floor
    own = jnp.arange(rows, dtype=jnp.int32) + (LINE_RIM - BOX)
    starts = own[None] + window(jnp.stack([band_offsets[0] - excess, band_offsets[1] + excess]))
    tap_rows = window(along_weights).astype(jnp.float32)
    starts = starts.astype(jnp.float32)
    line_params = jnp.concatenate(
        [starts[0:1], tap_rows[0], starts[1:2], tap_rows[1], jnp.zeros((6, rows), jnp.float32)]
    ).T
    gap = jnp.zeros((3, cols), jnp.float32)
    shift = col_offsets.astype(jnp.float32)
    taps = cross_weights.astype(jnp.float32)
    col_params = jnp.concatenate([shift[0:1], taps[0], gap, shift[1:2], taps[1], gap])
    columns = cross_index * cols + jnp.arange(cols, dtype=jnp.int32)
    position = (columns.astype(jnp.float32) + 0.5) / total_cols + 0.25
    square = position * position
    pos = jnp.stack([position, square, square * position, square * square] + [position] * 4)
    basis = harmonics(window_start[0] + along_index * lines + jnp.arange(lines, dtype=jnp.int32))

    f32, bf16 = jnp.float32, jnp.bfloat16
    depth = lines // 2 + 2 * LINE_RIM
    limit = pltpu.CompilerParams(vmem_limit_bytes=40 * 1024 * 1024)
    slopes, center, texture, inverse, sums, bands = pl.pallas_call(
        functools.partial(prep_kernel, lines, cols),
        out_shape=(
            jax.ShapeDtypeStruct((rows, cols), f32),
            jax.ShapeDtypeStruct((rows, cols), f32),
            jax.ShapeDtypeStruct((lines, cols), f32),
            jax.ShapeDtypeStruct((lines, cols), f32),
            jax.ShapeDtypeStruct((lines, TILE), f32),
            jax.ShapeDtypeStruct((2, rows, depth), bf16),
        ),
        scratch_shapes=[pltpu.VMEM((lines + 2 * NADIR_RIM, whole), bf16)],
        compiler_params=limit,
        cost_estimate=pl.CostEstimate(
            flops=2 * rows * cols * 512, bytes_accessed=12 * rows * cols, transcendentals=0
        ),
        name="prep",
    )(nadir_view, nadir_left, nadir_right, nadir_above, nadir_below, line_params, pos)

    scale_sum = 1.0 / (lines * total_cols)
    scale_pull = 1.0 / (lines * total_cols) ** 0.5
    line_sums = sums[:, :8].T * scale_sum
    step = 1
    while step < cross_count:
        line_sums = line_sums + lax.ppermute(
            line_sums, "cross", [(i, i ^ step) for i in range(cross_count)]
        )
        step *= 2
    row_count = 4 * MODES // cross_count
    row_first = cross_index * row_count
    upper = row_first + jnp.arange(row_count, dtype=jnp.int32) >= 2 * MODES
    doubled = jnp.concatenate([basis, basis], axis=1)
    basis_rows = lax.dynamic_slice_in_dim(doubled, row_first, row_count, 1)
    left_coef = jnp.where(upper[None, :], line_sums[1][:, None], line_sums[0][:, None])
    right_coef = jnp.where(upper[None, :], line_sums[2][:, None], line_sums[1][:, None])
    weighted = jnp.concatenate([basis_rows * left_coef, basis_rows * right_coef], axis=1)
    grams = jnp.dot(weighted.T, basis, precision=lax.Precision.HIGHEST)
    normal_gram = jnp.concatenate([grams[:row_count], grams[row_count:]], axis=1)[None]

    slab_right = lax.ppermute(edges[:, :, :TILE], "cross", low_z)
    slab_left = lax.ppermute(edges[:, :, TILE:], "cross", high_z)

    def full_lines(at, ends_at):
        span = slice(at, at + LINE_RIM)
        crossed = jnp.concatenate(
            [
                slab_left[:, span],
                edges[:, span, :TILE],
                ends[:, ends_at : ends_at + LINE_RIM],
                edges[:, span, TILE:],
                slab_right[:, span],
            ],
            axis=2,
        )
        raw = []
        for s, slab in enumerate(slabs):
            halo = slice(
                lines + 2 * LINE_RIM * s + ends_at, lines + 2 * LINE_RIM * s + ends_at + LINE_RIM
            )
            raw.append(widened(slab[span], from_left[halo], from_right[halo]))
        return crossed, jnp.stack(raw)

    in_half = along_index % half_ring
    crossed_top, raw_top = full_lines(0, 0)
    crossed_bottom, raw_bottom = full_lines(lines - LINE_RIM, LINE_RIM)
    send_down = jnp.where(in_half == 0, raw_top, crossed_top)
    send_up = jnp.where(in_half == half_ring - 1, raw_bottom, crossed_bottom)
    slab_below = lax.ppermute(send_down, "along", half_down)
    slab_above = lax.ppermute(send_up, "along", half_up)

    def run(s, first, width, parts, spans, earlier, parallax):
        fresh = parallax is None
        any_space = pl.BlockSpec(memory_space=pl.ANY)
        vmem = pl.BlockSpec(memory_space=pltpu.VMEM)
        operands = [
            slopes, center, texture, inverse, bands, col_params, pos, basis, earlier,
            slab_above, slab_below, slab_left, slab_right, edges, ends, *parts,
        ]
        specs = [any_space] * 4 + [vmem] * 5 + [any_space] * (6 + len(parts))
        aliases = {}
        if not fresh:
            aliases = {len(operands): 0}
            operands.append(parallax)
            specs.append(any_space)
        return pl.pallas_call(
            functools.partial(slab_kernel, lines, cols, s, first, width, spans, fresh),
            out_shape=(
                jax.ShapeDtypeStruct((2, lines, cols), bf16),
                jax.ShapeDtypeStruct((8, TILE), f32),
            ),
            in_specs=specs,
            out_specs=(any_space, vmem),
            scratch_shapes=[
                pltpu.VMEM((lines + 2 * LINE_RIM, width + 2 * TILE), bf16),
                pltpu.VMEM((rows, width + 2 * TILE), bf16),
                pltpu.VMEM((rows, width), f32),
                pltpu.VMEM((rows, width), f32),
                pltpu.VMEM((lines, width), f32),
                pltpu.VMEM((lines, width), f32),
                pltpu.VMEM((lines, width), bf16),
                pltpu.SemaphoreType.DMA((16 + len(parts),)),
            ],
            input_output_aliases=aliases,
            compiler_params=limit,
            cost_estimate=pl.CostEstimate(
                flops=2 * rows * (width + 256) * 900,
                bytes_accessed=20 * rows * width,
                transcendentals=0,
            ),
            name=f"slab{s}_{first}",
        )(*operands)

    nothing = jnp.zeros((8, TILE), f32)
    lead_span = (2 * TILE, cols)
    parallax, pulled = run(0, 0, cols, [lead_inner], [lead_span], nothing, None)
    done = 0
    for n, cut in enumerate(cuts):
        upto = cols if n == len(cuts) - 1 else cut * TILE
        parts, spans = [], []
        for part, span in zip(trail_parts[: n + 1], trail_spans):
            if span[1] > done:
                parts.append(part)
                spans.append(span)
        parallax, pulled = run(1, done, upto - done, parts, spans, pulled, parallax)
        done = upto

    total = pulled
    for shift_by in range(1, cross_count):
        total = total + lax.ppermute(
            pulled, "cross", [(i, (i + shift_by) % cross_count) for i in range(cross_count)]
        )
    flat = total[:2].reshape(1, 4 * MODES) * scale_pull
    normal_rhs = lax.dynamic_slice_in_dim(flat, row_first, row_count, 1)
    return parallax, normal_gram, normal_rhs


def solution(mesh):
    placed = (
        P("along", "cross"),
        P("along", "cross"),
        P("along", "cross"),
        P(),
        P(None, None, "cross"),
        P(),
        P(None, "cross"),
        P(),
        P(),
    )
    return jax.shard_map(
        local,
        mesh=mesh,
        in_specs=placed,
        out_specs=(P(None, "along", "cross"), P("along", "cross", None), P("along", "cross")),
        check_vma=False,
    )
```

time: 98.8 us -> 96.6 us (0.978)
  the two profiles are of different devices: /device:TPU:0 before, /device:TPU:2 now
where the time goes in v1:
time: 96.6 us; the launch traced here: 96 us
  waiting for transfers between devices  31.8 us (33%)
  starting transfers between devices  26.5 us (27%)
  Pallas kernels  15.9 us (16%)
  local copies, waits for them, and re-layouts  13.2 us (14%)
  other arithmetic  6.24 us (6%)
  between operations  1.95 us (2%)
    pallas_call x5, Pallas kernels, run(): pl.pallas_call(functools.partial(slab_kernel, lines, cols, s, first, widt...  13.3 us
    ppermute x2, waiting for transfers between devices, local(): lax.ppermute(line_sums, 'cross', [(i, i ^ step) for i in range(cross_coun...  11.9 us
    ppermute x7, waiting for transfers between devices, over(): return lax.ppermute(value, 'along', across)  10.7 us
    ppermute x3, starting transfers between devices, local(): lax.ppermute(pulled, 'cross', [(i, (i + shift_by) % cross_count) for i in...  5.86 us
    ppermute x7, starting transfers between devices, over(): return lax.ppermute(value, 'along', across)  5.24 us
    ppermute x1, starting transfers between devices, local(): from_left = lax.ppermute(raw_right, 'cross', high_z)  5.2 us
    ppermute x1, waiting for transfers between devices, local(): slab_right = lax.ppermute(edges[:, :, :TILE], 'cross', low_z)  4.19 us
    ppermute x3, waiting for transfers between devices, local(): lax.ppermute(pulled, 'cross', [(i, (i + shift_by) % cross_count) for i in...  4.13 us
  transfers between devices with their start and end apart: 20, of which 9 were waited for; matrix products, arithmetic and copies ran while one was open for 17% of the time, Pallas kernels for 14%

profile of v1, /device:TPU:2, one launch (start us, length us, event | category | flops | bytes accessed | tf_op | source)
XLA Modules:
  0.0 96.0 jit_solution(8328693981227198873)
XLA Ops:
  0.7 1.0 %fusion.27 = (bf16[256,128]{1,0:T(8,128)(2,1)S(1)}, bf16[256,128]{1,0:T(8,128)(2,1)S(1)}) fusion(bf16[256,1536]{1,0:T(8,128)(2,1)} %param.10), kind=kLoop, calls=%fused_computation.94 | loop fusion | bytes 262144 | tf_op jit(solution)/shard_map/slice | solution.py:215
  1.7 0.9 fusion.28
  2.6 0.7 pad_maximum_fusion.1
  3.3 1.5 %collective-permute-start.4 = (bf16[2,256,256]{2,1,0:T(8,128)(2,1)}, bf16[2,256,256]{2,1,0:T(8,128)(2,1)S(1)}, u32[]{:S(2)}, u32[]{:S(2)}) collective-permute-start(bf16[2,256,256]{2,1,0:T(8,128)(2,1)} %pad_maximum_fusion.1), channel_id=1, source_target_pairs={{0,16},{4,20},{8,24},{12,28},{16,0},{20,4},{24,8},{28,12},{1,17},{... | collective-permute-start | bytes 786440 | tf_op jit(solution)/shard_map/ppermute | solution.py:210
  5.0 0.8 pad_maximum_fusion
  6.4 0.7 fusion.10
  7.1 1.3 %collective-permute-start.1 = (bf16[384,128]{1,0:T(8,128)(2,1)}, bf16[384,128]{1,0:T(8,128)(2,1)}, u32[]{:S(2)}, u32[]{:S(2)}) collective-permute-start(bf16[384,128]{1,0:T(8,128)(2,1)} %get-tuple-element.66), channel_id=1, source_target_pairs={{1,0},{2,1},{3,2},{5,4},{6,5},{7,6},{9,8},{10,9},{11,10},{13,12},{... | collective-permute-start | bytes 294920 | tf_op jit(solution)/shard_map/ppermute | solution.py:254
  8.4 5.2 %collective-permute-start = (bf16[384,128]{1,0:T(8,128)(2,1)}, bf16[384,128]{1,0:T(8,128)(2,1)}, u32[]{:S(2)}, u32[]{:S(2)}) collective-permute-start(bf16[384,128]{1,0:T(8,128)(2,1)} %get-tuple-element.67), channel_id=1, source_target_pairs={{0,1},{1,2},{2,3},{4,5},{5,6},{6,7},{8,9},{9,10},{10,11},{12,13},{... | collective-permute-start | bytes 294920 | tf_op jit(solution)/shard_map/ppermute | solution.py:255
  14.2 0.6 fusion.21
  14.8 0.6 multiply_add_fusion
  15.5 0.6 slice.293
  16.1 0.6 slice.292
  16.8 0.6 fusion.29
  17.4 0.7 slice.291
  18.1 0.7 slice.290
  18.8 0.8 slice.289
  21.1 0.6 fusion.15
  21.8 0.8 stack.59.pos
  22.7 0.7 fusion.37
  23.4 0.7 fusion.36
  24.2 1.7 %collective-permute-start.3 = (bf16[16,1792]{1,0:T(8,128)(2,1)S(1)}, bf16[16,1792]{1,0:T(8,128)(2,1)S(1)}, u32[]{:S(2)}, u32[]{:S(2)}) collective-permute-start(bf16[16,1792]{1,0:T(8,128)(2,1)S(1)} %pad_maximum_fusion.8), channel_id=1, source_target_pairs={{0,28},{4,0},{8,4},{12,8},{16,12},{20,16},{24,20},{28,24},{1,29},{... | collective-permute-start | bytes 172040 | tf_op jit(solution)/shard_map/ppermute | solution.py:267
  25.9 0.7 fusion.35
  26.7 0.7 fusion.34
  27.5 0.8 slice.302.right
  28.3 0.8 slice.301.left
  29.2 2.6 %prep.1 = (f32[272,1536]{1,0:T(8,128)S(1)}, f32[272,1536]{1,0:T(8,128)S(1)}, f32[256,1536]{1,0:T(8,128)S(1)}, f32[256,1536]{1,0:T(8,128)S(1)}, f32[256,128]{1,0:T(8,128)S(1)}, /*index=5*/bf16[2,272,192]{2,1,0:T(8,128)(2,1)S(1)}) custom-call(bf16[256,1536]{1,0:T(8,128)(2,1)S(1)} %copy-done, bf16[256,128]{1,0:T(8,128)(2,1)S(1)} %slice.301.left, ...), custom_call_target="tpu_custom_call" | custom-call | flops 427819008 | bytes 5013504 | tf_op jit(solution)/shard_map/prep/pallas_call | solution.py:295
  31.8 1.0 %collective-permute-start.15 = (f32[8,256]{0,1:T(8,128)S(1)}, f32[8,256]{0,1:T(8,128)S(1)}, u32[]{:S(2)}, u32[]{:S(2)}) collective-permute-start(f32[8,256]{0,1:T(8,128)S(1)} %multiply_bitcast_fusion), channel_id=1, source_target_pairs={{0,1},{1,0},{2,3},{3,2},{4,5},{5,4},{6,7},{7,6},{8,9},{9,8},{10,11... | collective-permute-start | bytes 24584 | tf_op jit(solution)/shard_map/ppermute | solution.py:318
  32.9 5.2 %collective-permute-done.15 = f32[8,256]{0,1:T(8,128)S(1)} collective-permute-done((f32[8,256]{0,1:T(8,128)S(1)}, f32[8,256]{0,1:T(8,128)S(1)}, u32[]{:S(2)}, u32[]{:S(2)}) %collective-permute-start.15) | collective-permute-done | bytes 8224 | tf_op jit(solution)/shard_map/ppermute | solution.py:318
  38.1 2.7 %collective-permute-start.16 = (f32[8,256]{0,1:T(8,128)S(1)}, f32[8,256]{0,1:T(8,128)S(1)}, u32[]{:S(2)}, u32[]{:S(2)}) collective-permute-start(f32[8,256]{0,1:T(8,128)S(1)} %fusion.23), channel_id=1, source_target_pairs={{0,2},{1,3},{2,0},{3,1},{4,6},{5,7},{6,4},{7,5},{8,10},{9,11},{10,... | collective-permute-start | bytes 24584 | tf_op jit(solution)/shard_map/ppermute | solution.py:318
  40.8 6.6 %collective-permute-done.16 = f32[8,256]{0,1:T(8,128)S(1)} collective-permute-done((f32[8,256]{0,1:T(8,128)S(1)}, f32[8,256]{0,1:T(8,128)S(1)}, u32[]{:S(2)}, u32[]{:S(2)}) %collective-permute-start.16) | collective-permute-done | bytes 8224 | tf_op jit(solution)/shard_map/ppermute | solution.py:318
  48.1 1.4 %collective-permute-start.5 = (bf16[2,256,128]{2,1,0:T(8,128)(2,1)S(1)}, bf16[2,256,128]{2,1,0:T(8,128)(2,1)S(1)}, u32[]{:S(2)}, u32[]{:S(2)}) collective-permute-start(bf16[2,256,128]{2,1,0:T(8,128)(2,1)S(1)} %get-tuple-element.75), channel_id=1, source_target_pairs={{0,1},{1,2},{2,3},{4,5},{5,6},{6,7},{8,9},{9,10},{10,11},{12,13},{... | collective-permute-start | bytes 393224 | tf_op jit(solution)/shard_map/ppermute | solution.py:334
  49.7 1.3 %collective-permute-start.7 = (bf16[2,256,128]{2,1,0:T(8,128)(2,1)S(1)}, bf16[2,256,128]{2,1,0:T(8,128)(2,1)S(1)}, u32[]{:S(2)}, u32[]{:S(2)}) collective-permute-start(bf16[2,256,128]{2,1,0:T(8,128)(2,1)S(1)} %get-tuple-element.74), channel_id=1, source_target_pairs={{1,0},{2,1},{3,2},{5,4},{6,5},{7,6},{9,8},{10,9},{11,10},{13,12},{... | collective-permute-start | bytes 393224 | tf_op jit(solution)/shard_map/ppermute | solution.py:333
  51.4 0.9 collective-permute-done.5.left
  52.4 4.2 %collective-permute-done.7.right = bf16[2,256,128]{2,1,0:T(8,128)(2,1)S(1)} collective-permute-done((bf16[2,256,128]{2,1,0:T(8,128)(2,1)S(1)}, bf16[2,256,128]{2,1,0:T(8,128)(2,1)S(1)}, u32[]{:S(2)}, u32[]{:S(2)}) %collective-permute-start.7) | collective-permute-done | bytes 131104 | tf_op jit(solution)/shard_map/ppermute | solution.py:333
  56.8 0.7 collective-permute-start.8
  58.3 6.9 %collective-permute-done.10.rest_0_ = bf16[192,1280]{1,0:T(8,128)(2,1)S(1)} collective-permute-done((bf16[192,1280]{1,0:T(8,128)(2,1)S(1)}, bf16[192,1280]{1,0:T(8,128)(2,1)S(1)}, u32[]{:S(2)}, u32[]{:S(2)}) %collective-permute-start.10) | collective-permute-done | bytes 491552 | tf_op jit(solution)/shard_map/ppermute | solution.py:210
  65.6 3.8 %collective-permute-done.11.rest_0_ = bf16[192,512]{1,0:T(8,128)(2,1)S(1)} collective-permute-done((bf16[192,512]{1,0:T(8,128)(2,1)S(1)}, bf16[192,512]{1,0:T(8,128)(2,1)S(1)}, u32[]{:S(2)}, u32[]{:S(2)}) %collective-permute-start.11) | collective-permute-done | bytes 196640 | tf_op jit(solution)/shard_map/ppermute | solution.py:210
  69.8 1.6 %collective-permute-start.13 = (bf16[192,256]{1,0:T(8,128)(2,1)S(1)}, bf16[192,256]{1,0:T(8,128)(2,1)S(1)}, u32[]{:S(2)}, u32[]{:S(2)}) collective-permute-start(bf16[192,256]{1,0:T(8,128)(2,1)S(1)} %copy-done.13), channel_id=1, source_target_pairs={{0,16},{4,20},{8,24},{12,28},{16,0},{20,4},{24,8},{28,12},{1,17},{... | collective-permute-start | bytes 294920 | tf_op jit(solution)/shard_map/ppermute | solution.py:210
  71.4 5.0 %slab0_0.1 = (bf16[2,256,1536]{2,1,0:T(8,128)(2,1)}, f32[8,128]{1,0:T(8,128)S(1)}) custom-call(f32[272,1536]{1,0:T(8,128)S(1)} %get-tuple-element.24.slopes, f32[272,1536]{1,0:T(8,128)S(1)} %get-tuple-element.25.center, f32[256,1536]{1,0:T(8,128)S(1)} %get-tuple-element.26.texture, f32[256,1536]{1,0:T(8,128)S(1)} %get-tuple-element.27.inverse, ...), custom_call_target="tpu_custom_call" | custom-call | flops 877363200 | bytes 8355840 | tf_op jit(solution)/shard_map/slab0_0/pallas_call | solution.py:378
  76.4 2.3 %slab1_0.1 = (bf16[2,256,1536]{2,1,0:T(8,128)(2,1)}, f32[8,128]{1,0:T(8,128)S(1)}) custom-call(f32[272,1536]{1,0:T(8,128)S(1)} %get-tuple-element.24.slopes, f32[272,1536]{1,0:T(8,128)S(1)} %get-tuple-element.25.center, f32[256,1536]{1,0:T(8,128)S(1)} %get-tuple-element.26.texture, ...), custom_call_target="tpu_custom_call", output_to_operand_aliasing={{0}: (16, {})} | custom-call | flops 376012800 | bytes 2785280 | tf_op jit(solution)/shard_map/slab1_0/pallas_call | solution.py:378
  78.8 2.1 %slab1_512.1 = (bf16[2,256,1536]{2,1,0:T(8,128)(2,1)}, f32[8,128]{1,0:T(8,128)S(1)}) custom-call(f32[272,1536]{1,0:T(8,128)S(1)} %get-tuple-element.24.slopes, f32[272,1536]{1,0:T(8,128)S(1)} %get-tuple-element.25.center, f32[256,1536]{1,0:T(8,128)S(1)} %get-tuple-element.26.texture, ...), custom_call_target="tpu_custom_call", output_to_operand_aliasing={{0}: (17, {})} | custom-call | flops 313344000 | bytes 2088960 | tf_op jit(solution)/shard_map/slab1_512/pallas_call | solution.py:378
  80.9 1.8 %slab1_896.1 = (bf16[2,256,1536]{2,1,0:T(8,128)(2,1)}, f32[8,128]{1,0:T(8,128)S(1)}) custom-call(f32[272,1536]{1,0:T(8,128)S(1)} %get-tuple-element.24.slopes, f32[272,1536]{1,0:T(8,128)S(1)} %get-tuple-element.25.center, f32[256,1536]{1,0:T(8,128)S(1)} %get-tuple-element.26.texture, ...), custom_call_target="tpu_custom_call", output_to_operand_aliasing={{0}: (17, {})} | custom-call | flops 250675200 | bytes 1392640 | tf_op jit(solution)/shard_map/slab1_896/pallas_call | solution.py:378
  82.7 2.1 %slab1_1152.1 = (bf16[2,256,1536]{2,1,0:T(8,128)(2,1)}, f32[8,128]{1,0:T(8,128)S(1)}) custom-call(f32[272,1536]{1,0:T(8,128)S(1)} %get-tuple-element.24.slopes, f32[272,1536]{1,0:T(8,128)S(1)} %get-tuple-element.25.center, f32[256,1536]{1,0:T(8,128)S(1)} %get-tuple-element.26.texture, ...), custom_call_target="tpu_custom_call", output_to_operand_aliasing={{0}: (17, {})} | custom-call | flops 313344000 | bytes 2088960 | tf_op jit(solution)/shard_map/slab1_1152/pallas_call | solution.py:378
  84.8 5.2 %collective-permute-start.19 = (f32[8,128]{1,0:T(8,128)S(1)}, f32[8,128]{1,0:T(8,128)S(1)}, u32[]{:S(2)}, u32[]{:S(2)}) collective-permute-start(f32[8,128]{1,0:T(8,128)S(1)} %get-tuple-element.44), channel_id=1, source_target_pairs={{0,3},{1,0},{2,1},{3,2},{4,7},{5,4},{6,5},{7,6},{8,11},{9,8},{10,9... | collective-permute-start | bytes 12296 | tf_op jit(solution)/shard_map/ppermute | solution.py:422
  90.0 0.6 collective-permute-start.17
  90.7 0.6 maximum_bitcast_fusion.8
  91.3 3.2 %collective-permute-done.18 = f32[8,128]{1,0:T(8,128)S(1)} collective-permute-done((f32[8,128]{1,0:T(8,128)S(1)}, f32[8,128]{1,0:T(8,128)S(1)}, u32[]{:S(2)}, u32[]{:S(2)}) %collective-permute-start.18) | collective-permute-done | bytes 4128 | tf_op jit(solution)/shard_map/ppermute | solution.py:422
  94.5 0.9 collective-permute-done.17
  (122 shorter events, 6.2 us)
Async XLA Ops:
  0.6 4.2 %copy-start.2 = (bf16[256,1536]{1,0:T(8,128)(2,1)S(1)}, bf16[256,1536]{1,0:T(8,128)(2,1)}, u32[]{:S(2)}) copy-start(bf16[256,1536]{1,0:T(8,128)(2,1)} %param.10) | copy-start | bytes 2359300
  0.6 4.2 %copy-start.1 = (bf16[256,1536]{1,0:T(8,128)(2,1)S(1)}, bf16[256,1536]{1,0:T(8,128)(2,1)}, u32[]{:S(2)}) copy-start(bf16[256,1536]{1,0:T(8,128)(2,1)} %param.11) | copy-start | bytes 2359300
  2.6 3.7 %copy-start = (bf16[256,1536]{1,0:T(8,128)(2,1)S(1)}, bf16[256,1536]{1,0:T(8,128)(2,1)}, u32[]{:S(2)}) copy-start(bf16[256,1536]{1,0:T(8,128)(2,1)} %nadir.1) | copy-start | bytes 2359300
  3.3 44.7 %collective-permute-start.4 = (bf16[2,256,256]{2,1,0:T(8,128)(2,1)}, bf16[2,256,256]{2,1,0:T(8,128)(2,1)S(1)}, u32[]{:S(2)}, u32[]{:S(2)}) collective-permute-start(bf16[2,256,256]{2,1,0:T(8,128)(2,1)} %pad_maximum_fusion.1), channel_id=1, source_target_pairs={{0,16},{4,20},{8,24},{12,28},{16,0},{20,4},{24,8},{28,12},{1,17},{... | collective-permute-start | bytes 786440 | tf_op jit(solution)/shard_map/ppermute | solution.py:210
  4.9 9.2 %copy-start.15 = (bf16[2,4,2048]{2,1,0:T(4,128)(2,1)S(1)}, bf16[2,4,2048]{2,1,0:T(4,128)(2,1)}, u32[]{:S(2)}) copy-start(bf16[2,4,2048]{2,1,0:T(4,128)(2,1)} %param.12) | copy-start | bytes 98308
  4.9 10.5 %copy-start.17 = (s32[2,2048]{1,0:T(2,128)S(1)}, s32[2,2048]{1,0:T(2,128)}, u32[]{:S(2)}) copy-start(s32[2,2048]{1,0:T(2,128)} %param.14) | copy-start | bytes 49156
  4.9 10.5 %copy-start.19 = (s32[2048]{0:T(1024)S(1)}, s32[2048]{0:T(1024)}, u32[]{:S(2)}) copy-start(s32[2048]{0:T(1024)} %param.16) | copy-start | bytes 24580
  5.7 46.6 %collective-permute-start.6 = (bf16[2,64,1280]{2,1,0:T(8,128)(2,1)}, bf16[2,64,1280]{2,1,0:T(8,128)(2,1)S(1)}, u32[]{:S(2)}, u32[]{:S(2)}) collective-permute-start(bf16[2,64,1280]{2,1,0:T(8,128)(2,1)} %pad_maximum_fusion), channel_id=1, source_target_pairs={{0,16},{4,20},{8,24},{12,28},{16,0},{20,4},{24,8},{28,12},{1,17},{... | collective-permute-start | bytes 983048 | tf_op jit(solution)/shard_map/ppermute | solution.py:210
  6.3 13.3 %copy-start.3 = (bf16[32,1536]{1,0:T(8,128)(2,1)}, bf16[32,1536]{1,0:T(8,128)(2,1)S(1)}, u32[]{:S(2)}) copy-start(bf16[32,1536]{1,0:T(8,128)(2,1)S(1)} %get-tuple-element.108) | copy-start | bytes 294916
  6.3 13.3 %copy-start.5 = (bf16[32,1536]{1,0:T(8,128)(2,1)}, bf16[32,1536]{1,0:T(8,128)(2,1)S(1)}, u32[]{:S(2)}) copy-start(bf16[32,1536]{1,0:T(8,128)(2,1)S(1)} %get-tuple-element.109) | copy-start | bytes 294916
  6.3 13.3 %copy-start.7 = (bf16[32,1536]{1,0:T(8,128)(2,1)}, bf16[32,1536]{1,0:T(8,128)(2,1)S(1)}, u32[]{:S(2)}) copy-start(bf16[32,1536]{1,0:T(8,128)(2,1)S(1)} %get-tuple-element.62) | copy-start | bytes 294916
  6.3 14.0 %copy-start.18 = (s32[2,1536]{1,0:T(2,128)S(1)}, s32[2,1536]{1,0:T(2,128)}, u32[]{:S(2)}) copy-start(s32[2,1536]{1,0:T(2,128)} %param.15) | copy-start | bytes 36868
  6.4 14.2 %slice-start = ((bf16[2,4,2048]{2,1,0:T(4,128)(2,1)}), bf16[2,4,16]{2,1,0:T(4,128)(2,1)S(1)}, s32[]{:S(2)}) async-start(bf16[2,4,2048]{2,1,0:T(4,128)(2,1)} %param.12), calls=%async_computation | async-start | bytes 4096 | tf_op jit(solution)/shard_map/slice | solution.py:271
  6.4 14.5 %copy-start.16 = (bf16[2,4,1536]{2,1,0:T(4,128)(2,1)S(1)}, bf16[2,4,1536]{2,1,0:T(4,128)(2,1)}, u32[]{:S(2)}) copy-start(bf16[2,4,1536]{2,1,0:T(4,128)(2,1)} %param.13) | copy-start | bytes 73732
  7.1 15.7 %collective-permute-start.1 = (bf16[384,128]{1,0:T(8,128)(2,1)}, bf16[384,128]{1,0:T(8,128)(2,1)}, u32[]{:S(2)}, u32[]{:S(2)}) collective-permute-start(bf16[384,128]{1,0:T(8,128)(2,1)} %get-tuple-element.66), channel_id=1, source_target_pairs={{1,0},{2,1},{3,2},{5,4},{6,5},{7,6},{9,8},{10,9},{11,10},{13,12},{... | collective-permute-start | bytes 294920 | tf_op jit(solution)/shard_map/ppermute | solution.py:254
  8.4 15.1 %collective-permute-start = (bf16[384,128]{1,0:T(8,128)(2,1)}, bf16[384,128]{1,0:T(8,128)(2,1)}, u32[]{:S(2)}, u32[]{:S(2)}) collective-permute-start(bf16[384,128]{1,0:T(8,128)(2,1)} %get-tuple-element.67), channel_id=1, source_target_pairs={{0,1},{1,2},{2,3},{4,5},{5,6},{6,7},{8,9},{9,10},{10,11},{12,13},{... | collective-permute-start | bytes 294920 | tf_op jit(solution)/shard_map/ppermute | solution.py:255
  18.8 2.3 %copy-start.20 = (s32[64]{0:T(128)S(1)}, s32[64]{0:T(128)}, u32[]{:S(2)}) copy-start(s32[64]{0:T(128)} %multiply_add_fusion.1) | copy-start | bytes 772
  18.8 5.3 %copy-start.11 = (bf16[16,1536]{1,0:T(8,128)(2,1)S(1)}, bf16[16,1536]{1,0:T(8,128)(2,1)}, u32[]{:S(2)}) copy-start(bf16[16,1536]{1,0:T(8,128)(2,1)} %get-tuple-element.59) | copy-start | bytes 147460
  19.6 7.8 %copy-start.8 = (bf16[32,1536]{1,0:T(8,128)(2,1)S(1)}, bf16[32,1536]{1,0:T(8,128)(2,1)}, u32[]{:S(2)}) copy-start(bf16[32,1536]{1,0:T(8,128)(2,1)} %copy-done.7) | copy-start | bytes 294916
  19.6 7.9 %copy-start.6 = (bf16[32,1536]{1,0:T(8,128)(2,1)S(1)}, bf16[32,1536]{1,0:T(8,128)(2,1)}, u32[]{:S(2)}) copy-start(bf16[32,1536]{1,0:T(8,128)(2,1)} %copy-done.5) | copy-start | bytes 294916
  22.6 10.2 %copy-start.4 = (bf16[32,1536]{1,0:T(8,128)(2,1)S(1)}, bf16[32,1536]{1,0:T(8,128)(2,1)}, u32[]{:S(2)}) copy-start(bf16[32,1536]{1,0:T(8,128)(2,1)} %copy-done.3) | copy-start | bytes 294916
  24.1 5.0 %collective-permute-start.2 = (bf16[16,1792]{1,0:T(8,128)(2,1)S(1)}, bf16[16,1792]{1,0:T(8,128)(2,1)S(1)}, u32[]{:S(2)}, u32[]{:S(2)}) collective-permute-start(bf16[16,1792]{1,0:T(8,128)(2,1)S(1)} %pad_maximum_fusion.7), channel_id=1, source_target_pairs={{0,4},{4,8},{8,12},{12,16},{16,20},{20,24},{24,28},{28,0},{1,5},{5... | collective-permute-start | bytes 172040 | tf_op jit(solution)/shard_map/ppermute | solution.py:268
  24.2 5.0 %collective-permute-start.3 = (bf16[16,1792]{1,0:T(8,128)(2,1)S(1)}, bf16[16,1792]{1,0:T(8,128)(2,1)S(1)}, u32[]{:S(2)}, u32[]{:S(2)}) collective-permute-start(bf16[16,1792]{1,0:T(8,128)(2,1)S(1)} %pad_maximum_fusion.8), channel_id=1, source_target_pairs={{0,28},{4,0},{8,4},{12,8},{16,12},{20,16},{24,20},{28,24},{1,29},{... | collective-permute-start | bytes 172040 | tf_op jit(solution)/shard_map/ppermute | solution.py:267
  31.8 19.2 %copy-start.9 = (bf16[192,1280]{1,0:T(8,128)(2,1)S(1)}, bf16[192,1280]{1,0:T(8,128)(2,1)}, u32[]{:S(2)}) copy-start(bf16[192,1280]{1,0:T(8,128)(2,1)} %slice.289) | copy-start | bytes 1474564
  31.8 6.3 %collective-permute-start.15 = (f32[8,256]{0,1:T(8,128)S(1)}, f32[8,256]{0,1:T(8,128)S(1)}, u32[]{:S(2)}, u32[]{:S(2)}) collective-permute-start(f32[8,256]{0,1:T(8,128)S(1)} %multiply_bitcast_fusion), channel_id=1, source_target_pairs={{0,1},{1,0},{2,3},{3,2},{4,5},{5,4},{6,7},{7,6},{8,9},{9,8},{10,11... | collective-permute-start | bytes 24584 | tf_op jit(solution)/shard_map/ppermute | solution.py:318
  38.1 9.3 %collective-permute-start.16 = (f32[8,256]{0,1:T(8,128)S(1)}, f32[8,256]{0,1:T(8,128)S(1)}, u32[]{:S(2)}, u32[]{:S(2)}) collective-permute-start(f32[8,256]{0,1:T(8,128)S(1)} %fusion.23), channel_id=1, source_target_pairs={{0,2},{1,3},{2,0},{3,1},{4,6},{5,7},{6,4},{7,5},{8,10},{9,11},{10,... | collective-permute-start | bytes 24584 | tf_op jit(solution)/shard_map/ppermute | solution.py:318
  48.1 9.9 %copy-start.10 = (bf16[192,512]{1,0:T(8,128)(2,1)S(1)}, bf16[192,512]{1,0:T(8,128)(2,1)}, u32[]{:S(2)}) copy-start(bf16[192,512]{1,0:T(8,128)(2,1)} %slice.290) | copy-start | bytes 589828
  48.1 17.1 %copy-start.12 = (bf16[192,384]{1,0:T(8,128)(2,1)S(1)}, bf16[192,384]{1,0:T(8,128)(2,1)}, u32[]{:S(2)}) copy-start(bf16[192,384]{1,0:T(8,128)(2,1)} %slice.291) | copy-start | bytes 442372
  48.1 4.2 %collective-permute-start.5 = (bf16[2,256,128]{2,1,0:T(8,128)(2,1)S(1)}, bf16[2,256,128]{2,1,0:T(8,128)(2,1)S(1)}, u32[]{:S(2)}, u32[]{:S(2)}) collective-permute-start(bf16[2,256,128]{2,1,0:T(8,128)(2,1)S(1)} %get-tuple-element.75), channel_id=1, source_target_pairs={{0,1},{1,2},{2,3},{4,5},{5,6},{6,7},{8,9},{9,10},{10,11},{12,13},{... | collective-permute-start | bytes 393224 | tf_op jit(solution)/shard_map/ppermute | solution.py:334
  49.5 19.9 %copy-start.14 = (bf16[192,128]{1,0:T(8,128)(2,1)S(1)}, bf16[192,128]{1,0:T(8,128)(2,1)}, u32[]{:S(2)}) copy-start(bf16[192,128]{1,0:T(8,128)(2,1)} %slice.293) | copy-start | bytes 147460
  49.5 20.3 %copy-start.13 = (bf16[192,256]{1,0:T(8,128)(2,1)S(1)}, bf16[192,256]{1,0:T(8,128)(2,1)}, u32[]{:S(2)}) copy-start(bf16[192,256]{1,0:T(8,128)(2,1)} %slice.292) | copy-start | bytes 294916
  49.7 6.9 %collective-permute-start.7 = (bf16[2,256,128]{2,1,0:T(8,128)(2,1)S(1)}, bf16[2,256,128]{2,1,0:T(8,128)(2,1)S(1)}, u32[]{:S(2)}, u32[]{:S(2)}) collective-permute-start(bf16[2,256,128]{2,1,0:T(8,128)(2,1)S(1)} %get-tuple-element.74), channel_id=1, source_target_pairs={{1,0},{2,1},{3,2},{5,4},{6,5},{7,6},{9,8},{10,9},{11,10},{13,12},{... | collective-permute-start | bytes 393224 | tf_op jit(solution)/shard_map/ppermute | solution.py:333
  51.0 14.2 %collective-permute-start.10 = (bf16[192,1280]{1,0:T(8,128)(2,1)S(1)}, bf16[192,1280]{1,0:T(8,128)(2,1)S(1)}, u32[]{:S(2)}, u32[]{:S(2)}) collective-permute-start(bf16[192,1280]{1,0:T(8,128)(2,1)S(1)} %copy-done.9), channel_id=1, source_target_pairs={{0,16},{4,20},{8,24},{12,28},{16,0},{20,4},{24,8},{28,12},{1,17},{... | collective-permute-start | bytes 1474568 | tf_op jit(solution)/shard_map/ppermute | solution.py:210
  56.7 14.8 %collective-permute-start.9 = (bf16[2,32,1792]{2,1,0:T(8,128)(2,1)S(1)}, bf16[2,32,1792]{2,1,0:T(8,128)(2,1)S(1)}, u32[]{:S(2)}, u32[]{:S(2)}) collective-permute-start(bf16[2,32,1792]{2,1,0:T(8,128)(2,1)S(1)} %maximum_select_fusion.1), channel_id=1, source_target_pairs={{0,12},{4,0},{8,4},{12,8},{16,28},{20,16},{24,20},{28,24},{1,13},{... | collective-permute-start | bytes 688136 | tf_op jit(solution)/shard_map/ppermute | solution.py:361
  56.8 14.7 %collective-permute-start.8 = (bf16[2,32,1792]{2,1,0:T(8,128)(2,1)S(1)}, bf16[2,32,1792]{2,1,0:T(8,128)(2,1)S(1)}, u32[]{:S(2)}, u32[]{:S(2)}) collective-permute-start(bf16[2,32,1792]{2,1,0:T(8,128)(2,1)S(1)} %maximum_select_fusion), channel_id=1, source_target_pairs={{0,4},{4,8},{8,12},{12,0},{16,20},{20,24},{24,28},{28,16},{1,5},{5... | collective-permute-start | bytes 688136 | tf_op jit(solution)/shard_map/ppermute | solution.py:362
  58.0 11.4 %collective-permute-start.11 = (bf16[192,512]{1,0:T(8,128)(2,1)S(1)}, bf16[192,512]{1,0:T(8,128)(2,1)S(1)}, u32[]{:S(2)}, u32[]{:S(2)}) collective-permute-start(bf16[192,512]{1,0:T(8,128)(2,1)S(1)} %copy-done.10), channel_id=1, source_target_pairs={{0,16},{4,20},{8,24},{12,28},{16,0},{20,4},{24,8},{28,12},{1,17},{... | collective-permute-start | bytes 589832 | tf_op jit(solution)/shard_map/ppermute | solution.py:210
  65.2 13.6 %collective-permute-start.12 = (bf16[192,384]{1,0:T(8,128)(2,1)S(1)}, bf16[192,384]{1,0:T(8,128)(2,1)S(1)}, u32[]{:S(2)}, u32[]{:S(2)}) collective-permute-start(bf16[192,384]{1,0:T(8,128)(2,1)S(1)} %copy-done.12), channel_id=1, source_target_pairs={{0,16},{4,20},{8,24},{12,28},{16,0},{20,4},{24,8},{28,12},{1,17},{... | collective-permute-start | bytes 442376 | tf_op jit(solution)/shard_map/ppermute | solution.py:210
  69.4 13.3 %collective-permute-start.14 = (bf16[192,128]{1,0:T(8,128)(2,1)S(1)}, bf16[192,128]{1,0:T(8,128)(2,1)S(1)}, u32[]{:S(2)}, u32[]{:S(2)}) collective-permute-start(bf16[192,128]{1,0:T(8,128)(2,1)S(1)} %copy-done.14), channel_id=1, source_target_pairs={{0,16},{4,20},{8,24},{12,28},{16,0},{20,4},{24,8},{28,12},{1,17},{... | collective-permute-start | bytes 147464 | tf_op jit(solution)/shard_map/ppermute | solution.py:210
  69.8 11.1 %collective-permute-start.13 = (bf16[192,256]{1,0:T(8,128)(2,1)S(1)}, bf16[192,256]{1,0:T(8,128)(2,1)S(1)}, u32[]{:S(2)}, u32[]{:S(2)}) collective-permute-start(bf16[192,256]{1,0:T(8,128)(2,1)S(1)} %copy-done.13), channel_id=1, source_target_pairs={{0,16},{4,20},{8,24},{12,28},{16,0},{20,4},{24,8},{28,12},{1,17},{... | collective-permute-start | bytes 294920 | tf_op jit(solution)/shard_map/ppermute | solution.py:210
  84.8 6.5 %collective-permute-start.19 = (f32[8,128]{1,0:T(8,128)S(1)}, f32[8,128]{1,0:T(8,128)S(1)}, u32[]{:S(2)}, u32[]{:S(2)}) collective-permute-start(f32[8,128]{1,0:T(8,128)S(1)} %get-tuple-element.44), channel_id=1, source_target_pairs={{0,3},{1,0},{2,1},{3,2},{4,7},{5,4},{6,5},{7,6},{8,11},{9,8},{10,9... | collective-permute-start | bytes 12296 | tf_op jit(solution)/shard_map/ppermute | solution.py:422
  90.0 4.5 %collective-permute-start.18 = (f32[8,128]{1,0:T(8,128)S(1)}, f32[8,128]{1,0:T(8,128)S(1)}, u32[]{:S(2)}, u32[]{:S(2)}) collective-permute-start(f32[8,128]{1,0:T(8,128)S(1)} %get-tuple-element.44), channel_id=1, source_target_pairs={{0,2},{1,3},{2,0},{3,1},{4,6},{5,7},{6,4},{7,5},{8,10},{9,11},{10,... | collective-permute-start | bytes 12296 | tf_op jit(solution)/shard_map/ppermute | solution.py:422
  90.0 5.4 %collective-permute-start.17 = (f32[8,128]{1,0:T(8,128)S(1)}, f32[8,128]{1,0:T(8,128)S(1)}, u32[]{:S(2)}, u32[]{:S(2)}) collective-permute-start(f32[8,128]{1,0:T(8,128)S(1)} %get-tuple-element.44), channel_id=1, source_target_pairs={{0,1},{1,2},{2,3},{3,0},{4,5},{5,6},{6,7},{7,4},{8,9},{9,10},{10,1... | collective-permute-start | bytes 12296 | tf_op jit(solution)/shard_map/ppermute | solution.py:422

commit v2 on v1

v2 whole, which is shorter than its diff:
```python
import functools
import math

import jax
import jax.numpy as jnp
from jax import lax
from jax.experimental import pallas as pl
from jax.experimental.pallas import tpu as pltpu
from jax.sharding import PartitionSpec as P

TAPS = 4
CAMERA_LAG = 20480
BOX = 4
MODES = 64
LINE_RIM = 32
NADIR_RIM = 16
TILE = 128
WIDE = 256
EDGE = 16


def pairs_of(count, step):
    return [(i, i + step) for i in range(count) if 0 <= i + step < count]


def harmonics(absolute):
    period = 4 * MODES
    factor = 2 * jnp.arange(MODES, dtype=jnp.int32) + 1
    phases = (absolute % period)[:, None] * factor[None, :] % period
    angles = phases.astype(jnp.float32) * (2.0 * jnp.pi / period)
    return jnp.concatenate([jnp.cos(angles), jnp.sin(angles)], axis=1)


def box_sum(x, lines):
    rows = x.shape[0]
    two = x + pltpu.roll(x, rows - 1, 0)
    four = two + pltpu.roll(two, rows - 2, 0)
    eight = four + pltpu.roll(four, rows - 4, 0)
    return eight[:lines] + x[2 * BOX : lines + 2 * BOX]


def lane_fold(x):
    folded = x[:, :TILE]
    for at in range(TILE, x.shape[1], TILE):
        folded = folded + x[:, at : at + TILE]
    return folded


def copy_all(moves, sem):
    copies = [pltpu.make_async_copy(a, b, sem.at[n]) for n, (a, b) in enumerate(moves)]
    for copy in copies:
        copy.start()
    for copy in copies:
        copy.wait()


def pack_kernel(lines, cols, nadir, forward, backward, first, last, near_first, near_last, side, sem):
    moves = []
    for n, (begin, near) in enumerate(((0, near_first), (cols - TILE, near_last))):
        moves.append((nadir.at[:, pl.ds(begin, TILE)], near.at[pl.ds(0, lines), :]))
        for s, slab in enumerate((forward, backward)):
            moves.append((slab.at[:, pl.ds(begin, TILE)], side.at[s, n]))
    copy_all(moves, sem)
    for n, (row, packed, near) in enumerate(((0, first, near_first), (TILE - EDGE, last, near_last))):
        for s in range(2):
            turned = side[s, n].astype(jnp.float32).T[row : row + EDGE].astype(jnp.bfloat16)
            packed[:, s * lines : (s + 1) * lines] = turned
            for k in range(lines // TILE):
                at = lines + (s * (lines // TILE) + k) * EDGE
                near[at : at + EDGE, :] = turned[:, k * TILE : (k + 1) * TILE]


def cut_kernel(lines, spans, backward, ends, *rest):
    moves = []
    for n, row in enumerate((0, lines - LINE_RIM)):
        moves.append((backward.at[pl.ds(row, LINE_RIM), :], ends.at[pl.ds(n * LINE_RIM, LINE_RIM), :]))
    body = pl.ds(LINE_RIM, lines - 2 * LINE_RIM)
    for (begin, end), part in zip(spans, rest):
        moves.append((backward.at[body, pl.ds(begin, end - begin)], part))
    copy_all(moves, rest[-1])


def nadir_lines_kernel(lines, cols, nadir, from_left, from_right, first, last, sem):
    moves = []
    for out, row in ((first, 0), (last, lines - NADIR_RIM)):
        span = pl.ds(row, NADIR_RIM)
        moves.append((from_left.at[span, :], out.at[:, pl.ds(0, TILE)]))
        moves.append((nadir.at[span, :], out.at[:, pl.ds(TILE, cols)]))
        moves.append((from_right.at[span, :], out.at[:, pl.ds(TILE + cols, TILE)]))
    copy_all(moves, sem)


def lines_kernel(
    lines, cols, half_ring, place, forward, backward, near_left, near_right,
    lead, ends, left, right, down, up, sem,
):
    in_half = lax.rem(place[0], half_ring)
    packed = pl.ds(2 * LINE_RIM, EDGE)
    for out, row, n, raw_place in (
        (down, 0, 0, 0),
        (up, lines - LINE_RIM, 1, half_ring - 1),
    ):
        span = pl.ds(row, LINE_RIM)
        out[2 * LINE_RIM :, 4 * lines :] = jnp.zeros((EDGE, cols - 4 * lines), jnp.bfloat16)

        @pl.when(in_half == raw_place)
        def _(out=out, span=span):
            moves = [(slab.at[span, :], out.at[pl.ds(s * LINE_RIM, LINE_RIM), :]) for s, slab in enumerate((forward, backward))]
            for n, near in enumerate((near_left, near_right)):
                for k in range(2 * lines // TILE):
                    moves.append(
                        (
                            near.at[pl.ds(lines + k * EDGE, EDGE), :],
                            out.at[packed, pl.ds(2 * n * lines + k * TILE, TILE)],
                        )
                    )
            copy_all(moves, sem)

        @pl.when(in_half != raw_place)
        def _(out=out, span=span, n=n):
            moves = [
                (lead.at[span, :], out.at[pl.ds(0, LINE_RIM), :]),
                (ends.at[pl.ds(n * LINE_RIM, LINE_RIM), :], out.at[pl.ds(LINE_RIM, LINE_RIM), :]),
                (left, out.at[packed, pl.ds(0, 2 * lines)]),
                (right, out.at[packed, pl.ds(2 * lines, 2 * lines)]),
            ]
            copy_all(moves, sem)


def positions(place, cols, total_cols, at, span):
    column = lax.broadcasted_iota(jnp.int32, (1, span), 1) + (place[1] * cols + at)
    position = (column.astype(jnp.float32) + 0.5) / total_cols + 0.25
    return position, position * position


def prep_kernel(
    lines, cols, total_lines, total_cols, lag_floor, place,
    nadir, left, right, above, below, lag, offsets, weights,
    slopes, center, texture, sums, bands, framed, slope_v, center_v, texture_v, bands_v, sem,
):
    tall = lines + 2 * NADIR_RIM
    rows = lines + 16
    framed[0:NADIR_RIM, :] = above[...]
    framed[NADIR_RIM + lines : tall, :] = below[...]
    framed[NADIR_RIM : NADIR_RIM + lines, 0:TILE] = left[0:lines, :]
    framed[NADIR_RIM : NADIR_RIM + lines, TILE : TILE + cols] = nadir[...]
    framed[NADIR_RIM : NADIR_RIM + lines, TILE + cols :] = right[0:lines, :]
    row = lax.broadcasted_iota(jnp.int32, (2 * WIDE, WIDE), 0)
    col = lax.broadcasted_iota(jnp.int32, (2 * WIDE, WIDE), 1)
    gap = jnp.abs(row - TILE - col)
    smear = jnp.where(gap == 0, 2.0, jnp.where(gap == 1, 1.0, 0.0)).astype(jnp.bfloat16)
    totals = [jnp.zeros((lines, TILE), jnp.float32) for _ in range(3)]
    copies = []
    for at in range(0, cols, WIDE):
        across = jnp.dot(
            framed[:, at : at + 2 * WIDE], smear, preferred_element_type=jnp.float32
        )
        change = pltpu.roll(across, tall - 5, 0) - pltpu.roll(across, tall - 3, 0)
        slope = change[8 : 8 + rows] * 0.25
        slope_v[:, at : at + WIDE] = slope
        middle = framed[:, TILE + at : TILE + at + WIDE].astype(jnp.float32)
        middle = pltpu.roll(middle, tall - 4, 0)[8 : 8 + rows]
        center_v[:, at : at + WIDE] = middle.astype(jnp.bfloat16)
        level = box_sum(slope * slope, lines) * (1.0 / (2 * BOX + 1))
        texture_v[:, at : at + WIDE] = level
        for source, target in ((slope_v, slopes), (center_v, center), (texture_v, texture)):
            window = (slice(None), pl.ds(at, WIDE))
            copy = pltpu.make_async_copy(source.at[window], target.at[window], sem.at[len(copies)])
            copy.start()
            copies.append(copy)
        position, square = positions(place, cols, total_cols, at, WIDE)
        for k, lever in enumerate((square, square * position, square * square)):
            totals[k] = totals[k] + lane_fold(level * lever)
    lane = lax.broadcasted_iota(jnp.int32, (lines, TILE), 1)
    packed = jnp.zeros((lines, TILE), jnp.float32)
    for k in range(3):
        packed = jnp.where(lane == k, jnp.sum(totals[k], axis=1, keepdims=True), packed)
    sums[...] = packed.T[0:8, :] * (1.0 / (lines * total_cols))
    begin = place[0] * lines
    ahead = pl.multiple_of(lax.rem(begin + total_lines - TILE, total_lines), TILE)
    behind = pl.multiple_of(lax.rem(begin + lines, total_lines), TILE)
    begin = pl.multiple_of(begin, TILE)

    def window(ref, lead):
        parts = [
            ref[lead + (slice(None), pl.ds(start, size))].astype(jnp.float32)
            for start, size in ((ahead, TILE), (begin, lines), (behind, TILE))
        ]
        return jnp.concatenate(parts, axis=1)

    wide = lines + 2 * TILE
    lags = window(lag, ()) - float(lag_floor)
    shifts = window(offsets, ())
    stacked = jnp.concatenate(
        [
            jnp.broadcast_to(shifts[0:1] - lags, (8, wide)),
            jnp.broadcast_to(shifts[1:2] + lags, (8, wide)),
            window(weights, (0,)),
            window(weights, (1,)),
            jnp.zeros((TILE - 24, wide), jnp.float32),
        ],
        axis=0,
    )
    as_columns = pltpu.roll(stacked.T, wide - (TILE - BOX), 0)[0:rows]
    half = lines // 2
    depth = half + 2 * LINE_RIM
    for s in range(2):
        for first, last in ((0, half), (half, rows)):
            at = lax.broadcasted_iota(jnp.int32, (last - first, depth), 1)
            own = lax.broadcasted_iota(jnp.int32, (last - first, depth), 0)
            distance = (at - own - (LINE_RIM - BOX)).astype(jnp.float32)
            distance = distance - as_columns[first:last, 8 * s : 8 * s + 1]
            band = jnp.zeros((last - first, depth), jnp.float32)
            for tap in range(TAPS):
                weight = as_columns[first:last, 16 + 4 * s + tap : 17 + 4 * s + tap]
                band = jnp.where(distance == float(tap), weight, band)
            bands_v[s, first:last, :] = band.astype(jnp.bfloat16)
    copy = pltpu.make_async_copy(bands_v, bands, sem.at[len(copies)])
    copy.start()
    for waited in (*copies, copy):
        waited.wait()


def slab_kernel(
    lines, cols, s, first, width, spans, fresh,
    slopes, center, texture, bands, params, basis, earlier, above, below, left, right, *rest,
):
    sources = rest[: len(spans)]
    rest = rest[len(spans) + (0 if fresh else 1) :]
    (
        parallax, pulled, ext, along, slope_v, center_v, texture_v, bands_v, params_v, basis_v,
        earlier_v, packed, result, sem,
    ) = rest
    rows = lines + 16
    half = lines // 2
    depth = half + 2 * LINE_RIM
    low, high = first - TILE, first + width + TILE
    copies = []

    def fetch(source, target):
        copy = pltpu.make_async_copy(source, target, sem.at[len(copies)])
        copy.start()
        copies.append(copy)

    def place(ref, row, target, height, begin, end):
        a, b = max(begin, low), min(end, high)
        if a < b:
            fetch(
                ref.at[pl.ds(row, height), pl.ds(a - begin, b - a)],
                ext.at[pl.ds(target, height), pl.ds(a - low, b - a)],
            )

    fetch(bands.at[s], bands_v)
    place(above, s * LINE_RIM, 0, LINE_RIM, 0, cols)
    place(below, s * LINE_RIM, LINE_RIM + lines, LINE_RIM, 0, cols)
    for ref, (row, target, height, begin, end) in zip(sources, spans):
        place(ref, row, target, height, begin, end)
    sides = [n for n in range(2) if (low < 0, high > cols)[n]]
    for n in sides:
        window = pl.ds((2 * n + s) * lines, lines)
        for k, ref in enumerate((above, below)):
            fetch(ref.at[pl.ds(2 * LINE_RIM, EDGE), window], packed.at[n, k])
        fetch((left, right)[n].at[:, pl.ds(s * lines, lines)], packed.at[n, 2])
    loaded = len(copies)
    columns = pl.ds(first, width)
    fetch(params.at[:, columns], params_v)
    fetch(slopes.at[:, columns], slope_v)
    fetch(center.at[:, columns], center_v)
    fetch(texture.at[:, columns], texture_v)
    fetch(basis, basis_v)
    fetch(earlier, earlier_v)
    for copy in copies[:loaded]:
        copy.wait()
    for n in sides:
        at = 0 if n == 0 else width + TILE
        blank = jnp.zeros((TILE - EDGE, lines), jnp.float32)
        for k, (source, target, height) in enumerate(
            ((lines - LINE_RIM, 0, LINE_RIM), (0, LINE_RIM + lines, LINE_RIM), (0, LINE_RIM, lines))
        ):
            piece = packed[n, k].astype(jnp.float32)
            piece = jnp.concatenate([blank, piece] if n == 0 else [piece, blank], axis=0)
            turned = piece.T[source : source + height].astype(jnp.bfloat16)
            ext[target : target + height, at : at + TILE] = turned
    for at in range(0, width + 2 * TILE, WIDE):
        end = min(at + WIDE, width + 2 * TILE)
        for start, stop in ((0, half), (half, rows)):
            along[start:stop, at:end] = jnp.dot(
                bands_v[start:stop, :],
                ext[start : start + depth, at:end],
                preferred_element_type=jnp.float32,
            ).astype(jnp.bfloat16)
    for copy in copies[loaded:]:
        copy.wait()
    pulls = [jnp.zeros((lines, TILE), jnp.float32) for _ in range(2)]
    for at in range(0, width, WIDE):
        span = min(WIDE, width - at)
        here = slice(at, at + span)
        row = lax.broadcasted_iota(jnp.int32, (span + 2 * EDGE, span), 0)
        col = lax.broadcasted_iota(jnp.int32, (span + 2 * EDGE, span), 1)
        distance = (row - col - EDGE).astype(jnp.float32) - params_v[8 * s : 8 * s + 1, here]
        band = jnp.zeros((span + 2 * EDGE, span), jnp.float32)
        for tap in range(TAPS):
            weight = params_v[8 * s + 1 + tap : 8 * s + 2 + tap, here]
            band = jnp.where(distance == float(tap), weight, band)
        blank = jnp.zeros((TILE - EDGE, span), jnp.bfloat16)
        resampled = jnp.dot(
            along[:, at : at + span + 2 * TILE],
            jnp.concatenate([blank, band.astype(jnp.bfloat16), blank], axis=0),
            preferred_element_type=jnp.float32,
        ).astype(jnp.bfloat16)
        mismatch = resampled.astype(jnp.float32) - center_v[:, here].astype(jnp.float32)
        level = texture_v[:, here]
        inverse = (-1.0 / (2 * BOX + 1)) / jnp.maximum(level, 0.4)
        estimate = box_sum(slope_v[:, here] * mismatch, lines) * inverse
        result[:, here] = estimate.astype(jnp.bfloat16)
        weighted = level * estimate
        for k in range(2):
            pulls[k] = pulls[k] + lane_fold(weighted * params_v[16 + k : 17 + k, here])
    out = pltpu.make_async_copy(result, parallax.at[s, :, columns], sem.at[len(copies)])
    out.start()
    pulled[...] = earlier_v[...]
    for k in range(2):
        per_line = jnp.sum(pulls[k], axis=1, keepdims=True)
        pulled[k : k + 1, :] += jnp.sum(basis_v[...] * per_line, axis=0, keepdims=True)
    out.wait()


def local(
    nadir_view, forward, backward, along_weights, cross_weights, band_offsets, col_offsets,
    lag_lines, window_start,
):
    lines, cols = nadir_view.shape
    along_count = lax.axis_size("along")
    cross_count = lax.axis_size("cross")
    along_index = lax.axis_index("along")
    cross_index = lax.axis_index("cross")
    total_lines = lines * along_count
    total_cols = cols * cross_count
    half_ring = along_count // 2
    lag_floor = CAMERA_LAG // total_lines * total_lines + half_ring * lines
    rows = lines + 16
    whole = cols + 2 * TILE
    low_z, high_z = pairs_of(cross_count, -1), pairs_of(cross_count, 1)
    ring_down = [(i, (i - 1) % along_count) for i in range(along_count)]
    ring_up = [(i, (i + 1) % along_count) for i in range(along_count)]
    half_down, half_up = [], []
    for i in range(along_count):
        base = i // half_ring * half_ring
        half_down.append((i, base + (i - base - 1) % half_ring))
        half_up.append((i, base + (i - base + 1) % half_ring))
    across = [(i, (i + half_ring) % along_count) for i in range(along_count)]

    def aslant(pairs):
        return [(a * cross_count + c, b * cross_count + d) for a, b in across for c, d in pairs]

    def over(value):
        return lax.ppermute(value, "along", across)

    def after(value, *others):
        return lax.optimization_barrier((value, *others))[0]

    def hbm(value):
        return pltpu.with_memory_space_constraint(value, pltpu.HBM)

    f32, bf16 = jnp.float32, jnp.bfloat16
    any_space = pl.BlockSpec(memory_space=pl.ANY)
    vmem = pl.BlockSpec(memory_space=pltpu.VMEM)
    smem = pl.BlockSpec(memory_space=pltpu.SMEM)
    limit = pltpu.CompilerParams(vmem_limit_bytes=24 * 1024 * 1024)

    def mover(kernel, name, shapes, operands, copies, scalars=0, scratch=()):
        return pl.pallas_call(
            kernel,
            out_shape=tuple(jax.ShapeDtypeStruct(shape, bf16) for shape in shapes),
            in_specs=[smem] * scalars + [any_space] * (len(operands) - scalars),
            out_specs=(vmem,) * len(shapes),
            scratch_shapes=[*scratch, pltpu.SemaphoreType.DMA((copies,))],
            compiler_params=limit,
            cost_estimate=pl.CostEstimate(
                flops=0, bytes_accessed=4 * sum(math.prod(s) for s in shapes), transcendentals=0
            ),
            name=name,
        )(*operands[:scalars], *(hbm(v) for v in operands[scalars:]))

    lead = over(forward)
    near = lines + 2 * EDGE * lines // TILE
    first, last, near_first, near_last = mover(
        functools.partial(pack_kernel, lines, cols),
        "pack",
        ((EDGE, 2 * lines), (EDGE, 2 * lines), (near, TILE), (near, TILE)),
        (nadir_view, forward, backward),
        6,
        scratch=[pltpu.VMEM((2, 2, lines, TILE), bf16)],
    )
    slab_right = lax.ppermute(first, ("along", "cross"), aslant(low_z))
    slab_left = lax.ppermute(last, ("along", "cross"), aslant(high_z))
    from_right = lax.ppermute(near_first, "cross", low_z)
    from_left = lax.ppermute(near_last, "cross", high_z)

    cuts = [0, cols - 3 * TILE, cols]
    spans = list(zip(cuts[:-1], cuts[1:]))
    height = lines - 2 * LINE_RIM
    ends, *parts = mover(
        functools.partial(cut_kernel, lines, spans),
        "cut",
        ((2 * LINE_RIM, cols), *((height, end - begin) for begin, end in spans)),
        (after(backward, first),),
        2 + len(spans),
    )
    ends = over(ends)

    place = jnp.stack([along_index, cross_index]).astype(jnp.int32)
    gap = jnp.zeros((3, cols), f32)
    shift = col_offsets.astype(f32)
    taps = cross_weights.astype(f32)
    columns = cross_index * cols + jnp.arange(cols, dtype=jnp.int32)
    position = ((columns.astype(f32) + 0.5) / total_cols + 0.25)[None]
    params = jnp.concatenate(
        [shift[0:1], taps[0], gap, shift[1:2], taps[1], gap, position, position * position, gap, gap]
    )
    basis = harmonics(window_start[0] + along_index * lines + jnp.arange(lines, dtype=jnp.int32))

    first_lines, last_lines = mover(
        functools.partial(nadir_lines_kernel, lines, cols),
        "nadir_lines",
        ((NADIR_RIM, whole), (NADIR_RIM, whole)),
        (nadir_view, from_left, from_right),
        6,
    )
    nadir_below = lax.ppermute(first_lines, "along", ring_down)
    nadir_above = lax.ppermute(last_lines, "along", ring_up)
    depth = lines // 2 + 2 * LINE_RIM
    slopes, center, texture, sums, bands = pl.pallas_call(
        functools.partial(prep_kernel, lines, cols, total_lines, total_cols, lag_floor),
        out_shape=(
            pltpu.HBM((rows, cols), f32),
            pltpu.HBM((rows, cols), bf16),
            pltpu.HBM((lines, cols), f32),
            jax.ShapeDtypeStruct((8, lines), f32),
            pltpu.HBM((2, rows, depth), bf16),
        ),
        in_specs=[smem] + [vmem] * 8,
        out_specs=(any_space, any_space, any_space, vmem, any_space),
        scratch_shapes=[
            pltpu.VMEM((lines + 2 * NADIR_RIM, whole), bf16),
            pltpu.VMEM((rows, cols), f32),
            pltpu.VMEM((rows, cols), bf16),
            pltpu.VMEM((lines, cols), f32),
            pltpu.VMEM((2, rows, depth), bf16),
            pltpu.SemaphoreType.DMA((3 * (cols // WIDE) + 1,)),
        ],
        compiler_params=limit,
        cost_estimate=pl.CostEstimate(
            flops=2 * rows * cols * 512, bytes_accessed=12 * rows * cols, transcendentals=0
        ),
        name="prep",
    )(
        place, hbm(after(nadir_view, params, basis, parts[0])), hbm(from_left), hbm(from_right),
        hbm(nadir_above), hbm(nadir_below), lag_lines[None], hbm(band_offsets), hbm(along_weights),
    )

    down, up = mover(
        functools.partial(lines_kernel, lines, cols, half_ring),
        "lines",
        ((2 * LINE_RIM + EDGE, cols), (2 * LINE_RIM + EDGE, cols)),
        (
            place, forward, backward, from_left, from_right, after(lead, sums), ends,
            slab_left, slab_right,
        ),
        2 + 4 * lines // TILE,
        1,
    )
    slab_below = lax.ppermute(down, "along", half_down)
    slab_above = lax.ppermute(up, "along", half_up)
    for n in range(len(parts)):
        parts[n] = over(after(parts[n], from_left if n == 0 else ends))

    def run(s, begin, end, sources, spans, earlier, parallax):
        fresh = parallax is None
        width = end - begin
        operands = [
            slopes, center, texture, bands, params, basis, earlier, slab_above, slab_below,
            slab_left, slab_right, *sources,
        ]
        aliases = {}
        if not fresh:
            aliases = {len(operands): 0}
            operands.append(parallax)
        return pl.pallas_call(
            functools.partial(slab_kernel, lines, cols, s, begin, width, spans, fresh),
            out_shape=(
                pltpu.HBM((2, lines, cols), bf16),
                jax.ShapeDtypeStruct((8, TILE), f32),
            ),
            in_specs=[any_space] * len(operands),
            out_specs=(any_space, vmem),
            scratch_shapes=[
                pltpu.VMEM((lines + 2 * LINE_RIM, width + 2 * TILE), bf16),
                pltpu.VMEM((rows, width + 2 * TILE), bf16),
                pltpu.VMEM((rows, width), f32),
                pltpu.VMEM((rows, width), bf16),
                pltpu.VMEM((lines, width), f32),
                pltpu.VMEM((rows, depth), bf16),
                pltpu.VMEM((24, width), f32),
                pltpu.VMEM((lines, TILE), f32),
                pltpu.VMEM((8, TILE), f32),
                pltpu.VMEM((2, 3, EDGE, lines), bf16),
                pltpu.VMEM((lines, width), bf16),
                pltpu.SemaphoreType.DMA((20 + len(sources),)),
            ],
            input_output_aliases=aliases,
            compiler_params=limit,
            cost_estimate=pl.CostEstimate(
                flops=2 * rows * (width + 256) * 900,
                bytes_accessed=20 * rows * width,
                transcendentals=0,
            ),
            name=f"slab{s}_{begin}",
        )(*(hbm(v) for v in operands))

    nothing = jnp.zeros((8, TILE), f32)
    lead_span = (0, LINE_RIM, lines, 0, cols)
    parallax, pulled = run(0, 0, cols, [lead], [lead_span], nothing, None)
    ends_spans = [(0, LINE_RIM, LINE_RIM, 0, cols), (LINE_RIM, lines, LINE_RIM, 0, cols)]
    done = 0
    for n, (_, cut) in enumerate(spans):
        upto = cols if cut == cols else cut - TILE
        use = [k for k in range(n + 1) if spans[k][1] > done - TILE]
        held = [(0, 2 * LINE_RIM, height, *spans[k]) for k in use]
        parallax, pulled = run(
            1, done, upto, [ends, ends, *(parts[k] for k in use)], ends_spans + held, pulled, parallax
        )
        done = upto

    share = jnp.concatenate([sums, pulled], axis=1)
    total = share
    for shift_by in range(1, cross_count):
        total = total + lax.ppermute(
            share, "cross", [(i, (i + shift_by) % cross_count) for i in range(cross_count)]
        )
    scale_pull = 1.0 / (lines * total_cols) ** 0.5
    line_sums = total[:, :lines]
    row_count = 4 * MODES // cross_count
    row_first = cross_index * row_count
    upper = row_first + jnp.arange(row_count, dtype=jnp.int32) >= 2 * MODES
    doubled = jnp.concatenate([basis, basis], axis=1)
    basis_rows = lax.dynamic_slice_in_dim(doubled, row_first, row_count, 1)
    left_coef = jnp.where(upper[None, :], line_sums[1][:, None], line_sums[0][:, None])
    right_coef = jnp.where(upper[None, :], line_sums[2][:, None], line_sums[1][:, None])
    weighted = jnp.concatenate([basis_rows * left_coef, basis_rows * right_coef], axis=1)
    grams = jnp.dot(weighted.T, basis, precision=lax.Precision.HIGHEST)
    normal_gram = jnp.concatenate([grams[:row_count], grams[row_count:]], axis=1)[None]
    flat = total[:2, lines:].reshape(1, 4 * MODES) * scale_pull
    normal_rhs = lax.dynamic_slice_in_dim(flat, row_first, row_count, 1)
    return parallax, normal_gram, normal_rhs


def solution(mesh):
    placed = (
        P("along", "cross"),
        P("along", "cross"),
        P("along", "cross"),
        P(),
        P(None, None, "cross"),
        P(),
        P(None, "cross"),
        P(),
        P(),
    )
    return jax.shard_map(
        local,
        mesh=mesh,
        in_specs=placed,
        out_specs=(P(None, "along", "cross"), P("along", "cross", None), P("along", "cross")),
        check_vma=False,
    )
```

time: 96.6 us -> 73.9 us (0.77)
  the two profiles are of different devices: /device:TPU:2 before, /device:TPU:0 now
where the time goes in v2:
time: 73.9 us; the launch traced here: 73.4 us
  starting transfers between devices  28.6 us (39%)
  Pallas kernels  24.6 us (33%)
  local copies, waits for them, and re-layouts  8.8 us (12%)
  waiting for transfers between devices  6.73 us (9%)
  other arithmetic  2.53 us (3%)
  between operations  1.66 us (2%)
    pallas_call x3, Pallas kernels, run(): pl.pallas_call(functools.partial(slab_kernel, lines, cols, s, begin, widt...  13.9 us
    ppermute x1, starting transfers between devices, local(): slab_left = lax.ppermute(last, ('along', 'cross'), aslant(high_z))  6.13 us
    ppermute x3, starting transfers between devices, local(): lax.ppermute(share, 'cross', [(i, (i + shift_by) % cross_count) for i in...  5.96 us
    ppermute x4, starting transfers between devices, over(): return lax.ppermute(value, 'along', across)  5.95 us
    pallas_call x4, Pallas kernels, mover(): pl.pallas_call(kernel, out_shape=tuple((jax.ShapeDtypeStruct(shape, bf16)...  5.83 us
    unnamed x37, local copies, waits for them, and re-layouts  5.59 us
    ppermute x1, waiting for transfers between devices, local(): slab_above = lax.ppermute(up, 'along', half_up)  4.94 us
    pallas_call x1, Pallas kernels, local(): pl.pallas_call(functools.partial(prep_kernel, lines, cols, total_lines, t...  4.85 us
  transfers between devices with their start and end apart: 15, of which 4 were waited for; matrix products, arithmetic and copies ran while one was open for 6% of the time, Pallas kernels for 29%

profile of v2, /device:TPU:0, one launch (start us, length us, event | category | flops | bytes accessed | tf_op | source)
XLA Modules:
  0.0 73.4 jit_solution(11052789522704244457)
XLA Ops:
  0.7 3.0 %collective-permute-start.4 = (bf16[256,1536]{1,0:T(8,128)(2,1)}, bf16[256,1536]{1,0:T(8,128)(2,1)S(1)}, u32[]{:S(2)}, u32[]{:S(2)}) collective-permute-start(bf16[256,1536]{1,0:T(8,128)(2,1)} %forward.3), channel_id=1, source_target_pairs={{0,16},{4,20},{8,24},{12,28},{16,0},{20,4},{24,8},{28,12},{1,17},{... | collective-permute-start | bytes 2359304 | tf_op jit(solution)/shard_map/ppermute | solution.py:357
  3.7 1.2 %pack.1 = (bf16[16,512]{1,0:T(8,128)(2,1)S(1)}, bf16[16,512]{1,0:T(8,128)(2,1)S(1)}, bf16[320,128]{1,0:T(8,128)(2,1)S(1)}, bf16[320,128]{1,0:T(8,128)(2,1)S(1)}) custom-call(bf16[256,1536]{1,0:T(8,128)(2,1)} %nadir.4, bf16[256,1536]{1,0:T(8,128)(2,1)} %forward.3, bf16[256,1536]{1,0:T(8,128)(2,1)} %backward.4), custom_call_target="tpu_custom_call" | custom-call | bytes 393216 | tf_op jit(solution)/shard_map/pack/pallas_call | solution.py:372
  4.9 0.0 copy-start.2
  4.9 3.5 %collective-permute-start = (bf16[320,128]{1,0:T(8,128)(2,1)S(1)}, bf16[320,128]{1,0:T(8,128)(2,1)S(1)}, u32[]{:S(2)}, u32[]{:S(2)}) collective-permute-start(bf16[320,128]{1,0:T(8,128)(2,1)S(1)} %get-tuple-element.34), channel_id=1, source_target_pairs={{0,1},{1,2},{2,3},{4,5},{5,6},{6,7},{8,9},{9,10},{10,11},{12,13},{... | collective-permute-start | bytes 245768 | tf_op jit(solution)/shard_map/ppermute | solution.py:398
  8.4 1.3 %collective-permute-start.1 = (bf16[320,128]{1,0:T(8,128)(2,1)S(1)}, bf16[320,128]{1,0:T(8,128)(2,1)S(1)}, u32[]{:S(2)}, u32[]{:S(2)}) collective-permute-start(bf16[320,128]{1,0:T(8,128)(2,1)S(1)} %get-tuple-element.35), channel_id=1, source_target_pairs={{1,0},{2,1},{3,2},{5,4},{6,5},{7,6},{9,8},{10,9},{11,10},{13,12},{... | collective-permute-start | bytes 245768 | tf_op jit(solution)/shard_map/ppermute | solution.py:397
  9.7 1.2 %cut.1 = (bf16[64,1536]{1,0:T(8,128)(2,1)S(1)}, bf16[192,1152]{1,0:T(8,128)(2,1)S(1)}, bf16[192,384]{1,0:T(8,128)(2,1)S(1)}) custom-call(bf16[256,1536]{1,0:T(8,128)(2,1)} %backward.4), custom_call_target="tpu_custom_call" | custom-call | bytes 1572864 | tf_op jit(solution)/shard_map/cut/pallas_call | solution.py:372
  10.9 0.6 collective-permute-start.5
  12.2 0.6 fusion.11
  12.8 0.8 %pad_maximum_fusion.basis = f32[256,128]{1,0:T(8,128)} fusion(f32[256,64]{1,0:T(8,128)S(1)} %get-tuple-element.69, f32[256,64]{1,0:T(8,128)S(1)} %get-tuple-element.68), kind=kLoop, calls=%fused_computation.15 | loop fusion | flops 32768 | bytes 262144 | tf_op jit(solution)/shard_map/concatenate | solution.py:31
  13.6 1.9 %concatenate.23.params = f32[24,1536]{1,0:T(8,128)} concatenate(f32[1,1536]{1,0:T(1,128)S(1)} %get-tuple-element.67, f32[4,1536]{1,0:T(4,128)S(1)} %get-tuple-element.62, f32[3,1536]{1,0:T(4,128)S(1)} %broadcast_in_dim.58, f32[1,1536]{1,0:T(1,128)S(1)} %get-tuple-element.66, f32[4,1536]{1,0:T(4,128)S(1)} %get-tuple-element.61, f32[3,1536]{1,0:T(4,128)S(1)} %broadcast_in_dim.58, ...), dimensions={0} | concatenate | bytes 294912 | tf_op jit(solution)/shard_map/concatenate | solution.py:418
  15.5 0.6 copy-done.9
  16.2 0.6 copy-done.10
  16.8 0.9 %nadir_lines.1 = (bf16[16,1792]{1,0:T(8,128)(2,1)S(1)}, bf16[16,1792]{1,0:T(8,128)(2,1)S(1)}) custom-call(bf16[256,1536]{1,0:T(8,128)(2,1)} %nadir.4, bf16[320,128]{1,0:T(8,128)(2,1)} %copy-done.9, bf16[320,128]{1,0:T(8,128)(2,1)} %copy-done.10), custom_call_target="tpu_custom_call" | custom-call | bytes 229376 | tf_op jit(solution)/shard_map/nadir_lines/pallas_call | solution.py:372
  17.7 0.1 collective-permute-start.2
  17.8 2.6 %collective-permute-start.3 = (bf16[16,1792]{1,0:T(8,128)(2,1)S(1)}, bf16[16,1792]{1,0:T(8,128)(2,1)S(1)}, u32[]{:S(2)}, u32[]{:S(2)}) collective-permute-start(bf16[16,1792]{1,0:T(8,128)(2,1)S(1)} %get-tuple-element.37), channel_id=1, source_target_pairs={{0,28},{4,0},{8,4},{12,8},{16,12},{20,16},{24,20},{28,24},{1,29},{... | collective-permute-start | bytes 172040 | tf_op jit(solution)/shard_map/ppermute | solution.py:430
  20.4 1.5 %collective-permute-start.10 = (bf16[192,1152]{1,0:T(8,128)(2,1)S(1)}, bf16[192,1152]{1,0:T(8,128)(2,1)S(1)}, u32[]{:S(2)}, u32[]{:S(2)}) collective-permute-start(bf16[192,1152]{1,0:T(8,128)(2,1)S(1)} %get-tuple-element.49), channel_id=1, source_target_pairs={{0,16},{4,20},{8,24},{12,28},{16,0},{20,4},{24,8},{28,12},{1,17},{... | collective-permute-start | bytes 1327112 | tf_op jit(solution)/shard_map/ppermute | solution.py:357
  21.9 0.1 pad_add_fusion.place
  22.0 0.4 collective-permute-done.2.above
  22.4 1.3 %collective-permute-start.7 = (bf16[16,512]{1,0:T(8,128)(2,1)S(1)}, bf16[16,512]{1,0:T(8,128)(2,1)S(1)}, u32[]{:S(2)}, u32[]{:S(2)}) collective-permute-start(bf16[16,512]{1,0:T(8,128)(2,1)S(1)} %get-tuple-element.30), channel_id=1, source_target_pairs={{1,16},{2,17},{3,18},{5,20},{6,21},{7,22},{9,24},{10,25},{11,26},{... | collective-permute-start | bytes 49160 | tf_op jit(solution)/shard_map/ppermute | solution.py:395
  23.7 6.1 %collective-permute-start.6 = (bf16[16,512]{1,0:T(8,128)(2,1)S(1)}, bf16[16,512]{1,0:T(8,128)(2,1)S(1)}, u32[]{:S(2)}, u32[]{:S(2)}) collective-permute-start(bf16[16,512]{1,0:T(8,128)(2,1)S(1)} %get-tuple-element.45), channel_id=1, source_target_pairs={{0,17},{1,18},{2,19},{4,21},{5,22},{6,23},{8,25},{9,26},{10,27},{1... | collective-permute-start | bytes 49160 | tf_op jit(solution)/shard_map/ppermute | solution.py:396
  29.9 4.9 %prep.1 = (f32[272,1536]{1,0:T(8,128)}, bf16[272,1536]{1,0:T(8,128)(2,1)}, f32[256,1536]{1,0:T(8,128)}, f32[8,256]{1,0:T(8,128)S(1)}, bf16[2,272,192]{2,1,0:T(8,128)(2,1)}) custom-call(s32[2]{0:T(128)S(1)} %pad_add_fusion.place, bf16[256,1536]{1,0:T(8,128)(2,1)} %nadir.4, bf16[320,128]{1,0:T(8,128)(2,1)} %copy-done.9, bf16[320,128]{1,0:T(8,128)(2,1)} %copy-done.10, ...), custom_call_target="tpu_custom_call" | custom-call | flops 427819008 | bytes 5013504 | tf_op jit(solution)/shard_map/prep/pallas_call | solution.py:433
  34.8 0.9 %copy-done.5 = bf16[256,1536]{1,0:T(8,128)(2,1)} copy-done((bf16[256,1536]{1,0:T(8,128)(2,1)}, bf16[256,1536]{1,0:T(8,128)(2,1)S(1)}, u32[]{:S(2)}) %copy-start.5) | copy-done | bytes 786456
  35.7 0.7 copy-done.3
  36.4 2.5 %lines.1 = (bf16[80,1536]{1,0:T(8,128)(2,1)S(1)}, bf16[80,1536]{1,0:T(8,128)(2,1)S(1)}) custom-call(s32[2]{0:T(128)S(1)} %pad_add_fusion.place, bf16[256,1536]{1,0:T(8,128)(2,1)} %forward.3, bf16[256,1536]{1,0:T(8,128)(2,1)} %backward.4, bf16[320,128]{1,0:T(8,128)(2,1)} %copy-done.9, bf16[320,128]{1,0:T(8,128)(2,1)} %copy-done.10, ...), custom_call_target="tpu_custom_call" | custom-call | bytes 983040 | tf_op jit(solution)/shard_map/lines/pallas_call | solution.py:372
  38.9 0.1 collective-permute-start.8
  39.0 1.7 %collective-permute-start.9 = (bf16[80,1536]{1,0:T(8,128)(2,1)S(1)}, bf16[80,1536]{1,0:T(8,128)(2,1)S(1)}, u32[]{:S(2)}, u32[]{:S(2)}) collective-permute-start(bf16[80,1536]{1,0:T(8,128)(2,1)S(1)} %get-tuple-element.47), channel_id=1, source_target_pairs={{0,12},{4,0},{8,4},{12,8},{16,28},{20,16},{24,20},{28,24},{1,13},{... | collective-permute-start | bytes 737288 | tf_op jit(solution)/shard_map/ppermute | solution.py:473
  40.7 0.8 %collective-permute-start.11 = (bf16[192,384]{1,0:T(8,128)(2,1)S(1)}, bf16[192,384]{1,0:T(8,128)(2,1)S(1)}, u32[]{:S(2)}, u32[]{:S(2)}) collective-permute-start(bf16[192,384]{1,0:T(8,128)(2,1)S(1)} %get-tuple-element.53), channel_id=1, source_target_pairs={{0,16},{4,20},{8,24},{12,28},{16,0},{20,4},{24,8},{28,12},{1,17},{... | collective-permute-start | bytes 442376 | tf_op jit(solution)/shard_map/ppermute | solution.py:357
  41.5 4.9 %collective-permute-done.8.above = bf16[80,1536]{1,0:T(8,128)(2,1)S(1)} collective-permute-done((bf16[80,1536]{1,0:T(8,128)(2,1)S(1)}, bf16[80,1536]{1,0:T(8,128)(2,1)S(1)}, u32[]{:S(2)}, u32[]{:S(2)}) %collective-permute-start.8) | collective-permute-done | bytes 245792 | tf_op jit(solution)/shard_map/ppermute | solution.py:474
  46.5 0.6 broadcast_in_dim.60.earlier
  47.1 0.1 copy-done.6
  47.2 0.1 copy-done.7
  47.2 5.9 %slab0_0.1 = (bf16[2,256,1536]{2,1,0:T(8,128)(2,1)}, f32[8,128]{1,0:T(8,128)S(1)}) custom-call(f32[272,1536]{1,0:T(8,128)} %get-tuple-element.38.slopes, bf16[272,1536]{1,0:T(8,128)(2,1)} %get-tuple-element.39.center, f32[256,1536]{1,0:T(8,128)} %get-tuple-element.40.texture, bf16[2,272,192]{2,1,0:T(8,128)(2,1)} %get-tuple-element.41.bands, ...), custom_call_target="tpu_custom_call" | custom-call | flops 877363200 | bytes 8355840 | tf_op jit(solution)/shard_map/slab0_0/pallas_call | solution.py:489
  53.2 0.6 copy-done.1
  53.8 0.8 %copy-done.8 = bf16[192,1152]{1,0:T(8,128)(2,1)} copy-done((bf16[192,1152]{1,0:T(8,128)(2,1)}, bf16[192,1152]{1,0:T(8,128)(2,1)S(1)}, u32[]{:S(2)}) %copy-start.8) | copy-done | bytes 442392
  54.6 4.6 %slab1_0.1 = (bf16[2,256,1536]{2,1,0:T(8,128)(2,1)}, f32[8,128]{1,0:T(8,128)S(1)}) custom-call(f32[272,1536]{1,0:T(8,128)} %get-tuple-element.38.slopes, bf16[272,1536]{1,0:T(8,128)(2,1)} %get-tuple-element.39.center, f32[256,1536]{1,0:T(8,128)} %get-tuple-element.40.texture, ...), custom_call_target="tpu_custom_call", output_to_operand_aliasing={{0}: (14, {})} | custom-call | flops 626688000 | bytes 5570560 | tf_op jit(solution)/shard_map/slab1_0/pallas_call | solution.py:489
  59.2 0.6 copy-done
  59.8 0.6 copy-done.13
  60.4 3.4 %slab1_1024.1 = (bf16[2,256,1536]{2,1,0:T(8,128)(2,1)}, f32[8,128]{1,0:T(8,128)S(1)}) custom-call(f32[272,1536]{1,0:T(8,128)} %get-tuple-element.38.slopes, bf16[272,1536]{1,0:T(8,128)(2,1)} %get-tuple-element.39.center, f32[256,1536]{1,0:T(8,128)} %get-tuple-element.40.texture, ...), custom_call_target="tpu_custom_call", output_to_operand_aliasing={{0}: (15, {})} | custom-call | flops 376012800 | bytes 2785280 | tf_op jit(solution)/shard_map/slab1_1024/pallas_call | solution.py:489
  63.9 2.0 %collective-permute-start.12 = (f32[8,384]{1,0:T(8,128)S(1)}, f32[8,384]{1,0:T(8,128)S(1)}, u32[]{:S(2)}, u32[]{:S(2)}) collective-permute-start(f32[8,384]{1,0:T(8,128)S(1)} %constant_dynamic-update-slice_fusion), channel_id=1, source_target_pairs={{0,1},{1,2},{2,3},{3,0},{4,5},{5,6},{6,7},{7,4},{8,9},{9,10},{10,1... | collective-permute-start | bytes 36872 | tf_op jit(solution)/shard_map/ppermute | solution.py:538
  65.9 1.1 %collective-permute-start.13 = (f32[8,384]{1,0:T(8,128)S(1)}, f32[8,384]{1,0:T(8,128)S(1)}, u32[]{:S(2)}, u32[]{:S(2)}) collective-permute-start(f32[8,384]{1,0:T(8,128)S(1)} %constant_dynamic-update-slice_fusion), channel_id=1, source_target_pairs={{0,2},{1,3},{2,0},{3,1},{4,6},{5,7},{6,4},{7,5},{8,10},{9,11},{10,... | collective-permute-start | bytes 36872 | tf_op jit(solution)/shard_map/ppermute | solution.py:538
  67.0 2.8 %collective-permute-start.14 = (f32[8,384]{1,0:T(8,128)S(1)}, f32[8,384]{1,0:T(8,128)S(1)}, u32[]{:S(2)}, u32[]{:S(2)}) collective-permute-start(f32[8,384]{1,0:T(8,128)S(1)} %constant_dynamic-update-slice_fusion), channel_id=1, source_target_pairs={{0,3},{1,0},{2,1},{3,2},{4,7},{5,4},{6,5},{7,6},{8,11},{9,8},{10,9... | collective-permute-start | bytes 36872 | tf_op jit(solution)/shard_map/ppermute | solution.py:538
  69.8 0.7 collective-permute-done.13
  70.5 0.7 collective-permute-done.14
  71.2 0.3 select_multiply_fusion.1
  71.5 0.1 select_multiply_fusion
  71.7 0.5 fusion.6
  72.2 0.6 constant_dynamic-slice_fusion
  72.7 0.6 maximum_bitcast_fusion
  (52 shorter events, 0.2 us)
Async XLA Ops:
  0.6 10.8 %copy-start.15 = (s32[2,1536]{1,0:T(2,128)S(1)}, s32[2,1536]{1,0:T(2,128)}, u32[]{:S(2)}) copy-start(s32[2,1536]{1,0:T(2,128)} %param.15) | copy-start | bytes 36868
  0.6 12.1 %copy-start.14 = (bf16[2,4,1536]{2,1,0:T(4,128)(2,1)S(1)}, bf16[2,4,1536]{2,1,0:T(4,128)(2,1)}, u32[]{:S(2)}) copy-start(bf16[2,4,1536]{2,1,0:T(4,128)(2,1)} %param.13) | copy-start | bytes 73732
  0.7 34.1 %collective-permute-start.4 = (bf16[256,1536]{1,0:T(8,128)(2,1)}, bf16[256,1536]{1,0:T(8,128)(2,1)S(1)}, u32[]{:S(2)}, u32[]{:S(2)}) collective-permute-start(bf16[256,1536]{1,0:T(8,128)(2,1)} %forward.3), channel_id=1, source_target_pairs={{0,16},{4,20},{8,24},{12,28},{16,0},{20,4},{24,8},{28,12},{1,17},{... | collective-permute-start | bytes 2359304 | tf_op jit(solution)/shard_map/ppermute | solution.py:357
  4.9 25.0 %copy-start.2 = (s32[2048]{0:T(1024)S(1)}, s32[2048]{0:T(1024)}, u32[]{:S(2)}) copy-start(s32[2048]{0:T(1024)} %param.16) | copy-start | bytes 24580
  4.9 10.6 %collective-permute-start = (bf16[320,128]{1,0:T(8,128)(2,1)S(1)}, bf16[320,128]{1,0:T(8,128)(2,1)S(1)}, u32[]{:S(2)}, u32[]{:S(2)}) collective-permute-start(bf16[320,128]{1,0:T(8,128)(2,1)S(1)} %get-tuple-element.34), channel_id=1, source_target_pairs={{0,1},{1,2},{2,3},{4,5},{5,6},{6,7},{8,9},{9,10},{10,11},{12,13},{... | collective-permute-start | bytes 245768 | tf_op jit(solution)/shard_map/ppermute | solution.py:398
  8.4 7.2 %collective-permute-start.1 = (bf16[320,128]{1,0:T(8,128)(2,1)S(1)}, bf16[320,128]{1,0:T(8,128)(2,1)S(1)}, u32[]{:S(2)}, u32[]{:S(2)}) collective-permute-start(bf16[320,128]{1,0:T(8,128)(2,1)S(1)} %get-tuple-element.35), channel_id=1, source_target_pairs={{1,0},{2,1},{3,2},{5,4},{6,5},{7,6},{9,8},{10,9},{11,10},{13,12},{... | collective-permute-start | bytes 245768 | tf_op jit(solution)/shard_map/ppermute | solution.py:397
  10.9 23.9 %collective-permute-start.5 = (bf16[64,1536]{1,0:T(8,128)(2,1)S(1)}, bf16[64,1536]{1,0:T(8,128)(2,1)S(1)}, u32[]{:S(2)}, u32[]{:S(2)}) collective-permute-start(bf16[64,1536]{1,0:T(8,128)(2,1)S(1)} %get-tuple-element.44), channel_id=1, source_target_pairs={{0,16},{4,20},{8,24},{12,28},{16,0},{20,4},{24,8},{28,12},{1,17},{... | collective-permute-start | bytes 589832 | tf_op jit(solution)/shard_map/ppermute | solution.py:357
  15.5 0.6 copy-start.9
  16.2 0.6 copy-start.10
  17.7 4.7 %collective-permute-start.2 = (bf16[16,1792]{1,0:T(8,128)(2,1)S(1)}, bf16[16,1792]{1,0:T(8,128)(2,1)S(1)}, u32[]{:S(2)}, u32[]{:S(2)}) collective-permute-start(bf16[16,1792]{1,0:T(8,128)(2,1)S(1)} %get-tuple-element.36), channel_id=1, source_target_pairs={{0,4},{4,8},{8,12},{12,16},{16,20},{20,24},{24,28},{28,0},{1,5},{5... | collective-permute-start | bytes 172040 | tf_op jit(solution)/shard_map/ppermute | solution.py:431
  17.8 5.9 %collective-permute-start.3 = (bf16[16,1792]{1,0:T(8,128)(2,1)S(1)}, bf16[16,1792]{1,0:T(8,128)(2,1)S(1)}, u32[]{:S(2)}, u32[]{:S(2)}) collective-permute-start(bf16[16,1792]{1,0:T(8,128)(2,1)S(1)} %get-tuple-element.37), channel_id=1, source_target_pairs={{0,28},{4,0},{8,4},{12,8},{16,12},{20,16},{24,20},{28,24},{1,29},{... | collective-permute-start | bytes 172040 | tf_op jit(solution)/shard_map/ppermute | solution.py:430
  20.4 33.3 %collective-permute-start.10 = (bf16[192,1152]{1,0:T(8,128)(2,1)S(1)}, bf16[192,1152]{1,0:T(8,128)(2,1)S(1)}, u32[]{:S(2)}, u32[]{:S(2)}) collective-permute-start(bf16[192,1152]{1,0:T(8,128)(2,1)S(1)} %get-tuple-element.49), channel_id=1, source_target_pairs={{0,16},{4,20},{8,24},{12,28},{16,0},{20,4},{24,8},{28,12},{1,17},{... | collective-permute-start | bytes 1327112 | tf_op jit(solution)/shard_map/ppermute | solution.py:357
  22.4 7.5 %copy-start.16 = (bf16[16,1792]{1,0:T(8,128)(2,1)}, bf16[16,1792]{1,0:T(8,128)(2,1)S(1)}, u32[]{:S(2)}) copy-start(bf16[16,1792]{1,0:T(8,128)(2,1)S(1)} %collective-permute-done.2.above) | copy-start | bytes 172036
  22.4 12.4 %collective-permute-start.7 = (bf16[16,512]{1,0:T(8,128)(2,1)S(1)}, bf16[16,512]{1,0:T(8,128)(2,1)S(1)}, u32[]{:S(2)}, u32[]{:S(2)}) collective-permute-start(bf16[16,512]{1,0:T(8,128)(2,1)S(1)} %get-tuple-element.30), channel_id=1, source_target_pairs={{1,16},{2,17},{3,18},{5,20},{6,21},{7,22},{9,24},{10,25},{11,26},{... | collective-permute-start | bytes 49160 | tf_op jit(solution)/shard_map/ppermute | solution.py:395
  23.7 6.2 %copy-start.17 = (bf16[16,1792]{1,0:T(8,128)(2,1)}, bf16[16,1792]{1,0:T(8,128)(2,1)S(1)}, u32[]{:S(2)}) copy-start(bf16[16,1792]{1,0:T(8,128)(2,1)S(1)} %collective-permute-done.3.below) | copy-start | bytes 172036
  23.7 11.1 %collective-permute-start.6 = (bf16[16,512]{1,0:T(8,128)(2,1)S(1)}, bf16[16,512]{1,0:T(8,128)(2,1)S(1)}, u32[]{:S(2)}, u32[]{:S(2)}) collective-permute-start(bf16[16,512]{1,0:T(8,128)(2,1)S(1)} %get-tuple-element.45), channel_id=1, source_target_pairs={{0,17},{1,18},{2,19},{4,21},{5,22},{6,23},{8,25},{9,26},{10,27},{1... | collective-permute-start | bytes 49160 | tf_op jit(solution)/shard_map/ppermute | solution.py:396
  34.7 0.9 %copy-start.5 = (bf16[256,1536]{1,0:T(8,128)(2,1)}, bf16[256,1536]{1,0:T(8,128)(2,1)S(1)}, u32[]{:S(2)}) copy-start(bf16[256,1536]{1,0:T(8,128)(2,1)S(1)} %collective-permute-done.4.lead.rest_0_) | copy-start | bytes 2359300
  34.8 0.9 %copy-start.11 = (bf16[16,512]{1,0:T(8,128)(2,1)}, bf16[16,512]{1,0:T(8,128)(2,1)S(1)}, u32[]{:S(2)}) copy-start(bf16[16,512]{1,0:T(8,128)(2,1)S(1)} %collective-permute-done.7.right) | copy-start | bytes 49156
  34.8 0.9 %copy-start.12 = (bf16[16,512]{1,0:T(8,128)(2,1)}, bf16[16,512]{1,0:T(8,128)(2,1)S(1)}, u32[]{:S(2)}) copy-start(bf16[16,512]{1,0:T(8,128)(2,1)S(1)} %collective-permute-done.6.left) | copy-start | bytes 49156
  35.7 0.7 copy-start.3
  38.9 7.6 %collective-permute-start.8 = (bf16[80,1536]{1,0:T(8,128)(2,1)S(1)}, bf16[80,1536]{1,0:T(8,128)(2,1)S(1)}, u32[]{:S(2)}, u32[]{:S(2)}) collective-permute-start(bf16[80,1536]{1,0:T(8,128)(2,1)S(1)} %get-tuple-element.46), channel_id=1, source_target_pairs={{0,4},{4,8},{8,12},{12,0},{16,20},{20,24},{24,28},{28,16},{1,5},{5... | collective-permute-start | bytes 737288 | tf_op jit(solution)/shard_map/ppermute | solution.py:474
  39.0 7.5 %collective-permute-start.9 = (bf16[80,1536]{1,0:T(8,128)(2,1)S(1)}, bf16[80,1536]{1,0:T(8,128)(2,1)S(1)}, u32[]{:S(2)}, u32[]{:S(2)}) collective-permute-start(bf16[80,1536]{1,0:T(8,128)(2,1)S(1)} %get-tuple-element.47), channel_id=1, source_target_pairs={{0,12},{4,0},{8,4},{12,8},{16,28},{20,16},{24,20},{28,24},{1,13},{... | collective-permute-start | bytes 737288 | tf_op jit(solution)/shard_map/ppermute | solution.py:473
  40.7 19.1 %collective-permute-start.11 = (bf16[192,384]{1,0:T(8,128)(2,1)S(1)}, bf16[192,384]{1,0:T(8,128)(2,1)S(1)}, u32[]{:S(2)}, u32[]{:S(2)}) collective-permute-start(bf16[192,384]{1,0:T(8,128)(2,1)S(1)} %get-tuple-element.53), channel_id=1, source_target_pairs={{0,16},{4,20},{8,24},{12,28},{16,0},{20,4},{24,8},{28,12},{1,17},{... | collective-permute-start | bytes 442376 | tf_op jit(solution)/shard_map/ppermute | solution.py:357
  46.5 0.7 copy-start.6
  46.5 0.8 %copy-start.7 = (bf16[80,1536]{1,0:T(8,128)(2,1)}, bf16[80,1536]{1,0:T(8,128)(2,1)S(1)}, u32[]{:S(2)}) copy-start(bf16[80,1536]{1,0:T(8,128)(2,1)S(1)} %collective-permute-done.9.below) | copy-start | bytes 737284
  53.2 0.6 copy-start.1
  53.8 0.8 %copy-start.8 = (bf16[192,1152]{1,0:T(8,128)(2,1)}, bf16[192,1152]{1,0:T(8,128)(2,1)S(1)}, u32[]{:S(2)}) copy-start(bf16[192,1152]{1,0:T(8,128)(2,1)S(1)} %collective-permute-done.10.rest_2_) | copy-start | bytes 1327108
  59.2 0.6 copy-start
  59.8 0.7 copy-start.13
  60.4 11.3 %copy-start.4 = (f32[256,128]{1,0:T(8,128)S(1)}, f32[256,128]{1,0:T(8,128)}, u32[]{:S(2)}) copy-start(f32[256,128]{1,0:T(8,128)} %pad_maximum_fusion.basis) | copy-start | bytes 393220
  63.9 6.0 %collective-permute-start.12 = (f32[8,384]{1,0:T(8,128)S(1)}, f32[8,384]{1,0:T(8,128)S(1)}, u32[]{:S(2)}, u32[]{:S(2)}) collective-permute-start(f32[8,384]{1,0:T(8,128)S(1)} %constant_dynamic-update-slice_fusion), channel_id=1, source_target_pairs={{0,1},{1,2},{2,3},{3,0},{4,5},{5,6},{6,7},{7,4},{8,9},{9,10},{10,1... | collective-permute-start | bytes 36872 | tf_op jit(solution)/shard_map/ppermute | solution.py:538
  65.9 4.7 %collective-permute-start.13 = (f32[8,384]{1,0:T(8,128)S(1)}, f32[8,384]{1,0:T(8,128)S(1)}, u32[]{:S(2)}, u32[]{:S(2)}) collective-permute-start(f32[8,384]{1,0:T(8,128)S(1)} %constant_dynamic-update-slice_fusion), channel_id=1, source_target_pairs={{0,2},{1,3},{2,0},{3,1},{4,6},{5,7},{6,4},{7,5},{8,10},{9,11},{10,... | collective-permute-start | bytes 36872 | tf_op jit(solution)/shard_map/ppermute | solution.py:538
  67.0 4.3 %collective-permute-start.14 = (f32[8,384]{1,0:T(8,128)S(1)}, f32[8,384]{1,0:T(8,128)S(1)}, u32[]{:S(2)}, u32[]{:S(2)}) collective-permute-start(f32[8,384]{1,0:T(8,128)S(1)} %constant_dynamic-update-slice_fusion), channel_id=1, source_target_pairs={{0,3},{1,0},{2,1},{3,2},{4,7},{5,4},{6,5},{7,6},{8,11},{9,8},{10,9... | collective-permute-start | bytes 36872 | tf_op jit(solution)/shard_map/ppermute | solution.py:538

commit v3 on v2

v3 whole, which is shorter than its diff:
```python
import functools
import math

import jax
import jax.numpy as jnp
from jax import lax
from jax.experimental import pallas as pl
from jax.experimental.pallas import tpu as pltpu
from jax.sharding import PartitionSpec as P

TAPS = 4
CAMERA_LAG = 20480
BOX = 4
MODES = 64
LINE_RIM = 32
NADIR_RIM = 16
TILE = 128
WIDE = 256
EDGE = 16


def pairs_of(count, step):
    return [(i, i + step) for i in range(count) if 0 <= i + step < count]


def harmonics(absolute):
    period = 4 * MODES
    factor = 2 * jnp.arange(MODES, dtype=jnp.int32) + 1
    phases = (absolute % period)[:, None] * factor[None, :] % period
    angles = phases.astype(jnp.float32) * (2.0 * jnp.pi / period)
    return jnp.concatenate([jnp.cos(angles), jnp.sin(angles)], axis=1)


def box_sum(x, lines):
    rows = x.shape[0]
    two = x + pltpu.roll(x, rows - 1, 0)
    four = two + pltpu.roll(two, rows - 2, 0)
    eight = four + pltpu.roll(four, rows - 4, 0)
    return eight[:lines] + x[2 * BOX : lines + 2 * BOX]


def lane_fold(x):
    folded = x[:, :TILE]
    for at in range(TILE, x.shape[1], TILE):
        folded = folded + x[:, at : at + TILE]
    return folded


def copy_all(moves, sem):
    copies = [pltpu.make_async_copy(a, b, sem.at[n]) for n, (a, b) in enumerate(moves)]
    for copy in copies:
        copy.start()
    for copy in copies:
        copy.wait()


def pack_kernel(
    lines, cols, nadir, forward, backward, crossing, near_first, near_last, side, sem
):
    moves = []
    for n, (begin, near) in enumerate(((0, near_first), (cols - TILE, near_last))):
        moves.append((nadir.at[:, pl.ds(begin, TILE)], near.at[pl.ds(0, lines), :]))
        for s, slab in enumerate((forward, backward)):
            moves.append((slab.at[:, pl.ds(begin, TILE)], side.at[s, n]))
    copy_all(moves, sem)
    for n, (row, near) in enumerate(((0, near_first), (TILE - EDGE, near_last))):
        for s in range(2):
            turned = side[s, n].astype(jnp.float32).T[row : row + EDGE].astype(jnp.bfloat16)
            for k in range(lines // TILE):
                at = lines + (s * (lines // TILE) + k) * EDGE
                near[at : at + EDGE, :] = turned[:, k * TILE : (k + 1) * TILE]


def cross_kernel(lines, forward, backward, crossing, sem):
    moves = [(forward, crossing.at[pl.ds(0, lines), :])]
    for n, row in enumerate((0, lines - LINE_RIM)):
        target = pl.ds(lines + n * LINE_RIM, LINE_RIM)
        moves.append((backward.at[pl.ds(row, LINE_RIM), :], crossing.at[target, :]))
    copy_all(moves, sem)


def nadir_lines_kernel(lines, cols, nadir, from_left, from_right, params, basis, first, last, sem):
    moves = []
    for out, row in ((first, 0), (last, lines - NADIR_RIM)):
        span, top = pl.ds(row, NADIR_RIM), pl.ds(0, NADIR_RIM)
        moves.append((from_left.at[span, :], out.at[top, pl.ds(0, TILE)]))
        moves.append((nadir.at[span, :], out.at[top, pl.ds(TILE, cols)]))
        moves.append((from_right.at[span, :], out.at[top, pl.ds(TILE + cols, TILE)]))
        for n, near in enumerate((from_left, from_right)):
            for k in range(2 * lines // TILE):
                moves.append(
                    (
                        near.at[pl.ds(lines + k * EDGE, EDGE), :],
                        out.at[pl.ds(NADIR_RIM, EDGE), pl.ds(2 * n * lines + k * TILE, TILE)],
                    )
                )
        out[NADIR_RIM:, 4 * lines :] = jnp.zeros((EDGE, cols + 2 * TILE - 4 * lines), jnp.bfloat16)
    copy_all(moves, sem)


def middle_kernel(lines, cols, backward, own, above, below, middle, sem):
    height = lines - 2 * LINE_RIM
    row, packed = pl.ds(height, EDGE), slice(NADIR_RIM, NADIR_RIM + EDGE)
    moves = [
        (backward.at[pl.ds(LINE_RIM, height), :], middle.at[pl.ds(0, height), :]),
        (
            own.at[pl.ds(NADIR_RIM, EDGE), pl.ds(0, 4 * lines)],
            middle.at[row, pl.ds(0, 4 * lines)],
        ),
    ]
    lane = lax.broadcasted_iota(jnp.int32, (EDGE, TILE), 1)
    for k in range(4):
        ahead = above[packed, (k + 1) * lines - TILE : (k + 1) * lines].astype(jnp.float32)
        behind = below[packed, k * lines : k * lines + TILE].astype(jnp.float32)
        both = jnp.where(lane < TILE // 2, behind, ahead).astype(jnp.bfloat16)
        middle[height : height + EDGE, 4 * lines + k * TILE : 4 * lines + (k + 1) * TILE] = both
    copy_all(moves, sem)


def lines_kernel(lines, half_ring, place, forward, backward, crossed, down, up, sem):
    in_half = lax.rem(place[0], half_ring)
    most, least = LINE_RIM, LINE_RIM // 2
    for out, counts, raw_place in ((down, (least, most), 0), (up, (most, least), half_ring - 1)):
        starts = (0, 0) if out is down else (lines - counts[0], lines - counts[1])
        ended = lines if out is down else lines + 2 * LINE_RIM - counts[1]
        tops = pl.ds(0, counts[0]), pl.ds(counts[0], counts[1])

        @pl.when(in_half == raw_place)
        def _(out=out, counts=counts, starts=starts, tops=tops):
            copy_all(
                [
                    (slab.at[pl.ds(start, count), :], out.at[top, :])
                    for slab, start, count, top in zip((forward, backward), starts, counts, tops)
                ],
                sem,
            )

        @pl.when(in_half != raw_place)
        def _(out=out, counts=counts, starts=starts, ended=ended, tops=tops):
            copy_all(
                [
                    (crossed.at[pl.ds(starts[0], counts[0]), :], out.at[tops[0], :]),
                    (crossed.at[pl.ds(ended, counts[1]), :], out.at[tops[1], :]),
                ],
                sem,
            )


def positions(place, cols, total_cols, at, span):
    column = lax.broadcasted_iota(jnp.int32, (1, span), 1) + (place[1] * cols + at)
    position = (column.astype(jnp.float32) + 0.5) / total_cols + 0.25
    return position, position * position


def prep_kernel(
    lines, cols, total_lines, total_cols, lag_floor, place,
    nadir, left, right, above, below, lag, offsets, weights, down,
    slopes, center, texture, sums, bands, framed, slope_v, center_v, texture_v, bands_v, sem,
):
    tall = lines + 2 * NADIR_RIM
    rows = lines + 16
    framed[0:NADIR_RIM, :] = above[0:NADIR_RIM, :]
    framed[NADIR_RIM + lines : tall, :] = below[0:NADIR_RIM, :]
    framed[NADIR_RIM : NADIR_RIM + lines, 0:TILE] = left[0:lines, :]
    framed[NADIR_RIM : NADIR_RIM + lines, TILE : TILE + cols] = nadir[...]
    framed[NADIR_RIM : NADIR_RIM + lines, TILE + cols :] = right[0:lines, :]
    row = lax.broadcasted_iota(jnp.int32, (2 * WIDE, WIDE), 0)
    col = lax.broadcasted_iota(jnp.int32, (2 * WIDE, WIDE), 1)
    gap = jnp.abs(row - TILE - col)
    smear = jnp.where(gap == 0, 2.0, jnp.where(gap == 1, 1.0, 0.0)).astype(jnp.bfloat16)
    totals = [jnp.zeros((lines, TILE), jnp.float32) for _ in range(3)]
    copies = []
    for at in range(0, cols, WIDE):
        across = jnp.dot(
            framed[:, at : at + 2 * WIDE], smear, preferred_element_type=jnp.float32
        )
        change = pltpu.roll(across, tall - 5, 0) - pltpu.roll(across, tall - 3, 0)
        slope = change[8 : 8 + rows] * 0.25
        slope_v[:, at : at + WIDE] = slope
        middle = framed[:, TILE + at : TILE + at + WIDE].astype(jnp.float32)
        middle = pltpu.roll(middle, tall - 4, 0)[8 : 8 + rows]
        center_v[:, at : at + WIDE] = middle.astype(jnp.bfloat16)
        level = box_sum(slope * slope, lines) * (1.0 / (2 * BOX + 1))
        texture_v[:, at : at + WIDE] = level
        for source, target in ((slope_v, slopes), (center_v, center), (texture_v, texture)):
            window = (slice(None), pl.ds(at, WIDE))
            copy = pltpu.make_async_copy(source.at[window], target.at[window], sem.at[len(copies)])
            copy.start()
            copies.append(copy)
        position, square = positions(place, cols, total_cols, at, WIDE)
        for k, lever in enumerate((square, square * position, square * square)):
            totals[k] = totals[k] + lane_fold(level * lever)
    lane = lax.broadcasted_iota(jnp.int32, (lines, TILE), 1)
    packed = jnp.zeros((lines, TILE), jnp.float32)
    for k in range(3):
        packed = jnp.where(lane == k, jnp.sum(totals[k], axis=1, keepdims=True), packed)
    sums[...] = packed.T[0:8, :] * (1.0 / (lines * total_cols))
    begin = place[0] * lines
    ahead = pl.multiple_of(lax.rem(begin + total_lines - TILE, total_lines), TILE)
    behind = pl.multiple_of(lax.rem(begin + lines, total_lines), TILE)
    begin = pl.multiple_of(begin, TILE)

    def window(ref, lead):
        parts = [
            ref[lead + (slice(None), pl.ds(start, size))].astype(jnp.float32)
            for start, size in ((ahead, TILE), (begin, lines), (behind, TILE))
        ]
        return jnp.concatenate(parts, axis=1)

    wide = lines + 2 * TILE
    lags = window(lag, ()) - float(lag_floor)
    shifts = window(offsets, ())
    stacked = jnp.concatenate(
        [
            jnp.broadcast_to(shifts[0:1] - lags, (8, wide)),
            jnp.broadcast_to(shifts[1:2] + lags, (8, wide)),
            window(weights, (0,)),
            window(weights, (1,)),
            jnp.zeros((TILE - 24, wide), jnp.float32),
        ],
        axis=0,
    )
    as_columns = pltpu.roll(stacked.T, wide - (TILE - BOX), 0)[0:rows]
    half = lines // 2
    depth = half + 2 * LINE_RIM
    for s in range(2):
        for first, last in ((0, half), (half, rows)):
            at = lax.broadcasted_iota(jnp.int32, (last - first, depth), 1)
            own = lax.broadcasted_iota(jnp.int32, (last - first, depth), 0)
            distance = (at - own - (LINE_RIM - BOX)).astype(jnp.float32)
            distance = distance - as_columns[first:last, 8 * s : 8 * s + 1]
            band = jnp.zeros((last - first, depth), jnp.float32)
            for tap in range(TAPS):
                weight = as_columns[first:last, 16 + 4 * s + tap : 17 + 4 * s + tap]
                band = jnp.where(distance == float(tap), weight, band)
            bands_v[s, first:last, :] = band.astype(jnp.bfloat16)
    copy = pltpu.make_async_copy(bands_v, bands, sem.at[len(copies)])
    copy.start()
    for waited in (*copies, copy):
        waited.wait()


def slab_kernel(
    lines, cols, jobs, fresh,
    slopes, center, texture, bands, params, basis, earlier, above, below, crossed, *rest,
):
    middle = None
    if not fresh:
        middle, rest = rest[0], rest[2:]
    parallax, pulled, bands_v, params_v, basis_v, earlier_v, sem, *scratch = rest
    rows = lines + 16
    half = lines // 2
    depth = half + 2 * LINE_RIM
    height = lines - 2 * LINE_RIM
    most, least = LINE_RIM, LINE_RIM // 2
    copies = []

    def fetch(source, target):
        copy = pltpu.make_async_copy(source, target, sem.at[len(copies)])
        copy.start()
        copies.append(copy)

    fetch(bands, bands_v)
    fetch(params, params_v)
    loads = []
    for n, (s, first, width) in enumerate(jobs):
        ext, along, slope_v, center_v, texture_v, packed, result = scratch[7 * n : 7 * n + 7]
        low, high = first - TILE, first + width + TILE
        over, under = ((most, least), (least, most))[s]
        begin, end = max(low, 0), min(high, cols)
        columns, inside = pl.ds(begin, end - begin), pl.ds(begin - low, end - begin)
        pieces = [
            (above, (0, most)[s], LINE_RIM - over, over),
            (below, (0, least)[s], LINE_RIM + lines, under),
        ]
        if s == 0:
            pieces.append((crossed, 0, LINE_RIM, lines))
        else:
            pieces.append((crossed, lines, LINE_RIM, LINE_RIM))
            pieces.append((crossed, lines + LINE_RIM, lines, LINE_RIM))
            pieces.append((middle, 0, 2 * LINE_RIM, height))
        for ref, row, target, count in pieces:
            fetch(ref.at[pl.ds(row, count), columns], ext.at[pl.ds(target, count), inside])
        for side in range(2):
            if (low < 0, high > cols)[side]:
                kind = 2 * side + s
                row = pl.ds(height, EDGE)
                fetch(middle.at[row, pl.ds(kind * lines, lines)], packed.at[side, :, pl.ds(0, lines)])
                fetch(
                    middle.at[row, pl.ds(4 * lines + kind * TILE, TILE)],
                    packed.at[side, :, pl.ds(lines, TILE)],
                )
        loaded = len(copies)
        columns = pl.ds(first, width)
        fetch(slopes.at[:, columns], slope_v)
        fetch(center.at[:, columns], center_v)
        fetch(texture.at[:, columns], texture_v)
        loads.append((loaded, len(copies)))
    fetch(basis, basis_v)
    fetch(earlier, earlier_v)
    waited, writes = 0, []
    pulls = [jnp.zeros((lines, TILE), jnp.float32) for _ in range(2)]
    for n, (s, first, width) in enumerate(jobs):
        ext, along, slope_v, center_v, texture_v, packed, result = scratch[7 * n : 7 * n + 7]
        low, high = first - TILE, first + width + TILE
        over, under = ((most, least), (least, most))[s]
        blank = jnp.zeros((least, width + 2 * TILE), jnp.bfloat16)
        if s == 0:
            ext[2 * LINE_RIM + lines - least :, :] = blank
        else:
            ext[:least, :] = blank
        for copy in copies[waited : loads[n][0]]:
            copy.wait()
        for side in range(2):
            if (low < 0, high > cols)[side]:
                at = 0 if side == 0 else width + TILE
                piece = packed[side].astype(jnp.float32)
                gap = jnp.zeros((TILE - EDGE, lines + TILE), jnp.float32)
                piece = jnp.concatenate([gap, piece] if side == 0 else [piece, gap], axis=0)
                turned = piece.T.astype(jnp.bfloat16)
                ext[LINE_RIM : LINE_RIM + lines, at : at + TILE] = turned[:lines]
                ext[LINE_RIM - over : LINE_RIM, at : at + TILE] = turned[lines + TILE - over :]
                ext[LINE_RIM + lines : LINE_RIM + lines + under, at : at + TILE] = turned[
                    lines : lines + under
                ]
        for at in range(0, width + 2 * TILE, WIDE):
            end = min(at + WIDE, width + 2 * TILE)
            for start, stop in ((0, half), (half, rows)):
                along[start:stop, at:end] = jnp.dot(
                    bands_v[s, start:stop, :],
                    ext[start : start + depth, at:end],
                    preferred_element_type=jnp.float32,
                ).astype(jnp.bfloat16)
        for copy in copies[loads[n][0] : loads[n][1]]:
            copy.wait()
        waited = loads[n][1]
        for at in range(0, width, WIDE):
            span = min(WIDE, width - at)
            place_of = slice(first + at, first + at + span)
            row = lax.broadcasted_iota(jnp.int32, (span + 2 * EDGE, span), 0)
            col = lax.broadcasted_iota(jnp.int32, (span + 2 * EDGE, span), 1)
            distance = (row - col - EDGE).astype(jnp.float32) - params_v[8 * s : 8 * s + 1, place_of]
            band = jnp.zeros((span + 2 * EDGE, span), jnp.float32)
            for tap in range(TAPS):
                weight = params_v[8 * s + 1 + tap : 8 * s + 2 + tap, place_of]
                band = jnp.where(distance == float(tap), weight, band)
            blank = jnp.zeros((TILE - EDGE, span), jnp.bfloat16)
            resampled = jnp.dot(
                along[:, at : at + span + 2 * TILE],
                jnp.concatenate([blank, band.astype(jnp.bfloat16), blank], axis=0),
                preferred_element_type=jnp.float32,
            ).astype(jnp.bfloat16)
            for part in range(0, span, TILE):
                here = slice(at + part, at + part + TILE)
                there = slice(first + at + part, first + at + part + TILE)
                mismatch = resampled[:, part : part + TILE].astype(jnp.float32)
                mismatch = mismatch - center_v[:, here].astype(jnp.float32)
                level = texture_v[:, here]
                inverse = (-1.0 / (2 * BOX + 1)) / jnp.maximum(level, 0.4)
                estimate = box_sum(slope_v[:, here] * mismatch, lines) * inverse
                result[:, here] = estimate.astype(jnp.bfloat16)
                weighted = level * estimate
                for k in range(2):
                    pulls[k] = pulls[k] + weighted * params_v[16 + k : 17 + k, there]
        write = pltpu.make_async_copy(
            result, parallax.at[s, :, pl.ds(first, width)], sem.at[len(copies) + n]
        )
        write.start()
        writes.append(write)
    for copy in copies[waited:]:
        copy.wait()
    pulled[...] = earlier_v[...]
    for k in range(2):
        per_line = jnp.sum(pulls[k], axis=1, keepdims=True)
        pulled[k : k + 1, :] += jnp.sum(basis_v[...] * per_line, axis=0, keepdims=True)
    for write in writes:
        write.wait()


def local(
    nadir_view, forward, backward, along_weights, cross_weights, band_offsets, col_offsets,
    lag_lines, window_start,
):
    lines, cols = nadir_view.shape
    along_count = lax.axis_size("along")
    cross_count = lax.axis_size("cross")
    along_index = lax.axis_index("along")
    cross_index = lax.axis_index("cross")
    total_lines = lines * along_count
    total_cols = cols * cross_count
    half_ring = along_count // 2
    lag_floor = CAMERA_LAG // total_lines * total_lines + half_ring * lines
    rows = lines + 16
    whole = cols + 2 * TILE
    low_z, high_z = pairs_of(cross_count, -1), pairs_of(cross_count, 1)
    ring_down = [(i, (i - 1) % along_count) for i in range(along_count)]
    ring_up = [(i, (i + 1) % along_count) for i in range(along_count)]
    half_down, half_up = [], []
    for i in range(along_count):
        base = i // half_ring * half_ring
        half_down.append((i, base + (i - base - 1) % half_ring))
        half_up.append((i, base + (i - base + 1) % half_ring))
    across = [(i, (i + half_ring) % along_count) for i in range(along_count)]

    def over(value):
        return lax.ppermute(value, "along", across)

    def hbm(value):
        return pltpu.with_memory_space_constraint(value, pltpu.HBM)

    f32, bf16 = jnp.float32, jnp.bfloat16
    any_space = pl.BlockSpec(memory_space=pl.ANY)
    vmem = pl.BlockSpec(memory_space=pltpu.VMEM)
    smem = pl.BlockSpec(memory_space=pltpu.SMEM)
    limit = pltpu.CompilerParams(vmem_limit_bytes=24 * 1024 * 1024)

    def mover(kernel, name, shapes, operands, copies, scalars=0, scratch=()):
        return pl.pallas_call(
            kernel,
            out_shape=tuple(jax.ShapeDtypeStruct(shape, bf16) for shape in shapes),
            in_specs=[smem] * scalars + [any_space] * (len(operands) - scalars),
            out_specs=(vmem,) * len(shapes),
            scratch_shapes=[*scratch, pltpu.SemaphoreType.DMA((copies,))],
            compiler_params=limit,
            cost_estimate=pl.CostEstimate(
                flops=0, bytes_accessed=4 * sum(math.prod(s) for s in shapes), transcendentals=0
            ),
            name=name,
        )(*operands)

    place = jnp.stack([along_index, cross_index]).astype(jnp.int32)
    gap = jnp.zeros((3, cols), f32)
    shift = col_offsets.astype(f32)
    taps = cross_weights.astype(f32)
    columns = cross_index * cols + jnp.arange(cols, dtype=jnp.int32)
    position = ((columns.astype(f32) + 0.5) / total_cols + 0.25)[None]
    params = jnp.concatenate(
        [shift[0:1], taps[0], gap, shift[1:2], taps[1], gap, position, position * position, gap, gap]
    )
    basis = harmonics(window_start[0] + along_index * lines + jnp.arange(lines, dtype=jnp.int32))

    (crossing,) = mover(
        functools.partial(cross_kernel, lines),
        "cross",
        ((lines + 2 * LINE_RIM, cols),),
        (hbm(forward), hbm(backward)),
        3,
    )
    crossed = over(crossing)

    near = lines + 2 * EDGE * lines // TILE
    near_first, near_last = mover(
        functools.partial(pack_kernel, lines, cols),
        "pack",
        ((near, TILE), (near, TILE)),
        (hbm(nadir_view), hbm(forward), hbm(backward), crossing),
        6,
        scratch=[pltpu.VMEM((2, 2, lines, TILE), bf16)],
    )
    from_right = lax.ppermute(near_first, "cross", low_z)
    from_left = lax.ppermute(near_last, "cross", high_z)
    first_lines, last_lines = mover(
        functools.partial(nadir_lines_kernel, lines, cols),
        "nadir_lines",
        ((NADIR_RIM + EDGE, whole), (NADIR_RIM + EDGE, whole)),
        (hbm(nadir_view), from_left, from_right, params, basis),
        6 + 8 * lines // TILE,
    )
    nadir_below = lax.ppermute(first_lines, "along", ring_down)
    nadir_above = lax.ppermute(last_lines, "along", ring_up)

    (middle,) = pl.pallas_call(
        functools.partial(middle_kernel, lines, cols),
        out_shape=(jax.ShapeDtypeStruct((lines - 2 * LINE_RIM + EDGE, cols), bf16),),
        in_specs=[any_space, any_space, vmem, vmem],
        out_specs=(vmem,),
        scratch_shapes=[pltpu.SemaphoreType.DMA((2,))],
        compiler_params=limit,
        cost_estimate=pl.CostEstimate(
            flops=0, bytes_accessed=4 * lines * cols, transcendentals=0
        ),
        name="middle",
    )(hbm(backward), first_lines, nadir_above, nadir_below)
    middle = over(middle)

    down, up = mover(
        functools.partial(lines_kernel, lines, half_ring),
        "lines",
        ((3 * LINE_RIM // 2, cols), (3 * LINE_RIM // 2, cols)),
        (place, hbm(forward), hbm(backward), crossed),
        2,
        1,
    )
    slab_below = lax.ppermute(down, "along", half_down)
    slab_above = lax.ppermute(up, "along", half_up)

    depth = lines // 2 + 2 * LINE_RIM
    slopes, center, texture, sums, bands = pl.pallas_call(
        functools.partial(prep_kernel, lines, cols, total_lines, total_cols, lag_floor),
        out_shape=(
            pltpu.HBM((rows, cols), f32),
            pltpu.HBM((rows, cols), bf16),
            pltpu.HBM((lines, cols), f32),
            jax.ShapeDtypeStruct((8, lines), f32),
            pltpu.HBM((2, rows, depth), bf16),
        ),
        in_specs=[smem] + [vmem] * 8 + [any_space],
        out_specs=(any_space, any_space, any_space, vmem, any_space),
        scratch_shapes=[
            pltpu.VMEM((lines + 2 * NADIR_RIM, whole), bf16),
            pltpu.VMEM((rows, cols), f32),
            pltpu.VMEM((rows, cols), bf16),
            pltpu.VMEM((lines, cols), f32),
            pltpu.VMEM((2, rows, depth), bf16),
            pltpu.SemaphoreType.DMA((3 * (cols // WIDE) + 1,)),
        ],
        compiler_params=limit,
        cost_estimate=pl.CostEstimate(
            flops=2 * rows * cols * 512, bytes_accessed=12 * rows * cols, transcendentals=0
        ),
        name="prep",
    )(
        place, hbm(nadir_view), from_left, from_right, nadir_above,
        nadir_below, lag_lines[None], hbm(band_offsets), hbm(along_weights), down,
    )

    def run(jobs, earlier, middle, parallax):
        fresh = parallax is None
        operands = [
            slopes, center, texture, bands, params, basis, earlier, slab_above, slab_below, crossed,
        ]
        aliases = {}
        if not fresh:
            operands += [middle, parallax]
            aliases = {len(operands) - 1: 0}
        scratch = []
        for _, _, width in jobs:
            scratch += [
                pltpu.VMEM((lines + 2 * LINE_RIM, width + 2 * TILE), bf16),
                pltpu.VMEM((rows, width + 2 * TILE), bf16),
                pltpu.VMEM((rows, width), f32),
                pltpu.VMEM((rows, width), bf16),
                pltpu.VMEM((lines, width), f32),
                pltpu.VMEM((2, EDGE, lines + TILE), bf16),
                pltpu.VMEM((lines, width), bf16),
            ]
        done = sum(width for _, _, width in jobs)
        return pl.pallas_call(
            functools.partial(slab_kernel, lines, cols, jobs, fresh),
            out_shape=(
                pltpu.HBM((2, lines, cols), bf16),
                jax.ShapeDtypeStruct((8, TILE), f32),
            ),
            in_specs=[any_space] * len(operands),
            out_specs=(any_space, vmem),
            scratch_shapes=[
                pltpu.VMEM((2, rows, depth), bf16),
                pltpu.VMEM((24, cols), f32),
                pltpu.VMEM((lines, TILE), f32),
                pltpu.VMEM((8, TILE), f32),
                pltpu.SemaphoreType.DMA((4 + 14 * len(jobs),)),
                *scratch,
            ],
            input_output_aliases=aliases,
            compiler_params=limit,
            cost_estimate=pl.CostEstimate(
                flops=2 * rows * (done + 256) * 900, bytes_accessed=20 * rows * done, transcendentals=0
            ),
            name="inner" if fresh else "rest",
        )(*(hbm(v) if n < 4 else v for n, v in enumerate(operands)))

    nothing = jnp.zeros((8, TILE), f32)
    parallax, pulled = run([(0, TILE, cols - 2 * TILE)], nothing, None, None)
    jobs = [(0, 0, TILE), (0, cols - TILE, TILE), (1, 0, cols)]
    parallax, pulled = run(jobs, pulled, middle, parallax)

    share = jnp.concatenate([sums, pulled], axis=1)
    total = share
    for shift_by in range(1, cross_count):
        total = total + lax.ppermute(
            share, "cross", [(i, (i + shift_by) % cross_count) for i in range(cross_count)]
        )
    scale_pull = 1.0 / (lines * total_cols) ** 0.5
    line_sums = total[:, :lines]
    row_count = 4 * MODES // cross_count
    row_first = cross_index * row_count
    assert 2 * MODES % row_count == 0
    upper = row_first >= 2 * MODES
    doubled = jnp.concatenate([basis, basis], axis=1)
    basis_rows = lax.dynamic_slice_in_dim(doubled, row_first, row_count, 1)
    left_coef = jnp.where(upper, line_sums[1], line_sums[0])
    right_coef = jnp.where(upper, line_sums[2], line_sums[1])
    weighted = jnp.concatenate([basis * left_coef[:, None], basis * right_coef[:, None]], axis=1)
    normal_gram = jnp.dot(basis_rows.T, weighted, precision=lax.Precision.HIGHEST)[None]
    flat = total[:2, lines:].reshape(1, 4 * MODES) * scale_pull
    normal_rhs = lax.dynamic_slice_in_dim(flat, row_first, row_count, 1)
    return parallax, normal_gram, normal_rhs


def solution(mesh):
    placed = (
        P("along", "cross"),
        P("along", "cross"),
        P("along", "cross"),
        P(),
        P(None, None, "cross"),
        P(),
        P(None, "cross"),
        P(),
        P(),
    )
    return jax.shard_map(
        local,
        mesh=mesh,
        in_specs=placed,
        out_specs=(P(None, "along", "cross"), P("along", "cross", None), P("along", "cross")),
        check_vma=False,
    )
```

time: 73.9 us -> 59.7 us (0.81)
  starting transfers between devices: 28.6 us -> 15.3 us
  waiting for transfers between devices: 6.73 us -> 17 us
  local copies, waits for them, and re-layouts: 8.8 us -> 0.76 us
  Pallas kernels: 24.6 us -> 22.5 us
  other arithmetic: 2.53 us -> 0.96 us
  matrix products: 0.46 us -> 1.22 us
    ppermute x2 -> x0, starting transfers between devices: 7.41 us -> none  [the longest x1 6.13 us: local(): slab_left = lax.ppermute(last, ('along', 'cross'), aslant(high_z))]
    unnamed x37 -> x7, local copies, waits for them, and re-layouts: 5.59 us -> 0.02 us
    ppermute x1, waiting for transfers between devices: 4.94 us -> 0.7 us  [local(): slab_above = lax.ppermute(up, 'along', half_up)]
    ppermute x4 -> x2, waiting for transfers between devices: 0.01 us -> 3.45 us  [over(): return lax.ppermute(value, 'along', across)]
    ppermute x1, waiting for transfers between devices: 0.01 us -> 3.38 us  [local(): from_right = lax.ppermute(near_first, 'cross', low_z)]
    ppermute x3, waiting for transfers between devices: 1.4 us -> 4.48 us  [local(): lax.ppermute(share, 'cross', [(i, (i + shift_by) % cross_count) for i in...]
    ppermute x1, starting transfers between devices: 2.63 us -> 0.06 us  [local(): nadir_below = lax.ppermute(first_lines, 'along', ring_down)]
    ppermute x1, waiting for transfers between devices: 0.37 us -> 2.87 us  [local(): nadir_above = lax.ppermute(last_lines, 'along', ring_up)]
  transfers between devices with their start and end apart: 15 -> 11, of which waited for: 4 -> 7; matrix products, arithmetic and copies ran while one was open for 6% -> 2% of each run, Pallas kernels for 29% -> 25%
where the time goes in v3:
time: 59.7 us; the launch traced here: 59.3 us
  Pallas kernels  22.5 us (38%)
  waiting for transfers between devices  17 us (28%)
  starting transfers between devices  15.3 us (26%)
  between operations  1.58 us (3%)
  matrix products  1.22 us (2%)
  other arithmetic  0.96 us (2%)
  local copies, waits for them, and re-layouts  0.76 us (1%)
    pallas_call x2, Pallas kernels, run(): pl.pallas_call(functools.partial(slab_kernel, lines, cols, jobs, fresh),...  11.5 us
    pallas_call x4, Pallas kernels, mover(): pl.pallas_call(kernel, out_shape=tuple((jax.ShapeDtypeStruct(shape, bf16)...  5.06 us
    pallas_call x1, Pallas kernels, local(): pl.pallas_call(functools.partial(prep_kernel, lines, cols, total_lines, t...  4.81 us
    ppermute x3, starting transfers between devices, local(): lax.ppermute(share, 'cross', [(i, (i + shift_by) % cross_count) for i in...  4.8 us
    ppermute x2, starting transfers between devices, over(): return lax.ppermute(value, 'along', across)  4.59 us
    ppermute x3, waiting for transfers between devices, local(): lax.ppermute(share, 'cross', [(i, (i + shift_by) % cross_count) for i in...  4.48 us
    ppermute x1, starting transfers between devices, local(): from_left = lax.ppermute(near_last, 'cross', high_z)  3.48 us
    ppermute x2, waiting for transfers between devices, over(): return lax.ppermute(value, 'along', across)  3.45 us
  transfers between devices with their start and end apart: 11, of which 7 were waited for; matrix products, arithmetic and copies ran while one was open for 2% of the time, Pallas kernels for 25%

profile of v3, /device:TPU:0, one launch (start us, length us, event | category | flops | bytes accessed | tf_op | source)
XLA Modules:
  0.0 59.3 jit_solution(12715953604435919015)
XLA Ops:
  0.6 1.2 %cross.1.crossing = bf16[320,1536]{1,0:T(8,128)(2,1)S(1)} custom-call(bf16[256,1536]{1,0:T(8,128)(2,1)} %forward.5, bf16[256,1536]{1,0:T(8,128)(2,1)} %backward.7), custom_call_target="tpu_custom_call" | custom-call | bytes 1966080 | tf_op jit(solution)/shard_map/cross/pallas_call | solution.py:418
  1.8 0.0 copy-start.1
  1.8 0.0 copy-start.2
  1.8 3.0 %collective-permute-start.4 = (bf16[320,1536]{1,0:T(8,128)(2,1)S(1)}, bf16[320,1536]{1,0:T(8,128)(2,1)S(1)}, u32[]{:S(2)}, u32[]{:S(2)}) collective-permute-start(bf16[320,1536]{1,0:T(8,128)(2,1)S(1)} %cross.1.crossing), channel_id=1, source_target_pairs={{0,16},{4,20},{8,24},{12,28},{16,0},{20,4},{24,8},{28,12},{1,17},{... | collective-permute-start | bytes 2949128 | tf_op jit(solution)/shard_map/ppermute | solution.py:406
  4.9 1.2 %pack.1 = (bf16[320,128]{1,0:T(8,128)(2,1)S(1)}, bf16[320,128]{1,0:T(8,128)(2,1)S(1)}) custom-call(bf16[256,1536]{1,0:T(8,128)(2,1)} %nadir.5, bf16[256,1536]{1,0:T(8,128)(2,1)} %forward.5, bf16[256,1536]{1,0:T(8,128)(2,1)} %backward.7, bf16[320,1536]{1,0:T(8,128)(2,1)S(1)} %cross.1.crossing), custom_call_target="tpu_custom_call" | custom-call | bytes 327680 | tf_op jit(solution)/shard_map/pack/pallas_call | solution.py:418
  6.1 3.5 %collective-permute-start = (bf16[320,128]{1,0:T(8,128)(2,1)S(1)}, bf16[320,128]{1,0:T(8,128)(2,1)S(1)}, u32[]{:S(2)}, u32[]{:S(2)}) collective-permute-start(bf16[320,128]{1,0:T(8,128)(2,1)S(1)} %get-tuple-element.18), channel_id=1, source_target_pairs={{0,1},{1,2},{2,3},{4,5},{5,6},{6,7},{8,9},{9,10},{10,11},{12,13},{... | collective-permute-start | bytes 245768 | tf_op jit(solution)/shard_map/ppermute | solution.py:461
  9.6 1.3 %collective-permute-start.1 = (bf16[320,128]{1,0:T(8,128)(2,1)S(1)}, bf16[320,128]{1,0:T(8,128)(2,1)S(1)}, u32[]{:S(2)}, u32[]{:S(2)}) collective-permute-start(bf16[320,128]{1,0:T(8,128)(2,1)S(1)} %get-tuple-element.19), channel_id=1, source_target_pairs={{1,0},{2,1},{3,2},{5,4},{6,5},{7,6},{9,8},{10,9},{11,10},{13,12},{... | collective-permute-start | bytes 245768 | tf_op jit(solution)/shard_map/ppermute | solution.py:460
  10.9 0.0 copy-done.1
  10.9 0.0 copy-done.2
  11.7 0.1 concatenate.20.params
  11.8 0.6 fusion.11
  12.4 0.1 pad_maximum_fusion.basis
  12.5 0.0 collective-permute-done.from_left.left
  12.5 3.4 %collective-permute-done.1.from_right.right = bf16[320,128]{1,0:T(8,128)(2,1)S(1)} collective-permute-done((bf16[320,128]{1,0:T(8,128)(2,1)S(1)}, bf16[320,128]{1,0:T(8,128)(2,1)S(1)}, u32[]{:S(2)}, u32[]{:S(2)}) %collective-permute-start.1) | collective-permute-done | bytes 81952 | tf_op jit(solution)/shard_map/ppermute | solution.py:460
  15.9 1.0 %nadir_lines.1 = (bf16[32,1792]{1,0:T(8,128)(2,1)S(1)}, bf16[32,1792]{1,0:T(8,128)(2,1)S(1)}) custom-call(bf16[256,1536]{1,0:T(8,128)(2,1)} %nadir.5, bf16[320,128]{1,0:T(8,128)(2,1)S(1)} %collective-permute-done.from_left.left, bf16[320,128]{1,0:T(8,128)(2,1)S(1)} %collective-permute-done.1.from_right.right, f32[24,1536]{1,0:T(8,128)S(1)} %concatenate.20.params, ...), custom_call_target="tpu_custom_call" | custom-call | bytes 458752 | tf_op jit(solution)/shard_map/nadir_lines/pallas_call | solution.py:418
  17.0 0.1 collective-permute-start.3
  17.0 0.5 collective-permute-start.2
  17.5 2.1 %collective-permute-done.3.below = bf16[32,1792]{1,0:T(8,128)(2,1)S(1)} collective-permute-done((bf16[32,1792]{1,0:T(8,128)(2,1)S(1)}, bf16[32,1792]{1,0:T(8,128)(2,1)S(1)}, u32[]{:S(2)}, u32[]{:S(2)}) %collective-permute-start.3) | collective-permute-done | bytes 114720 | tf_op jit(solution)/shard_map/ppermute | solution.py:469
  19.6 2.9 %collective-permute-done.2.above = bf16[32,1792]{1,0:T(8,128)(2,1)S(1)} collective-permute-done((bf16[32,1792]{1,0:T(8,128)(2,1)S(1)}, bf16[32,1792]{1,0:T(8,128)(2,1)S(1)}, u32[]{:S(2)}, u32[]{:S(2)}) %collective-permute-start.2) | collective-permute-done | bytes 114720 | tf_op jit(solution)/shard_map/ppermute | solution.py:470
  22.5 1.1 %middle.1 = bf16[208,1536]{1,0:T(8,128)(2,1)S(1)} custom-call(bf16[256,1536]{1,0:T(8,128)(2,1)} %backward.7, bf16[32,1792]{1,0:T(8,128)(2,1)S(1)} %get-tuple-element.21.own, bf16[32,1792]{1,0:T(8,128)(2,1)S(1)} %collective-permute-done.2.above, bf16[32,1792]{1,0:T(8,128)(2,1)S(1)} %collective-permute-done.3.below), custom_call_target="tpu_custom_call" | custom-call | bytes 1572864 | tf_op jit(solution)/shard_map/middle/pallas_call | solution.py:472
  23.6 0.0 copy-start
  23.6 1.6 %collective-permute-start.7 = (bf16[208,1536]{1,0:T(8,128)(2,1)S(1)}, bf16[208,1536]{1,0:T(8,128)(2,1)S(1)}, u32[]{:S(2)}, u32[]{:S(2)}) collective-permute-start(bf16[208,1536]{1,0:T(8,128)(2,1)S(1)} %middle.1), channel_id=1, source_target_pairs={{0,16},{4,20},{8,24},{12,28},{16,0},{20,4},{24,8},{28,12},{1,17},{... | collective-permute-start | bytes 1916936 | tf_op jit(solution)/shard_map/ppermute | solution.py:406
  25.2 0.1 pad_add_fusion.place
  25.2 3.4 %collective-permute-done.4.crossed = bf16[320,1536]{1,0:T(8,128)(2,1)S(1)} collective-permute-done((bf16[320,1536]{1,0:T(8,128)(2,1)S(1)}, bf16[320,1536]{1,0:T(8,128)(2,1)S(1)}, u32[]{:S(2)}, u32[]{:S(2)}) %collective-permute-start.4) | collective-permute-done | bytes 983072 | tf_op jit(solution)/shard_map/ppermute | solution.py:406
  28.7 1.6 %lines.1 = (bf16[48,1536]{1,0:T(8,128)(2,1)S(1)}, bf16[48,1536]{1,0:T(8,128)(2,1)S(1)}) custom-call(s32[2]{0:T(128)S(1)} %pad_add_fusion.place, bf16[256,1536]{1,0:T(8,128)(2,1)} %forward.5, bf16[256,1536]{1,0:T(8,128)(2,1)} %backward.7, bf16[320,1536]{1,0:T(8,128)(2,1)S(1)} %collective-permute-done.4.crossed), custom_call_target="tpu_custom_call" | custom-call | bytes 589824 | tf_op jit(solution)/shard_map/lines/pallas_call | solution.py:418
  30.3 0.1 collective-permute-start.6
  30.4 0.5 collective-permute-start.5
  30.9 0.0 copy-done
  30.9 4.8 %prep.1 = (f32[272,1536]{1,0:T(8,128)}, bf16[272,1536]{1,0:T(8,128)(2,1)}, f32[256,1536]{1,0:T(8,128)}, f32[8,256]{1,0:T(8,128)S(1)}, bf16[2,272,192]{2,1,0:T(8,128)(2,1)}) custom-call(s32[2]{0:T(128)S(1)} %pad_add_fusion.place, bf16[256,1536]{1,0:T(8,128)(2,1)} %nadir.5, bf16[320,128]{1,0:T(8,128)(2,1)S(1)} %collective-permute-done.from_left.left, ...), custom_call_target="tpu_custom_call" | custom-call | flops 427819008 | bytes 5013504 | tf_op jit(solution)/shard_map/prep/pallas_call | solution.py:498
  35.7 0.0 collective-permute-done.6.below
  35.7 0.7 %collective-permute-done.5.above = bf16[48,1536]{1,0:T(8,128)(2,1)S(1)} collective-permute-done((bf16[48,1536]{1,0:T(8,128)(2,1)S(1)}, bf16[48,1536]{1,0:T(8,128)(2,1)S(1)}, u32[]{:S(2)}, u32[]{:S(2)}) %collective-permute-start.5) | collective-permute-done | bytes 147488 | tf_op jit(solution)/shard_map/ppermute | solution.py:495
  36.4 5.2 %inner.1 = (bf16[2,256,1536]{2,1,0:T(8,128)(2,1)}, f32[8,128]{1,0:T(8,128)S(1)}) custom-call(f32[272,1536]{1,0:T(8,128)} %get-tuple-element.23.slopes, bf16[272,1536]{1,0:T(8,128)(2,1)} %get-tuple-element.24.center, f32[256,1536]{1,0:T(8,128)} %get-tuple-element.25.texture, bf16[2,272,192]{2,1,0:T(8,128)(2,1)} %get-tuple-element.26.bands, ...), custom_call_target="tpu_custom_call" | custom-call | flops 752025600 | bytes 6963200 | tf_op jit(solution)/shard_map/inner/pallas_call | solution.py:548
  41.6 0.0 collective-permute-done.7.rest_0_
  41.6 6.4 %rest.1 = (bf16[2,256,1536]{2,1,0:T(8,128)(2,1)}, f32[8,128]{1,0:T(8,128)S(1)}) custom-call(f32[272,1536]{1,0:T(8,128)} %get-tuple-element.23.slopes, bf16[272,1536]{1,0:T(8,128)(2,1)} %get-tuple-element.24.center, f32[256,1536]{1,0:T(8,128)} %get-tuple-element.25.texture, ...), custom_call_target="tpu_custom_call", output_to_operand_aliasing={{0}: (11, {})} | custom-call | flops 1002700800 | bytes 9748480 | tf_op jit(solution)/shard_map/rest/pallas_call | solution.py:548
  48.0 3.8 %collective-permute-start.10 = (f32[8,384]{1,0:T(8,128)S(1)}, f32[8,384]{1,0:T(8,128)S(1)}, u32[]{:S(2)}, u32[]{:S(2)}) collective-permute-start(f32[8,384]{1,0:T(8,128)S(1)} %constant_dynamic-update-slice_fusion), channel_id=1, source_target_pairs={{0,3},{1,0},{2,1},{3,2},{4,7},{5,4},{6,5},{7,6},{8,11},{9,8},{10,9... | collective-permute-start | bytes 36872 | tf_op jit(solution)/shard_map/ppermute | solution.py:580
  51.8 0.0 collective-permute-start.8
  51.8 1.0 %collective-permute-start.9 = (f32[8,384]{1,0:T(8,128)S(1)}, f32[8,384]{1,0:T(8,128)S(1)}, u32[]{:S(2)}, u32[]{:S(2)}) collective-permute-start(f32[8,384]{1,0:T(8,128)S(1)} %constant_dynamic-update-slice_fusion), channel_id=1, source_target_pairs={{0,2},{1,3},{2,0},{3,1},{4,6},{5,7},{6,4},{7,5},{8,10},{9,11},{10,... | collective-permute-start | bytes 36872 | tf_op jit(solution)/shard_map/ppermute | solution.py:580
  52.8 0.4 collective-permute-done.10
  53.2 4.1 %collective-permute-done.8 = f32[8,384]{1,0:T(8,128)S(1)} collective-permute-done((f32[8,384]{1,0:T(8,128)S(1)}, f32[8,384]{1,0:T(8,128)S(1)}, u32[]{:S(2)}, u32[]{:S(2)}) %collective-permute-start.8) | collective-permute-done | bytes 12320 | tf_op jit(solution)/shard_map/ppermute | solution.py:580
  57.3 0.0 collective-permute-done.9
  57.3 0.1 broadcast_multiply_fusion.1
  57.5 0.6 constant_dynamic-slice_fusion
  58.1 1.2 %convolution_bitcast_fusion = f32[1,64,256]{2,1,0:T(8,128)} fusion(f32[256,128]{1,0:T(8,128)S(1)} %get-tuple-element.34, f32[256,128]{1,0:T(8,128)S(1)} %get-tuple-element.33, s32[]{:T(128)S(6)} %select_n.49, f32[256,64]{1,0:T(8,128)S(1)} %get-tuple-element.41, f32[256,64]{1,0:T(8,128)S(1)} %get-tuple-element.42), kind=kOutput, calls=%fused_computation | convolution fusion | flops 50446336 | bytes 458756 | tf_op jit(solution)/shard_map/dot_general | solution.py:594
  (15 shorter events, 0.1 us)
Async XLA Ops:
  1.8 9.1 %copy-start.1 = (bf16[2,4,1536]{2,1,0:T(4,128)(2,1)S(1)}, bf16[2,4,1536]{2,1,0:T(4,128)(2,1)}, u32[]{:S(2)}) copy-start(bf16[2,4,1536]{2,1,0:T(4,128)(2,1)} %param.13) | copy-start | bytes 73732
  1.8 9.1 %copy-start.2 = (s32[2,1536]{1,0:T(2,128)S(1)}, s32[2,1536]{1,0:T(2,128)}, u32[]{:S(2)}) copy-start(s32[2,1536]{1,0:T(2,128)} %param.15) | copy-start | bytes 36868
  1.8 26.8 %collective-permute-start.4 = (bf16[320,1536]{1,0:T(8,128)(2,1)S(1)}, bf16[320,1536]{1,0:T(8,128)(2,1)S(1)}, u32[]{:S(2)}, u32[]{:S(2)}) collective-permute-start(bf16[320,1536]{1,0:T(8,128)(2,1)S(1)} %cross.1.crossing), channel_id=1, source_target_pairs={{0,16},{4,20},{8,24},{12,28},{16,0},{20,4},{24,8},{28,12},{1,17},{... | collective-permute-start | bytes 2949128 | tf_op jit(solution)/shard_map/ppermute | solution.py:406
  6.1 6.4 %collective-permute-start = (bf16[320,128]{1,0:T(8,128)(2,1)S(1)}, bf16[320,128]{1,0:T(8,128)(2,1)S(1)}, u32[]{:S(2)}, u32[]{:S(2)}) collective-permute-start(bf16[320,128]{1,0:T(8,128)(2,1)S(1)} %get-tuple-element.18), channel_id=1, source_target_pairs={{0,1},{1,2},{2,3},{4,5},{5,6},{6,7},{8,9},{9,10},{10,11},{12,13},{... | collective-permute-start | bytes 245768 | tf_op jit(solution)/shard_map/ppermute | solution.py:461
  9.6 6.3 %collective-permute-start.1 = (bf16[320,128]{1,0:T(8,128)(2,1)S(1)}, bf16[320,128]{1,0:T(8,128)(2,1)S(1)}, u32[]{:S(2)}, u32[]{:S(2)}) collective-permute-start(bf16[320,128]{1,0:T(8,128)(2,1)S(1)} %get-tuple-element.19), channel_id=1, source_target_pairs={{1,0},{2,1},{3,2},{5,4},{6,5},{7,6},{9,8},{10,9},{11,10},{13,12},{... | collective-permute-start | bytes 245768 | tf_op jit(solution)/shard_map/ppermute | solution.py:460
  17.0 2.7 %collective-permute-start.3 = (bf16[32,1792]{1,0:T(8,128)(2,1)S(1)}, bf16[32,1792]{1,0:T(8,128)(2,1)S(1)}, u32[]{:S(2)}, u32[]{:S(2)}) collective-permute-start(bf16[32,1792]{1,0:T(8,128)(2,1)S(1)} %get-tuple-element.21.own), channel_id=1, source_target_pairs={{0,28},{4,0},{8,4},{12,8},{16,12},{20,16},{24,20},{28,24},{1,29},{... | collective-permute-start | bytes 344072 | tf_op jit(solution)/shard_map/ppermute | solution.py:469
  17.0 5.5 %collective-permute-start.2 = (bf16[32,1792]{1,0:T(8,128)(2,1)S(1)}, bf16[32,1792]{1,0:T(8,128)(2,1)S(1)}, u32[]{:S(2)}, u32[]{:S(2)}) collective-permute-start(bf16[32,1792]{1,0:T(8,128)(2,1)S(1)} %get-tuple-element.20), channel_id=1, source_target_pairs={{0,4},{4,8},{8,12},{12,16},{16,20},{20,24},{24,28},{28,0},{1,5},{5... | collective-permute-start | bytes 344072 | tf_op jit(solution)/shard_map/ppermute | solution.py:470
  23.6 7.3 %copy-start = (s32[2048]{0:T(1024)S(1)}, s32[2048]{0:T(1024)}, u32[]{:S(2)}) copy-start(s32[2048]{0:T(1024)} %param.16) | copy-start | bytes 24580
  23.6 18.0 %collective-permute-start.7 = (bf16[208,1536]{1,0:T(8,128)(2,1)S(1)}, bf16[208,1536]{1,0:T(8,128)(2,1)S(1)}, u32[]{:S(2)}, u32[]{:S(2)}) collective-permute-start(bf16[208,1536]{1,0:T(8,128)(2,1)S(1)} %middle.1), channel_id=1, source_target_pairs={{0,16},{4,20},{8,24},{12,28},{16,0},{20,4},{24,8},{28,12},{1,17},{... | collective-permute-start | bytes 1916936 | tf_op jit(solution)/shard_map/ppermute | solution.py:406
  30.3 5.4 %collective-permute-start.6 = (bf16[48,1536]{1,0:T(8,128)(2,1)S(1)}, bf16[48,1536]{1,0:T(8,128)(2,1)S(1)}, u32[]{:S(2)}, u32[]{:S(2)}) collective-permute-start(bf16[48,1536]{1,0:T(8,128)(2,1)S(1)} %get-tuple-element.22.down), channel_id=1, source_target_pairs={{0,12},{4,0},{8,4},{12,8},{16,28},{20,16},{24,20},{28,24},{1,13},{... | collective-permute-start | bytes 442376 | tf_op jit(solution)/shard_map/ppermute | solution.py:494
  30.4 6.0 %collective-permute-start.5 = (bf16[48,1536]{1,0:T(8,128)(2,1)S(1)}, bf16[48,1536]{1,0:T(8,128)(2,1)S(1)}, u32[]{:S(2)}, u32[]{:S(2)}) collective-permute-start(bf16[48,1536]{1,0:T(8,128)(2,1)S(1)} %get-tuple-element.27), channel_id=1, source_target_pairs={{0,4},{4,8},{8,12},{12,0},{16,20},{20,24},{24,28},{28,16},{1,5},{5... | collective-permute-start | bytes 442376 | tf_op jit(solution)/shard_map/ppermute | solution.py:495
  48.0 5.2 %collective-permute-start.10 = (f32[8,384]{1,0:T(8,128)S(1)}, f32[8,384]{1,0:T(8,128)S(1)}, u32[]{:S(2)}, u32[]{:S(2)}) collective-permute-start(f32[8,384]{1,0:T(8,128)S(1)} %constant_dynamic-update-slice_fusion), channel_id=1, source_target_pairs={{0,3},{1,0},{2,1},{3,2},{4,7},{5,4},{6,5},{7,6},{8,11},{9,8},{10,9... | collective-permute-start | bytes 36872 | tf_op jit(solution)/shard_map/ppermute | solution.py:580
  51.8 5.5 %collective-permute-start.8 = (f32[8,384]{1,0:T(8,128)S(1)}, f32[8,384]{1,0:T(8,128)S(1)}, u32[]{:S(2)}, u32[]{:S(2)}) collective-permute-start(f32[8,384]{1,0:T(8,128)S(1)} %constant_dynamic-update-slice_fusion), channel_id=1, source_target_pairs={{0,1},{1,2},{2,3},{3,0},{4,5},{5,6},{6,7},{7,4},{8,9},{9,10},{10,1... | collective-permute-start | bytes 36872 | tf_op jit(solution)/shard_map/ppermute | solution.py:580
  51.8 5.5 %collective-permute-start.9 = (f32[8,384]{1,0:T(8,128)S(1)}, f32[8,384]{1,0:T(8,128)S(1)}, u32[]{:S(2)}, u32[]{:S(2)}) collective-permute-start(f32[8,384]{1,0:T(8,128)S(1)} %constant_dynamic-update-slice_fusion), channel_id=1, source_target_pairs={{0,2},{1,3},{2,0},{3,1},{4,6},{5,7},{6,4},{7,5},{8,10},{9,11},{10,... | collective-permute-start | bytes 36872 | tf_op jit(solution)/shard_map/ppermute | solution.py:580

commit v4 on v3

v4 whole, which is shorter than its diff:
```python
import functools
import math

import jax
import jax.numpy as jnp
from jax import lax
from jax.experimental import pallas as pl
from jax.experimental.pallas import tpu as pltpu
from jax.sharding import PartitionSpec as P

TAPS = 4
CAMERA_LAG = 20480
BOX = 4
MODES = 64
LINE_RIM = 32
NADIR_RIM = 16
TILE = 128
WIDE = 256
EDGE = 16


def pairs_of(count, step):
    return [(i, i + step) for i in range(count) if 0 <= i + step < count]


def box_sum(x, lines):
    rows = x.shape[0]
    two = x + pltpu.roll(x, rows - 1, 0)
    four = two + pltpu.roll(two, rows - 2, 0)
    eight = four + pltpu.roll(four, rows - 4, 0)
    return eight[:lines] + x[2 * BOX : lines + 2 * BOX]


def lane_fold(x):
    folded = x[:, :TILE]
    for at in range(TILE, x.shape[1], TILE):
        folded = folded + x[:, at : at + TILE]
    return folded


def copy_all(moves, sem):
    copies = [pltpu.make_async_copy(a, b, sem.at[n]) for n, (a, b) in enumerate(moves)]
    for copy in copies:
        copy.start()
    for copy in copies:
        copy.wait()


def cut_kernel(
    lines, cols, cut, nadir, forward, backward, ends, first_part, near_first, near_last, side, sem
):
    body = pl.ds(LINE_RIM, lines - 2 * LINE_RIM)
    moves = [(backward.at[body, pl.ds(0, cut)], first_part)]
    for n, (begin, near) in enumerate(((0, near_first), (cols - TILE, near_last))):
        moves.append((nadir.at[:, pl.ds(begin, TILE)], near.at[pl.ds(0, lines), :]))
        for s, slab in enumerate((forward, backward)):
            moves.append((slab.at[:, pl.ds(begin, TILE)], side.at[s, n]))
    copy_all(moves, sem)
    for n, (row, near) in enumerate(((0, near_first), (TILE - EDGE, near_last))):
        for s in range(2):
            turned = side[s, n].astype(jnp.float32).T[row : row + EDGE].astype(jnp.bfloat16)
            for k in range(lines // TILE):
                at = lines + (s * (lines // TILE) + k) * EDGE
                near[at : at + EDGE, :] = turned[:, k * TILE : (k + 1) * TILE]


def ends_kernel(lines, backward, ends, sem):
    moves = []
    for n, row in enumerate((0, lines - LINE_RIM)):
        target = pl.ds(n * LINE_RIM, LINE_RIM)
        moves.append((backward.at[pl.ds(row, LINE_RIM), :], ends.at[target, :]))
    copy_all(moves, sem)


def nadir_lines_kernel(lines, cols, nadir, from_left, from_right, bands, first, last, sem):
    moves = []
    whole = cols + 2 * TILE
    for out, row, tile in ((first, 0, 0), (last, lines - NADIR_RIM, lines // TILE - 1)):
        span = pl.ds(row, NADIR_RIM)
        moves.append((from_left.at[span, :], out.at[:, pl.ds(0, TILE)]))
        moves.append((nadir.at[span, :], out.at[:, pl.ds(TILE, cols)]))
        moves.append((from_right.at[span, :], out.at[:, pl.ds(TILE + cols, TILE)]))
        for n, near in enumerate((from_left, from_right)):
            for s in range(2):
                at = lines + (s * (lines // TILE) + tile) * EDGE
                target = pl.ds(whole + (2 * n + s) * TILE, TILE)
                moves.append((near.at[pl.ds(at, EDGE), :], out.at[:, target]))
    copy_all(moves, sem)


def late_kernel(
    lines, cols, cuts, backward, from_left, from_right, above, below, second, third, sem
):
    height = lines - 2 * LINE_RIM
    whole = cols + 2 * TILE
    body = pl.ds(LINE_RIM, height)
    width = cuts[1] - cuts[0]
    moves = [
        (backward.at[body, pl.ds(cuts[0], width)], second.at[pl.ds(0, height), :]),
        (backward.at[body, pl.ds(cuts[1], cols - cuts[1])], third),
    ]
    lane = lax.broadcasted_iota(jnp.int32, (EDGE, TILE), 1)
    for k in range(4):
        row = height + k * EDGE
        near = (from_left, from_right)[k // 2]
        for tile in range(lines // TILE):
            at = lines + (k % 2 * (lines // TILE) + tile) * EDGE
            window = second.at[pl.ds(row, EDGE), pl.ds(tile * TILE, TILE)]
            moves.append((near.at[pl.ds(at, EDGE), :], window))
        here = slice(whole + k * TILE, whole + (k + 1) * TILE)
        ahead = above[:, here].astype(jnp.float32)
        behind = below[:, here].astype(jnp.float32)
        both = jnp.where(lane < TILE // 2, behind, ahead).astype(jnp.bfloat16)
        second[row : row + EDGE, lines : lines + TILE] = both
    if width > lines + TILE:
        second[height:, lines + TILE :] = jnp.zeros((4 * EDGE, width - lines - TILE), jnp.bfloat16)
    copy_all(moves, sem)


def lines_kernel(lines, half_ring, place, forward, backward, lead, ends, down, up, sem):
    in_half = lax.rem(place[0], half_ring)
    most, least = LINE_RIM, LINE_RIM // 2
    for out, counts, raw_place in ((down, (least, most), 0), (up, (most, least), half_ring - 1)):
        starts = (0, 0) if out is down else (lines - counts[0], lines - counts[1])
        ended = 0 if out is down else 2 * LINE_RIM - counts[1]
        tops = pl.ds(0, counts[0]), pl.ds(counts[0], counts[1])

        @pl.when(in_half == raw_place)
        def _(out=out, counts=counts, starts=starts, tops=tops):
            copy_all(
                [
                    (slab.at[pl.ds(start, count), :], out.at[top, :])
                    for slab, start, count, top in zip((forward, backward), starts, counts, tops)
                ],
                sem,
            )

        @pl.when(in_half != raw_place)
        def _(out=out, counts=counts, starts=starts, ended=ended, tops=tops):
            copy_all(
                [
                    (lead.at[pl.ds(starts[0], counts[0]), :], out.at[tops[0], :]),
                    (ends.at[pl.ds(ended, counts[1]), :], out.at[tops[1], :]),
                ],
                sem,
            )


def positions(place, cols, total_cols, at, span):
    column = lax.broadcasted_iota(jnp.int32, (1, span), 1) + (place[1] * cols + at)
    position = (column.astype(jnp.float32) + 0.5) / total_cols + 0.25
    return position, position * position


def prep_kernel(
    lines, cols, total_cols, place, nadir, left, right, above, below, down,
    slopes, center, inverse, lever, sums, framed,
):
    tall = lines + 2 * NADIR_RIM
    rows = lines + 16
    framed[0:NADIR_RIM, :] = above[:, 0 : cols + 2 * TILE]
    framed[NADIR_RIM + lines : tall, :] = below[:, 0 : cols + 2 * TILE]
    framed[NADIR_RIM : NADIR_RIM + lines, 0:TILE] = left[0:lines, :]
    framed[NADIR_RIM : NADIR_RIM + lines, TILE : TILE + cols] = nadir[...]
    framed[NADIR_RIM : NADIR_RIM + lines, TILE + cols :] = right[0:lines, :]
    row = lax.broadcasted_iota(jnp.int32, (2 * WIDE, WIDE), 0)
    col = lax.broadcasted_iota(jnp.int32, (2 * WIDE, WIDE), 1)
    gap = jnp.abs(row - TILE - col)
    smear = jnp.where(gap == 0, 2.0, jnp.where(gap == 1, 1.0, 0.0)).astype(jnp.bfloat16)
    totals = [jnp.zeros((lines, TILE), jnp.float32) for _ in range(3)]
    for at in range(0, cols, WIDE):
        across = jnp.dot(
            framed[:, at : at + 2 * WIDE], smear, preferred_element_type=jnp.float32
        )
        change = pltpu.roll(across, tall - 5, 0) - pltpu.roll(across, tall - 3, 0)
        slope = change[8 : 8 + rows] * 0.25
        slopes[:, at : at + WIDE] = slope
        middle = framed[:, TILE + at : TILE + at + WIDE].astype(jnp.float32)
        middle = pltpu.roll(middle, tall - 4, 0)[8 : 8 + rows]
        center[:, at : at + WIDE] = middle.astype(jnp.bfloat16)
        level = box_sum(slope * slope, lines) * (1.0 / (2 * BOX + 1))
        inverted = (-1.0 / (2 * BOX + 1)) / jnp.maximum(level, 0.4)
        inverse[:, at : at + WIDE] = inverted
        lever[:, at : at + WIDE] = level * inverted
        position, square = positions(place, cols, total_cols, at, WIDE)
        for k, power in enumerate((square, square * position, square * square)):
            totals[k] = totals[k] + lane_fold(level * power)
    lane = lax.broadcasted_iota(jnp.int32, (lines, TILE), 1)
    packed = jnp.zeros((lines, TILE), jnp.float32)
    for k in range(3):
        packed = jnp.where(lane == k, jnp.sum(totals[k], axis=1, keepdims=True), packed)
    sums[...] = packed.T[0:8, :] * (1.0 / (lines * total_cols))


def cosines(phases, sines):
    period = 4 * MODES
    turned = jnp.where(sines, phases + (period - MODES), phases) % period
    return jnp.cos(turned.astype(jnp.float32) * (2.0 * jnp.pi / period))


def bands_kernel(
    lines, cols, total_lines, total_cols, lag_floor, place, lag, offsets, weights, shifts, taps,
    line_bands, col_bands, levers, basis, rows_basis, upper, chosen,
):
    rows = lines + 16
    period = 4 * MODES
    for s in range(2):
        for n in range(cols // WIDE):
            here = slice(n * WIDE, (n + 1) * WIDE)
            row = lax.broadcasted_iota(jnp.int32, (WIDE + 2 * EDGE, WIDE), 0)
            col = lax.broadcasted_iota(jnp.int32, (WIDE + 2 * EDGE, WIDE), 1)
            distance = row - col - EDGE - shifts[s : s + 1, here]
            weight = taps[s, :, here].astype(jnp.float32)
            band = jnp.zeros((WIDE + 2 * EDGE, WIDE), jnp.float32)
            for tap in range(TAPS):
                band = jnp.where(distance == tap, weight[tap : tap + 1], band)
            col_bands[s, :, here] = band.astype(jnp.bfloat16)
    position, square = positions(place, cols, total_cols, 0, cols)
    levers[0:1, :] = position
    levers[1:2, :] = square
    levers[2:, :] = jnp.zeros((6, cols), jnp.float32)
    start = place[2] + place[0] * lines
    line = start + lax.broadcasted_iota(jnp.int32, (lines, 2 * MODES), 0)
    mode = lax.broadcasted_iota(jnp.int32, (lines, 2 * MODES), 1)
    basis[...] = cosines(line % period * (2 * (mode % MODES) + 1), mode >= MODES)
    count = rows_basis.shape[0]
    row_first = place[1] * count
    row_at = lax.rem(row_first, 2 * MODES)
    mode = row_at + lax.broadcasted_iota(jnp.int32, (count, lines), 0)
    line = start + lax.broadcasted_iota(jnp.int32, (count, lines), 1)
    rows_basis[...] = cosines(line % period * (2 * (mode % MODES) + 1), mode >= MODES)
    upper[...] = jnp.zeros_like(upper) + jnp.where(row_first >= 2 * MODES, 1.0, 0.0)
    own = row_at + lax.broadcasted_iota(jnp.int32, (2 * MODES, count), 1)
    mode = lax.broadcasted_iota(jnp.int32, (2 * MODES, count), 0)
    chosen[...] = jnp.where(own == mode, 1.0, 0.0)
    begin = place[0] * lines
    ahead = pl.multiple_of(lax.rem(begin + total_lines - TILE, total_lines), TILE)
    behind = pl.multiple_of(lax.rem(begin + lines, total_lines), TILE)
    begin = pl.multiple_of(begin, TILE)

    def window(ref, lead):
        parts = [
            ref[lead + (slice(None), pl.ds(start, size))].astype(jnp.float32)
            for start, size in ((ahead, TILE), (begin, lines), (behind, TILE))
        ]
        return jnp.concatenate(parts, axis=1)

    wide = lines + 2 * TILE
    lags = window(lag, ()) - float(lag_floor)
    shifts = window(offsets, ())
    stacked = jnp.concatenate(
        [
            jnp.broadcast_to(shifts[0:1] - lags, (8, wide)),
            jnp.broadcast_to(shifts[1:2] + lags, (8, wide)),
            window(weights, (0,)),
            window(weights, (1,)),
            jnp.zeros((TILE - 24, wide), jnp.float32),
        ],
        axis=0,
    )
    as_columns = pltpu.roll(stacked.T, wide - (TILE - BOX), 0)[0:rows]
    half = lines // 2
    depth = half + 2 * LINE_RIM
    for s in range(2):
        for first, last in ((0, half), (half, rows)):
            at = lax.broadcasted_iota(jnp.int32, (last - first, depth), 1)
            own = lax.broadcasted_iota(jnp.int32, (last - first, depth), 0)
            distance = (at - own - (LINE_RIM - BOX)).astype(jnp.float32)
            distance = distance - as_columns[first:last, 8 * s : 8 * s + 1]
            band = jnp.zeros((last - first, depth), jnp.float32)
            for tap in range(TAPS):
                weight = as_columns[first:last, 16 + 4 * s + tap : 17 + 4 * s + tap]
                band = jnp.where(distance == float(tap), weight, band)
            line_bands[s, first:last, :] = band.astype(jnp.bfloat16)


def slab_kernel(
    lines, cols, cuts, jobs, count, fresh, last,
    slopes, center, inverse, lever, line_bands, col_bands, levers, basis, above, below, ends, *rest,
):
    lead, first_part, second_part, third_part = (*rest[:count], None, None, None)[:4]
    rest = rest[count:]
    if not fresh:
        earlier, rest = rest[0], rest[2:]
    parallax, pulled, sem, *scratch = rest
    rows = lines + 16
    half = lines // 2
    depth = half + 2 * LINE_RIM
    height = lines - 2 * LINE_RIM
    most, least = LINE_RIM, LINE_RIM // 2
    writes = []
    if fresh:
        pulls = [jnp.zeros((lines, TILE), jnp.float32) for _ in range(2)]
    else:
        pulls = [earlier[k] for k in range(2)]
    for n, (s, first, width) in enumerate(jobs):
        ext, along, result = scratch[3 * n : 3 * n + 3]
        low, high = first - TILE, first + width + TILE
        over, under = ((most, least), (least, most))[s]
        pieces = [
            (above, (0, most)[s], LINE_RIM - over, over, 0, cols),
            (below, (0, least)[s], LINE_RIM + lines, under, 0, cols),
        ]
        if s == 0:
            pieces.append((lead, 0, LINE_RIM, lines, 0, cols))
        else:
            pieces.append((ends, 0, LINE_RIM, LINE_RIM, 0, cols))
            pieces.append((ends, LINE_RIM, lines, LINE_RIM, 0, cols))
            pieces.append((first_part, 0, 2 * LINE_RIM, height, 0, cuts[0]))
            pieces.append((second_part, 0, 2 * LINE_RIM, height, cuts[0], cuts[1]))
            pieces.append((third_part, 0, 2 * LINE_RIM, height, cuts[1], cols))
        for ref, row, target, tall, begin, end in pieces:
            a, b = max(low, begin), min(high, end)
            if a < b:
                ext[target : target + tall, a - low : b - low] = ref[
                    row : row + tall, a - begin : b - begin
                ]
        blank = jnp.zeros((least, width + 2 * TILE), jnp.bfloat16)
        if s == 0:
            ext[2 * LINE_RIM + lines - least :, :] = blank
        else:
            ext[:least, :] = blank
        for side in range(2):
            if (low < 0, high > cols)[side]:
                at = 0 if side == 0 else width + TILE
                row = height + (2 * side + s) * EDGE
                piece = second_part[row : row + EDGE, : lines + TILE].astype(jnp.float32)
                gap = jnp.zeros((TILE - EDGE, lines + TILE), jnp.float32)
                piece = jnp.concatenate([gap, piece] if side == 0 else [piece, gap], axis=0)
                turned = piece.T.astype(jnp.bfloat16)
                ext[LINE_RIM : LINE_RIM + lines, at : at + TILE] = turned[:lines]
                ext[LINE_RIM - over : LINE_RIM, at : at + TILE] = turned[lines + TILE - over :]
                ext[LINE_RIM + lines : LINE_RIM + lines + under, at : at + TILE] = turned[
                    lines : lines + under
                ]
        for at in range(0, width + 2 * TILE, WIDE):
            end = min(at + WIDE, width + 2 * TILE)
            for start, stop in ((0, half), (half, rows)):
                along[start:stop, at:end] = jnp.dot(
                    line_bands[s, start:stop, :],
                    ext[start : start + depth, at:end],
                    preferred_element_type=jnp.float32,
                ).astype(jnp.bfloat16)
        bounds = sorted({first, first + width, *range(-(-first // WIDE) * WIDE, first + width, WIDE)})
        for at, end in zip(bounds[:-1], bounds[1:]):
            at, span = at - first, end - at
            blank = jnp.zeros((TILE - EDGE, span), jnp.bfloat16)
            offset = first + at
            inner = offset % WIDE
            band = col_bands[s, inner : inner + span + 2 * EDGE, offset : offset + span]
            resampled = jnp.dot(
                along[:, at : at + span + 2 * TILE],
                jnp.concatenate([blank, band, blank], axis=0),
                preferred_element_type=jnp.float32,
            ).astype(jnp.bfloat16)
            for part in range(0, span, TILE):
                here = slice(at + part, at + part + TILE)
                there = slice(first + at + part, first + at + part + TILE)
                mismatch = resampled[:, part : part + TILE].astype(jnp.float32)
                mismatch = mismatch - center[:, there].astype(jnp.float32)
                boxed = box_sum(slopes[:, there] * mismatch, lines)
                result[:, here] = (boxed * inverse[:, there]).astype(jnp.bfloat16)
                weighted = boxed * lever[:, there]
                for k in range(2):
                    pulls[k] = pulls[k] + weighted * levers[k : k + 1, there]
        write = pltpu.make_async_copy(
            result, parallax.at[s, :, pl.ds(first, width)], sem.at[n]
        )
        write.start()
        writes.append(write)
    if last:
        pulled[...] = jnp.zeros_like(pulled)
        for k in range(2):
            per_line = jnp.sum(pulls[k], axis=1, keepdims=True)
            pulled[k : k + 1, :] = jnp.sum(basis[...] * per_line, axis=0, keepdims=True)
    else:
        for k in range(2):
            pulled[k] = pulls[k]
    for write in writes:
        write.wait()


def final_kernel(lines, scale_pull, basis, rows_basis, upper, chosen, *rest):
    shares, (gram, rhs) = rest[:-2], rest[-2:]
    total = shares[0][...]
    for share in shares[1:]:
        total = total + share[...]
    is_upper = upper[0:1, :] > 0.5
    sums = total[:, :lines]
    precision = lax.Precision.HIGHEST
    for n in range(2):
        coef = jnp.where(is_upper, sums[n + 1 : n + 2], sums[n : n + 1])
        gram[0, :, n * TILE : (n + 1) * TILE] = jnp.dot(
            rows_basis[...] * coef, basis[...], precision=precision, preferred_element_type=jnp.float32
        )
    pull = jnp.where(is_upper[:, :TILE], total[1:2, lines:], total[0:1, lines:]) * scale_pull
    rhs[...] = jnp.dot(
        jnp.broadcast_to(pull, (8, TILE)), chosen[...], precision=precision, preferred_element_type=jnp.float32
    )[0:1]


def local(
    nadir_view, forward, backward, along_weights, cross_weights, band_offsets, col_offsets,
    lag_lines, window_start,
):
    lines, cols = nadir_view.shape
    along_count = lax.axis_size("along")
    cross_count = lax.axis_size("cross")
    along_index = lax.axis_index("along")
    cross_index = lax.axis_index("cross")
    total_lines = lines * along_count
    total_cols = cols * cross_count
    half_ring = along_count // 2
    lag_floor = CAMERA_LAG // total_lines * total_lines + half_ring * lines
    rows = lines + 16
    whole = cols + 2 * TILE
    low_z, high_z = pairs_of(cross_count, -1), pairs_of(cross_count, 1)
    ring_down = [(i, (i - 1) % along_count) for i in range(along_count)]
    ring_up = [(i, (i + 1) % along_count) for i in range(along_count)]
    half_down, half_up = [], []
    for i in range(along_count):
        base = i // half_ring * half_ring
        half_down.append((i, base + (i - base - 1) % half_ring))
        half_up.append((i, base + (i - base + 1) % half_ring))
    across = [(i, (i + half_ring) % along_count) for i in range(along_count)]

    def over(value):
        return lax.ppermute(value, "along", across)

    def hbm(value):
        return pltpu.with_memory_space_constraint(value, pltpu.HBM)

    f32, bf16 = jnp.float32, jnp.bfloat16
    any_space = pl.BlockSpec(memory_space=pl.ANY)
    vmem = pl.BlockSpec(memory_space=pltpu.VMEM)
    smem = pl.BlockSpec(memory_space=pltpu.SMEM)
    limit = pltpu.CompilerParams(vmem_limit_bytes=24 * 1024 * 1024)

    def mover(kernel, name, shapes, operands, copies, scalars=0, scratch=()):
        return pl.pallas_call(
            kernel,
            out_shape=tuple(jax.ShapeDtypeStruct(shape, bf16) for shape in shapes),
            in_specs=[smem] * scalars + [any_space] * (len(operands) - scalars),
            out_specs=(vmem,) * len(shapes),
            scratch_shapes=[*scratch, pltpu.SemaphoreType.DMA((copies,))],
            compiler_params=limit,
            cost_estimate=pl.CostEstimate(
                flops=0, bytes_accessed=4 * sum(math.prod(s) for s in shapes), transcendentals=0
            ),
            name=name,
        )(*operands)

    place = jnp.stack([along_index, cross_index, window_start[0]]).astype(jnp.int32)

    lead = over(forward)
    (own_ends,) = mover(
        functools.partial(ends_kernel, lines),
        "ends",
        ((2 * LINE_RIM, cols),),
        (hbm(backward),),
        2,
    )
    ends = over(own_ends)
    cuts = (cols // 2, cols - lines - TILE)
    height = lines - 2 * LINE_RIM
    near = lines + 2 * EDGE * lines // TILE
    first_part, near_first, near_last = mover(
        functools.partial(cut_kernel, lines, cols, cuts[0]),
        "cut",
        ((height, cuts[0]), (near, TILE), (near, TILE)),
        (hbm(nadir_view), hbm(forward), hbm(backward), own_ends),
        7,
        scratch=[pltpu.VMEM((2, 2, lines, TILE), bf16)],
    )
    first_part = over(first_part)

    from_right = lax.ppermute(near_first, "cross", low_z)
    from_left = lax.ppermute(near_last, "cross", high_z)
    depth = lines // 2 + 2 * LINE_RIM
    row_count = 4 * MODES // cross_count
    assert 2 * MODES % row_count == 0
    bands = pl.pallas_call(
        functools.partial(bands_kernel, lines, cols, total_lines, total_cols, lag_floor),
        out_shape=(
            jax.ShapeDtypeStruct((2, rows, depth), bf16),
            jax.ShapeDtypeStruct((2, WIDE + 2 * EDGE, cols), bf16),
            jax.ShapeDtypeStruct((8, cols), f32),
            jax.ShapeDtypeStruct((lines, 2 * MODES), f32),
            jax.ShapeDtypeStruct((row_count, lines), f32),
            jax.ShapeDtypeStruct((8, lines), f32),
            jax.ShapeDtypeStruct((2 * MODES, row_count), f32),
        ),
        in_specs=[smem] + [vmem] * 5,
        out_specs=(vmem,) * 7,
        compiler_params=limit,
        cost_estimate=pl.CostEstimate(
            flops=20 * 300 * cols, bytes_accessed=4 * 300 * cols, transcendentals=0
        ),
        name="bands",
    )(
        place, lag_lines[None], hbm(band_offsets), hbm(along_weights), hbm(col_offsets),
        hbm(cross_weights),
    )
    line_bands, col_bands, levers, basis, rows_basis, upper, chosen = bands
    first_lines, last_lines = mover(
        functools.partial(nadir_lines_kernel, lines, cols),
        "nadir_lines",
        ((NADIR_RIM, whole + 4 * TILE), (NADIR_RIM, whole + 4 * TILE)),
        (hbm(nadir_view), from_left, from_right, line_bands),
        14,
    )
    nadir_below = lax.ppermute(first_lines, "along", ring_down)
    nadir_above = lax.ppermute(last_lines, "along", ring_up)

    down, up = mover(
        functools.partial(lines_kernel, lines, half_ring),
        "lines",
        ((3 * LINE_RIM // 2, cols), (3 * LINE_RIM // 2, cols)),
        (place, hbm(forward), hbm(backward), lead, ends),
        2,
        1,
    )
    slab_below = lax.ppermute(down, "along", half_down)
    slab_above = lax.ppermute(up, "along", half_up)

    second_part, third_part = pl.pallas_call(
        functools.partial(late_kernel, lines, cols, cuts),
        out_shape=(
            jax.ShapeDtypeStruct((height + 4 * EDGE, cuts[1] - cuts[0]), bf16),
            jax.ShapeDtypeStruct((height, cols - cuts[1]), bf16),
        ),
        in_specs=[any_space, any_space, any_space, vmem, vmem],
        out_specs=(vmem, vmem),
        scratch_shapes=[pltpu.SemaphoreType.DMA((2 + 4 * lines // TILE,))],
        compiler_params=limit,
        cost_estimate=pl.CostEstimate(flops=0, bytes_accessed=lines * cols, transcendentals=0),
        name="late_cut",
    )(hbm(backward), from_left, from_right, nadir_above, nadir_below)
    second_part, third_part = over(second_part), over(third_part)

    slopes, center, inverse, lever, sums = pl.pallas_call(
        functools.partial(prep_kernel, lines, cols, total_cols),
        out_shape=(
            jax.ShapeDtypeStruct((rows, cols), f32),
            jax.ShapeDtypeStruct((rows, cols), bf16),
            jax.ShapeDtypeStruct((lines, cols), f32),
            jax.ShapeDtypeStruct((lines, cols), f32),
            jax.ShapeDtypeStruct((8, lines), f32),
        ),
        in_specs=[smem] + [vmem] * 5 + [any_space],
        out_specs=(vmem,) * 5,
        scratch_shapes=[pltpu.VMEM((lines + 2 * NADIR_RIM, whole), bf16)],
        compiler_params=limit,
        cost_estimate=pl.CostEstimate(
            flops=2 * rows * cols * 512, bytes_accessed=12 * rows * cols, transcendentals=0
        ),
        name="prep",
    )(place, hbm(nadir_view), from_left, from_right, nadir_above, nadir_below, down)

    def run(name, jobs, crossed, so_far, last):
        fresh = so_far is None
        operands = [
            slopes, center, inverse, lever, line_bands, col_bands, levers, basis, slab_above, slab_below,
            ends, *crossed,
        ]
        specs = [vmem] * len(operands)
        aliases = {}
        if not fresh:
            aliases = {len(operands) + 1: 0}
            operands += [so_far[1], so_far[0]]
            specs += [vmem, any_space]
        scratch = []
        for _, _, width in jobs:
            scratch += [
                pltpu.VMEM((lines + 2 * LINE_RIM, width + 2 * TILE), bf16),
                pltpu.VMEM((rows, width + 2 * TILE), bf16),
                pltpu.VMEM((lines, width), bf16),
            ]
        done = sum(width for _, _, width in jobs)
        return pl.pallas_call(
            functools.partial(slab_kernel, lines, cols, cuts, jobs, len(crossed), fresh, last),
            out_shape=(
                pltpu.HBM((2, lines, cols), bf16),
                jax.ShapeDtypeStruct((8, TILE) if last else (2, lines, TILE), f32),
            ),
            in_specs=specs,
            out_specs=(any_space, vmem),
            scratch_shapes=[pltpu.SemaphoreType.DMA((len(jobs),)), *scratch],
            input_output_aliases=aliases,
            compiler_params=limit,
            cost_estimate=pl.CostEstimate(
                flops=2 * rows * (done + 256) * 900, bytes_accessed=20 * rows * done, transcendentals=0
            ),
            name=name,
        )(*operands)

    so_far = run("inner", [(0, TILE, cols - 2 * TILE)], [lead], None, False)
    jobs = [(1, 0, cuts[1] - TILE), (0, 0, TILE), (0, cols - TILE, TILE)]
    so_far = run("second", jobs, [lead, first_part, second_part], so_far, False)
    jobs = [(1, cuts[1] - TILE, cols - cuts[1] + TILE)]
    crossed = [lead, first_part, second_part, third_part]
    parallax, pulled = run("third", jobs, crossed, so_far, True)

    share = jnp.concatenate([sums, pulled], axis=1)
    shares = [share]
    for shift_by in range(1, cross_count):
        pairs = [(i, (i + shift_by) % cross_count) for i in range(cross_count)]
        shares.append(lax.ppermute(share, "cross", pairs))
    scale_pull = 1.0 / (lines * total_cols) ** 0.5
    normal_gram, normal_rhs = pl.pallas_call(
        functools.partial(final_kernel, lines, scale_pull),
        out_shape=(
            jax.ShapeDtypeStruct((1, row_count, 4 * MODES), f32),
            jax.ShapeDtypeStruct((1, row_count), f32),
        ),
        in_specs=[vmem] * (4 + len(shares)),
        out_specs=(vmem, vmem),
        compiler_params=limit,
        name="final",
    )(basis, rows_basis, upper, chosen, *shares)
    return parallax, normal_gram, normal_rhs


def solution(mesh):
    placed = (
        P("along", "cross"),
        P("along", "cross"),
        P("along", "cross"),
        P(),
        P(None, None, "cross"),
        P(),
        P(None, "cross"),
        P(),
        P(),
    )
    return jax.shard_map(
        local,
        mesh=mesh,
        in_specs=placed,
        out_specs=(P(None, "along", "cross"), P("along", "cross", None), P("along", "cross")),
        check_vma=False,
    )
```

time: 59.7 us -> 51.9 us (0.87)
  waiting for transfers between devices: 17 us -> 6.97 us
  starting transfers between devices: 15.3 us -> 22.6 us
  Pallas kernels: 22.5 us -> 20.3 us
  matrix products: 1.22 us -> 0 us
  other arithmetic: 0.96 us -> 0.08 us
  local copies, waits for them, and re-layouts: 0.76 us -> 0.01 us
    ppermute x1, starting transfers between devices: 0.06 us -> 2.63 us  [local(): nadir_below = lax.ppermute(first_lines, 'along', ring_down)]
    ppermute x1, waiting for transfers between devices: 3.38 us -> 0.99 us  [local(): from_right = lax.ppermute(near_first, 'cross', low_z)]
    ppermute x1, waiting for transfers between devices: 2.87 us -> 0.62 us  [local(): nadir_above = lax.ppermute(last_lines, 'along', ring_up)]
    ppermute x2 -> x5, starting transfers between devices: 4.59 us -> 6.75 us  [over(): return lax.ppermute(value, 'along', across)]
    ppermute x3, waiting for transfers between devices: 4.48 us -> 2.35 us  [local(): shares.append(lax.ppermute(share, 'cross', pairs))]
    ppermute x1, waiting for transfers between devices: 2.11 us -> 0.01 us  [local(): nadir_below = lax.ppermute(first_lines, 'along', ring_down)]
    pallas_call x4 -> x7, Pallas kernels: 17.4 us -> 15.5 us  [the longest x3 6.59 us: run(): pl.pallas_call(functools.partial(slab_kernel, lines, cols, cuts, jobs, le...]
    ppermute x1, starting transfers between devices: 0.06 us -> 1.73 us  [local(): slab_below = lax.ppermute(down, 'along', half_down)]
  transfers between devices with their start and end apart: 11 -> 14, of which waited for: 7 -> 6; matrix products, arithmetic and copies ran while one was open for 2% -> 0% of each run, Pallas kernels for 25% -> 35%
where the time goes in v4:
time: 51.9 us; the launch traced here: 51.4 us
  starting transfers between devices  22.6 us (44%)
  Pallas kernels  20.3 us (39%)
  waiting for transfers between devices  6.97 us (13%)
  between operations  1.44 us (3%)
    ppermute x5, starting transfers between devices, over(): return lax.ppermute(value, 'along', across)  6.75 us
    pallas_call x3, Pallas kernels, run(): pl.pallas_call(functools.partial(slab_kernel, lines, cols, cuts, jobs, le...  6.59 us
    ppermute x3, starting transfers between devices, local(): shares.append(lax.ppermute(share, 'cross', pairs))  6.11 us
    pallas_call x4, Pallas kernels, mover(): pl.pallas_call(kernel, out_shape=tuple((jax.ShapeDtypeStruct(shape, bf16)...  4.84 us
    ppermute x1, starting transfers between devices, local(): from_left = lax.ppermute(near_last, 'cross', high_z)  3.97 us
    pallas_call x1, Pallas kernels, local(): pl.pallas_call(functools.partial(prep_kernel, lines, cols, total_cols), o...  3.58 us
    pallas_call x1, Pallas kernels, local(): pl.pallas_call(functools.partial(bands_kernel, lines, cols, total_lines,...  3.3 us
    ppermute x5, waiting for transfers between devices, over(): return lax.ppermute(value, 'along', across)  3 us
  transfers between devices with their start and end apart: 14, of which 6 were waited for; matrix products, arithmetic and copies ran while one was open for 0% of the time, Pallas kernels for 35%

profile of v4, /device:TPU:0, one launch (start us, length us, event | category | flops | bytes accessed | tf_op | source)
XLA Modules:
  0.0 51.4 jit_solution(11584108898880709230)
XLA Ops:
  0.6 0.0 copy-start
  0.6 3.0 %collective-permute-start.4 = (bf16[256,1536]{1,0:T(8,128)(2,1)}, bf16[256,1536]{1,0:T(8,128)(2,1)S(1)}, u32[]{:S(2)}, u32[]{:S(2)}) collective-permute-start(bf16[256,1536]{1,0:T(8,128)(2,1)} %forward.3), channel_id=1, source_target_pairs={{0,16},{4,20},{8,24},{12,28},{16,0},{20,4},{24,8},{28,12},{1,17},{... | collective-permute-start | bytes 2359304 | tf_op jit(solution)/shard_map/ppermute | solution.py:428
  3.7 1.0 %ends.1 = bf16[64,1536]{1,0:T(8,128)(2,1)S(1)} custom-call(bf16[256,1536]{1,0:T(8,128)(2,1)} %backward.7), custom_call_target="tpu_custom_call" | custom-call | bytes 393216 | tf_op jit(solution)/shard_map/ends/pallas_call | solution.py:440
  4.6 0.1 collective-permute-start.5
  4.7 1.3 %cut.1 = (bf16[192,768]{1,0:T(8,128)(2,1)S(1)}, bf16[320,128]{1,0:T(8,128)(2,1)S(1)}, bf16[320,128]{1,0:T(8,128)(2,1)S(1)}) custom-call(bf16[256,1536]{1,0:T(8,128)(2,1)} %nadir.5, bf16[256,1536]{1,0:T(8,128)(2,1)} %forward.3, bf16[256,1536]{1,0:T(8,128)(2,1)} %backward.7, bf16[64,1536]{1,0:T(8,128)(2,1)S(1)} %ends.1), custom_call_target="tpu_custom_call" | custom-call | bytes 917504 | tf_op jit(solution)/shard_map/cut/pallas_call | solution.py:440
  6.0 4.0 %collective-permute-start = (bf16[320,128]{1,0:T(8,128)(2,1)S(1)}, bf16[320,128]{1,0:T(8,128)(2,1)S(1)}, u32[]{:S(2)}, u32[]{:S(2)}) collective-permute-start(bf16[320,128]{1,0:T(8,128)(2,1)S(1)} %get-tuple-element.32), channel_id=1, source_target_pairs={{0,1},{1,2},{2,3},{4,5},{5,6},{6,7},{8,9},{9,10},{10,11},{12,13},{... | collective-permute-start | bytes 245768 | tf_op jit(solution)/shard_map/ppermute | solution.py:478
  10.0 1.3 %collective-permute-start.1 = (bf16[320,128]{1,0:T(8,128)(2,1)S(1)}, bf16[320,128]{1,0:T(8,128)(2,1)S(1)}, u32[]{:S(2)}, u32[]{:S(2)}) collective-permute-start(bf16[320,128]{1,0:T(8,128)(2,1)S(1)} %get-tuple-element.33), channel_id=1, source_target_pairs={{1,0},{2,1},{3,2},{5,4},{6,5},{7,6},{9,8},{10,9},{11,10},{13,12},{... | collective-permute-start | bytes 245768 | tf_op jit(solution)/shard_map/ppermute | solution.py:477
  11.9 0.1 pad_add_fusion.place
  12.0 0.0 copy-done
  12.0 3.3 %bands.1 = (bf16[2,272,192]{2,1,0:T(8,128)(2,1)S(1)}, bf16[2,288,1536]{2,1,0:T(8,128)(2,1)S(1)}, f32[8,1536]{1,0:T(8,128)S(1)}, f32[256,128]{1,0:T(8,128)S(1)}, ...) custom-call(s32[3]{0:T(128)S(1)} %pad_add_fusion.place, s32[1,2048]{1,0:T(1,128)S(1)} %bitcast.3, ...), custom_call_target="tpu_custom_call" | custom-call | flops 9216000 | bytes 1843200 | tf_op jit(solution)/shard_map/bands/pallas_call | solution.py:482
  15.3 0.0 collective-permute-done.from_left.left
  15.3 1.0 %collective-permute-done.1.from_right.right = bf16[320,128]{1,0:T(8,128)(2,1)S(1)} collective-permute-done((bf16[320,128]{1,0:T(8,128)(2,1)S(1)}, bf16[320,128]{1,0:T(8,128)(2,1)S(1)}, u32[]{:S(2)}, u32[]{:S(2)}) %collective-permute-start.1) | collective-permute-done | bytes 81952 | tf_op jit(solution)/shard_map/ppermute | solution.py:477
  16.3 1.0 %nadir_lines.1 = (bf16[16,2304]{1,0:T(8,128)(2,1)S(1)}, bf16[16,2304]{1,0:T(8,128)(2,1)S(1)}) custom-call(bf16[256,1536]{1,0:T(8,128)(2,1)} %nadir.5, bf16[320,128]{1,0:T(8,128)(2,1)S(1)} %collective-permute-done.from_left.left, bf16[320,128]{1,0:T(8,128)(2,1)S(1)} %collective-permute-done.1.from_right.right, ...), custom_call_target="tpu_custom_call" | custom-call | bytes 294912 | tf_op jit(solution)/shard_map/nadir_lines/pallas_call | solution.py:440
  17.3 0.1 collective-permute-start.2
  17.4 2.6 %collective-permute-start.3 = (bf16[16,2304]{1,0:T(8,128)(2,1)S(1)}, bf16[16,2304]{1,0:T(8,128)(2,1)S(1)}, u32[]{:S(2)}, u32[]{:S(2)}) collective-permute-start(bf16[16,2304]{1,0:T(8,128)(2,1)S(1)} %get-tuple-element.36), channel_id=1, source_target_pairs={{0,28},{4,0},{8,4},{12,8},{16,12},{20,16},{24,20},{28,24},{1,29},{... | collective-permute-start | bytes 221192 | tf_op jit(solution)/shard_map/ppermute | solution.py:512
  20.0 1.5 %collective-permute-start.8 = (bf16[192,768]{1,0:T(8,128)(2,1)S(1)}, bf16[192,768]{1,0:T(8,128)(2,1)S(1)}, u32[]{:S(2)}, u32[]{:S(2)}) collective-permute-start(bf16[192,768]{1,0:T(8,128)(2,1)S(1)} %get-tuple-element.46), channel_id=1, source_target_pairs={{0,16},{4,20},{8,24},{12,28},{16,0},{20,4},{24,8},{28,12},{1,17},{... | collective-permute-start | bytes 884744 | tf_op jit(solution)/shard_map/ppermute | solution.py:428
  21.5 0.6 %collective-permute-done.2.above = bf16[16,2304]{1,0:T(8,128)(2,1)S(1)} collective-permute-done((bf16[16,2304]{1,0:T(8,128)(2,1)S(1)}, bf16[16,2304]{1,0:T(8,128)(2,1)S(1)}, u32[]{:S(2)}, u32[]{:S(2)}) %collective-permute-start.2) | collective-permute-done | bytes 73760 | tf_op jit(solution)/shard_map/ppermute | solution.py:513
  22.1 0.0 collective-permute-done.3.below
  22.1 1.1 %late_cut.1 = (bf16[256,384]{1,0:T(8,128)(2,1)S(1)}, bf16[192,384]{1,0:T(8,128)(2,1)S(1)}) custom-call(bf16[256,1536]{1,0:T(8,128)(2,1)} %backward.7, bf16[320,128]{1,0:T(8,128)(2,1)S(1)} %collective-permute-done.from_left.left, bf16[320,128]{1,0:T(8,128)(2,1)S(1)} %collective-permute-done.1.from_right.right, ...), custom_call_target="tpu_custom_call" | custom-call | bytes 393216 | tf_op jit(solution)/shard_map/late_cut/pallas_call | solution.py:526
  23.2 1.6 %collective-permute-start.9 = (bf16[256,384]{1,0:T(8,128)(2,1)S(1)}, bf16[256,384]{1,0:T(8,128)(2,1)S(1)}, u32[]{:S(2)}, u32[]{:S(2)}) collective-permute-start(bf16[256,384]{1,0:T(8,128)(2,1)S(1)} %get-tuple-element.47), channel_id=1, source_target_pairs={{0,16},{4,20},{8,24},{12,28},{16,0},{20,4},{24,8},{28,12},{1,17},{... | collective-permute-start | bytes 589832 | tf_op jit(solution)/shard_map/ppermute | solution.py:428
  24.8 0.5 %collective-permute-start.10 = (bf16[192,384]{1,0:T(8,128)(2,1)S(1)}, bf16[192,384]{1,0:T(8,128)(2,1)S(1)}, u32[]{:S(2)}, u32[]{:S(2)}) collective-permute-start(bf16[192,384]{1,0:T(8,128)(2,1)S(1)} %get-tuple-element.48), channel_id=1, source_target_pairs={{0,16},{4,20},{8,24},{12,28},{16,0},{20,4},{24,8},{28,12},{1,17},{... | collective-permute-start | bytes 442376 | tf_op jit(solution)/shard_map/ppermute | solution.py:428
  25.3 1.9 %collective-permute-done.5.ends = bf16[64,1536]{1,0:T(8,128)(2,1)S(1)} collective-permute-done((bf16[64,1536]{1,0:T(8,128)(2,1)S(1)}, bf16[64,1536]{1,0:T(8,128)(2,1)S(1)}, u32[]{:S(2)}, u32[]{:S(2)}) %collective-permute-start.5) | collective-permute-done | bytes 196640 | tf_op jit(solution)/shard_map/ppermute | solution.py:428
  27.3 0.0 collective-permute-done.4.lead.rest_0_
  27.3 1.6 %lines.1 = (bf16[48,1536]{1,0:T(8,128)(2,1)S(1)}, bf16[48,1536]{1,0:T(8,128)(2,1)S(1)}) custom-call(s32[3]{0:T(128)S(1)} %pad_add_fusion.place, bf16[256,1536]{1,0:T(8,128)(2,1)} %forward.3, bf16[256,1536]{1,0:T(8,128)(2,1)} %backward.7, bf16[256,1536]{1,0:T(8,128)(2,1)S(1)} %collective-permute-done.4.lead.rest_0_, ...), custom_call_target="tpu_custom_call" | custom-call | bytes 589824 | tf_op jit(solution)/shard_map/lines/pallas_call | solution.py:440
  28.9 0.1 collective-permute-start.6
  29.0 1.7 %collective-permute-start.7 = (bf16[48,1536]{1,0:T(8,128)(2,1)S(1)}, bf16[48,1536]{1,0:T(8,128)(2,1)S(1)}, u32[]{:S(2)}, u32[]{:S(2)}) collective-permute-start(bf16[48,1536]{1,0:T(8,128)(2,1)S(1)} %get-tuple-element.37.down), channel_id=1, source_target_pairs={{0,12},{4,0},{8,4},{12,8},{16,28},{20,16},{24,20},{28,24},{1,13},{... | collective-permute-start | bytes 442376 | tf_op jit(solution)/shard_map/ppermute | solution.py:523
  30.7 3.6 %prep.1 = (f32[272,1536]{1,0:T(8,128)S(1)}, bf16[272,1536]{1,0:T(8,128)(2,1)S(1)}, f32[256,1536]{1,0:T(8,128)S(1)}, f32[256,1536]{1,0:T(8,128)S(1)}, f32[8,256]{1,0:T(8,128)S(1)}) custom-call(s32[3]{0:T(128)S(1)} %pad_add_fusion.place, bf16[256,1536]{1,0:T(8,128)(2,1)} %nadir.5, bf16[320,128]{1,0:T(8,128)(2,1)S(1)} %collective-permute-done.from_left.left, ...), custom_call_target="tpu_custom_call" | custom-call | flops 427819008 | bytes 5013504 | tf_op jit(solution)/shard_map/prep/pallas_call | solution.py:541
  34.3 0.0 collective-permute-done.6.above
  34.3 0.0 collective-permute-done.7.below
  34.3 2.4 %inner.1 = (bf16[2,256,1536]{2,1,0:T(8,128)(2,1)}, f32[2,256,128]{2,1,0:T(8,128)S(1)}) custom-call(f32[272,1536]{1,0:T(8,128)S(1)} %get-tuple-element.38.slopes, bf16[272,1536]{1,0:T(8,128)(2,1)S(1)} %get-tuple-element.39.center, f32[256,1536]{1,0:T(8,128)S(1)} %get-tuple-element.40.inverse, f32[256,1536]{1,0:T(8,128)S(1)} %get-tuple-element.41.lever, ...), custom_call_target="tpu_custom_call" | custom-call | flops 752025600 | bytes 6963200 | tf_op jit(solution)/shard_map/inner/pallas_call | solution.py:580
  36.7 0.0 collective-permute-done.8.rest_1_
  36.7 1.1 %collective-permute-done.9.rest_2_ = bf16[256,384]{1,0:T(8,128)(2,1)S(1)} collective-permute-done((bf16[256,384]{1,0:T(8,128)(2,1)S(1)}, bf16[256,384]{1,0:T(8,128)(2,1)S(1)}, u32[]{:S(2)}, u32[]{:S(2)}) %collective-permute-start.9) | collective-permute-done | bytes 196640 | tf_op jit(solution)/shard_map/ppermute | solution.py:428
  37.8 2.6 %second.1 = (bf16[2,256,1536]{2,1,0:T(8,128)(2,1)}, f32[2,256,128]{2,1,0:T(8,128)S(1)}) custom-call(f32[272,1536]{1,0:T(8,128)S(1)} %get-tuple-element.38.slopes, bf16[272,1536]{1,0:T(8,128)(2,1)S(1)} %get-tuple-element.39.center, f32[256,1536]{1,0:T(8,128)S(1)} %get-tuple-element.40.inverse, ...), custom_call_target="tpu_custom_call", output_to_operand_aliasing={{0}: (15, {})} | custom-call | flops 752025600 | bytes 6963200 | tf_op jit(solution)/shard_map/second/pallas_call | solution.py:580
  40.4 0.0 collective-permute-done.10.rest_3_
  40.4 1.6 %third.1 = (bf16[2,256,1536]{2,1,0:T(8,128)(2,1)}, f32[8,128]{1,0:T(8,128)S(1)}) custom-call(f32[272,1536]{1,0:T(8,128)S(1)} %get-tuple-element.38.slopes, bf16[272,1536]{1,0:T(8,128)(2,1)S(1)} %get-tuple-element.39.center, f32[256,1536]{1,0:T(8,128)S(1)} %get-tuple-element.40.inverse, ...), custom_call_target="tpu_custom_call", output_to_operand_aliasing={{0}: (16, {})} | custom-call | flops 376012800 | bytes 2785280 | tf_op jit(solution)/shard_map/third/pallas_call | solution.py:580
  42.0 2.2 %collective-permute-start.11 = (f32[8,384]{1,0:T(8,128)S(1)}, f32[8,384]{1,0:T(8,128)S(1)}, u32[]{:S(2)}, u32[]{:S(2)}) collective-permute-start(f32[8,384]{1,0:T(8,128)S(1)} %constant_dynamic-update-slice_fusion.rest_0_), channel_id=1, source_target_pairs={{0,1},{1,2},{2,3},{3,0},{4,5},{5,6},{6,7},{7,4},{8,9},{9,10},{10,1... | collective-permute-start | bytes 36872 | tf_op jit(solution)/shard_map/ppermute | solution.py:608
  44.2 2.6 %collective-permute-start.12 = (f32[8,384]{1,0:T(8,128)S(1)}, f32[8,384]{1,0:T(8,128)S(1)}, u32[]{:S(2)}, u32[]{:S(2)}) collective-permute-start(f32[8,384]{1,0:T(8,128)S(1)} %constant_dynamic-update-slice_fusion.rest_0_), channel_id=1, source_target_pairs={{0,2},{1,3},{2,0},{3,1},{4,6},{5,7},{6,4},{7,5},{8,10},{9,11},{10,... | collective-permute-start | bytes 36872 | tf_op jit(solution)/shard_map/ppermute | solution.py:608
  46.8 1.3 %collective-permute-start.13 = (f32[8,384]{1,0:T(8,128)S(1)}, f32[8,384]{1,0:T(8,128)S(1)}, u32[]{:S(2)}, u32[]{:S(2)}) collective-permute-start(f32[8,384]{1,0:T(8,128)S(1)} %constant_dynamic-update-slice_fusion.rest_0_), channel_id=1, source_target_pairs={{0,3},{1,0},{2,1},{3,2},{4,7},{5,4},{6,5},{7,6},{8,11},{9,8},{10,9... | collective-permute-start | bytes 36872 | tf_op jit(solution)/shard_map/ppermute | solution.py:608
  48.2 0.0 collective-permute-done.11.rest_1_
  48.2 0.7 %collective-permute-done.12.rest_2_ = f32[8,384]{1,0:T(8,128)S(1)} collective-permute-done((f32[8,384]{1,0:T(8,128)S(1)}, f32[8,384]{1,0:T(8,128)S(1)}, u32[]{:S(2)}, u32[]{:S(2)}) %collective-permute-start.12) | collective-permute-done | bytes 12320 | tf_op jit(solution)/shard_map/ppermute | solution.py:608
  48.8 1.7 %collective-permute-done.13.rest_3_ = f32[8,384]{1,0:T(8,128)S(1)} collective-permute-done((f32[8,384]{1,0:T(8,128)S(1)}, f32[8,384]{1,0:T(8,128)S(1)}, u32[]{:S(2)}, u32[]{:S(2)}) %collective-permute-start.13) | collective-permute-done | bytes 12320 | tf_op jit(solution)/shard_map/ppermute | solution.py:608
  50.5 0.9 %final.1 = (f32[1,64,256]{2,1,0:T(8,128)}, f32[1,64]{1,0:T(1,128)}) custom-call(f32[256,128]{1,0:T(8,128)S(1)} %get-tuple-element.44.basis, f32[64,256]{1,0:T(8,128)S(1)} %get-tuple-element.54.rows_basis, f32[8,256]{1,0:T(8,128)S(1)} %get-tuple-element.55.upper, f32[128,64]{1,0:T(8,128)S(1)} %get-tuple-element.56.chosen, ...), custom_call_target="tpu_custom_call" | custom-call | tf_op jit(solution)/shard_map/final/pallas_call | solution.py:610
  (2 shorter events, 0.0 us)
Async XLA Ops:
  0.6 11.4 %copy-start = (s32[2048]{0:T(1024)S(1)}, s32[2048]{0:T(1024)}, u32[]{:S(2)}) copy-start(s32[2048]{0:T(1024)} %param.16) | copy-start | bytes 24580
  0.6 26.6 %collective-permute-start.4 = (bf16[256,1536]{1,0:T(8,128)(2,1)}, bf16[256,1536]{1,0:T(8,128)(2,1)S(1)}, u32[]{:S(2)}, u32[]{:S(2)}) collective-permute-start(bf16[256,1536]{1,0:T(8,128)(2,1)} %forward.3), channel_id=1, source_target_pairs={{0,16},{4,20},{8,24},{12,28},{16,0},{20,4},{24,8},{28,12},{1,17},{... | collective-permute-start | bytes 2359304 | tf_op jit(solution)/shard_map/ppermute | solution.py:428
  4.6 22.6 %collective-permute-start.5 = (bf16[64,1536]{1,0:T(8,128)(2,1)S(1)}, bf16[64,1536]{1,0:T(8,128)(2,1)S(1)}, u32[]{:S(2)}, u32[]{:S(2)}) collective-permute-start(bf16[64,1536]{1,0:T(8,128)(2,1)S(1)} %ends.1), channel_id=1, source_target_pairs={{0,16},{4,20},{8,24},{12,28},{16,0},{20,4},{24,8},{28,12},{1,17},{... | collective-permute-start | bytes 589832 | tf_op jit(solution)/shard_map/ppermute | solution.py:428
  6.0 9.3 %collective-permute-start = (bf16[320,128]{1,0:T(8,128)(2,1)S(1)}, bf16[320,128]{1,0:T(8,128)(2,1)S(1)}, u32[]{:S(2)}, u32[]{:S(2)}) collective-permute-start(bf16[320,128]{1,0:T(8,128)(2,1)S(1)} %get-tuple-element.32), channel_id=1, source_target_pairs={{0,1},{1,2},{2,3},{4,5},{5,6},{6,7},{8,9},{9,10},{10,11},{12,13},{... | collective-permute-start | bytes 245768 | tf_op jit(solution)/shard_map/ppermute | solution.py:478
  10.0 6.3 %collective-permute-start.1 = (bf16[320,128]{1,0:T(8,128)(2,1)S(1)}, bf16[320,128]{1,0:T(8,128)(2,1)S(1)}, u32[]{:S(2)}, u32[]{:S(2)}) collective-permute-start(bf16[320,128]{1,0:T(8,128)(2,1)S(1)} %get-tuple-element.33), channel_id=1, source_target_pairs={{1,0},{2,1},{3,2},{5,4},{6,5},{7,6},{9,8},{10,9},{11,10},{13,12},{... | collective-permute-start | bytes 245768 | tf_op jit(solution)/shard_map/ppermute | solution.py:477
  17.3 4.8 %collective-permute-start.2 = (bf16[16,2304]{1,0:T(8,128)(2,1)S(1)}, bf16[16,2304]{1,0:T(8,128)(2,1)S(1)}, u32[]{:S(2)}, u32[]{:S(2)}) collective-permute-start(bf16[16,2304]{1,0:T(8,128)(2,1)S(1)} %get-tuple-element.35), channel_id=1, source_target_pairs={{0,4},{4,8},{8,12},{12,16},{16,20},{20,24},{24,28},{28,0},{1,5},{5... | collective-permute-start | bytes 221192 | tf_op jit(solution)/shard_map/ppermute | solution.py:513
  17.4 4.8 %collective-permute-start.3 = (bf16[16,2304]{1,0:T(8,128)(2,1)S(1)}, bf16[16,2304]{1,0:T(8,128)(2,1)S(1)}, u32[]{:S(2)}, u32[]{:S(2)}) collective-permute-start(bf16[16,2304]{1,0:T(8,128)(2,1)S(1)} %get-tuple-element.36), channel_id=1, source_target_pairs={{0,28},{4,0},{8,4},{12,8},{16,12},{20,16},{24,20},{28,24},{1,29},{... | collective-permute-start | bytes 221192 | tf_op jit(solution)/shard_map/ppermute | solution.py:512
  20.0 16.7 %collective-permute-start.8 = (bf16[192,768]{1,0:T(8,128)(2,1)S(1)}, bf16[192,768]{1,0:T(8,128)(2,1)S(1)}, u32[]{:S(2)}, u32[]{:S(2)}) collective-permute-start(bf16[192,768]{1,0:T(8,128)(2,1)S(1)} %get-tuple-element.46), channel_id=1, source_target_pairs={{0,16},{4,20},{8,24},{12,28},{16,0},{20,4},{24,8},{28,12},{1,17},{... | collective-permute-start | bytes 884744 | tf_op jit(solution)/shard_map/ppermute | solution.py:428
  23.2 14.6 %collective-permute-start.9 = (bf16[256,384]{1,0:T(8,128)(2,1)S(1)}, bf16[256,384]{1,0:T(8,128)(2,1)S(1)}, u32[]{:S(2)}, u32[]{:S(2)}) collective-permute-start(bf16[256,384]{1,0:T(8,128)(2,1)S(1)} %get-tuple-element.47), channel_id=1, source_target_pairs={{0,16},{4,20},{8,24},{12,28},{16,0},{20,4},{24,8},{28,12},{1,17},{... | collective-permute-start | bytes 589832 | tf_op jit(solution)/shard_map/ppermute | solution.py:428
  24.8 15.6 %collective-permute-start.10 = (bf16[192,384]{1,0:T(8,128)(2,1)S(1)}, bf16[192,384]{1,0:T(8,128)(2,1)S(1)}, u32[]{:S(2)}, u32[]{:S(2)}) collective-permute-start(bf16[192,384]{1,0:T(8,128)(2,1)S(1)} %get-tuple-element.48), channel_id=1, source_target_pairs={{0,16},{4,20},{8,24},{12,28},{16,0},{20,4},{24,8},{28,12},{1,17},{... | collective-permute-start | bytes 442376 | tf_op jit(solution)/shard_map/ppermute | solution.py:428
  28.9 5.4 %collective-permute-start.6 = (bf16[48,1536]{1,0:T(8,128)(2,1)S(1)}, bf16[48,1536]{1,0:T(8,128)(2,1)S(1)}, u32[]{:S(2)}, u32[]{:S(2)}) collective-permute-start(bf16[48,1536]{1,0:T(8,128)(2,1)S(1)} %get-tuple-element.45), channel_id=1, source_target_pairs={{0,4},{4,8},{8,12},{12,0},{16,20},{20,24},{24,28},{28,16},{1,5},{5... | collective-permute-start | bytes 442376 | tf_op jit(solution)/shard_map/ppermute | solution.py:524
  29.0 5.3 %collective-permute-start.7 = (bf16[48,1536]{1,0:T(8,128)(2,1)S(1)}, bf16[48,1536]{1,0:T(8,128)(2,1)S(1)}, u32[]{:S(2)}, u32[]{:S(2)}) collective-permute-start(bf16[48,1536]{1,0:T(8,128)(2,1)S(1)} %get-tuple-element.37.down), channel_id=1, source_target_pairs={{0,12},{4,0},{8,4},{12,8},{16,28},{20,16},{24,20},{28,24},{1,13},{... | collective-permute-start | bytes 442376 | tf_op jit(solution)/shard_map/ppermute | solution.py:523
  42.0 6.1 %collective-permute-start.11 = (f32[8,384]{1,0:T(8,128)S(1)}, f32[8,384]{1,0:T(8,128)S(1)}, u32[]{:S(2)}, u32[]{:S(2)}) collective-permute-start(f32[8,384]{1,0:T(8,128)S(1)} %constant_dynamic-update-slice_fusion.rest_0_), channel_id=1, source_target_pairs={{0,1},{1,2},{2,3},{3,0},{4,5},{5,6},{6,7},{7,4},{8,9},{9,10},{10,1... | collective-permute-start | bytes 36872 | tf_op jit(solution)/shard_map/ppermute | solution.py:608
  44.2 4.6 %collective-permute-start.12 = (f32[8,384]{1,0:T(8,128)S(1)}, f32[8,384]{1,0:T(8,128)S(1)}, u32[]{:S(2)}, u32[]{:S(2)}) collective-permute-start(f32[8,384]{1,0:T(8,128)S(1)} %constant_dynamic-update-slice_fusion.rest_0_), channel_id=1, source_target_pairs={{0,2},{1,3},{2,0},{3,1},{4,6},{5,7},{6,4},{7,5},{8,10},{9,11},{10,... | collective-permute-start | bytes 36872 | tf_op jit(solution)/shard_map/ppermute | solution.py:608
  46.8 3.7 %collective-permute-start.13 = (f32[8,384]{1,0:T(8,128)S(1)}, f32[8,384]{1,0:T(8,128)S(1)}, u32[]{:S(2)}, u32[]{:S(2)}) collective-permute-start(f32[8,384]{1,0:T(8,128)S(1)} %constant_dynamic-update-slice_fusion.rest_0_), channel_id=1, source_target_pairs={{0,3},{1,0},{2,1},{3,2},{4,7},{5,4},{6,5},{7,6},{8,11},{9,8},{10,9... | collective-permute-start | bytes 36872 | tf_op jit(solution)/shard_map/ppermute | solution.py:608

commit v5 on v4

--- a/solution.py
+++ b/solution.py
@@ -17,10 +17,6 @@
 TILE = 128
 WIDE = 256
 EDGE = 16
-
-
-def pairs_of(count, step):
-    return [(i, i + step) for i in range(count) if 0 <= i + step < count]
 
 
 def box_sum(x, lines):
@@ -64,11 +60,12 @@
                 near[at : at + EDGE, :] = turned[:, k * TILE : (k + 1) * TILE]
 
 
-def ends_kernel(lines, backward, ends, sem):
+def ends_kernel(lines, forward, backward, lead_ends, ends, sem):
     moves = []
-    for n, row in enumerate((0, lines - LINE_RIM)):
-        target = pl.ds(n * LINE_RIM, LINE_RIM)
-        moves.append((backward.at[pl.ds(row, LINE_RIM), :], ends.at[target, :]))
+    for slab, out in ((backward, ends), (forward, lead_ends)):
+        for n, row in enumerate((0, lines - LINE_RIM)):
+            target = pl.ds(n * LINE_RIM, LINE_RIM)
+            moves.append((slab.at[pl.ds(row, LINE_RIM), :], out.at[target, :]))
     copy_all(moves, sem)
 
 
@@ -117,33 +114,21 @@
     copy_all(moves, sem)
 
 
-def lines_kernel(lines, half_ring, place, forward, backward, lead, ends, down, up, sem):
-    in_half = lax.rem(place[0], half_ring)
+def lines_kernel(lines, flags, own_lead, own_ends, lead, ends, down, up):
     most, least = LINE_RIM, LINE_RIM // 2
-    for out, counts, raw_place in ((down, (least, most), 0), (up, (most, least), half_ring - 1)):
-        starts = (0, 0) if out is down else (lines - counts[0], lines - counts[1])
-        ended = 0 if out is down else 2 * LINE_RIM - counts[1]
-        tops = pl.ds(0, counts[0]), pl.ds(counts[0], counts[1])
-
-        @pl.when(in_half == raw_place)
-        def _(out=out, counts=counts, starts=starts, tops=tops):
-            copy_all(
-                [
-                    (slab.at[pl.ds(start, count), :], out.at[top, :])
-                    for slab, start, count, top in zip((forward, backward), starts, counts, tops)
-                ],
-                sem,
-            )
-
-        @pl.when(in_half != raw_place)
-        def _(out=out, counts=counts, starts=starts, ended=ended, tops=tops):
-            copy_all(
-                [
-                    (lead.at[pl.ds(starts[0], counts[0]), :], out.at[tops[0], :]),
-                    (ends.at[pl.ds(ended, counts[1]), :], out.at[tops[1], :]),
-                ],
-                sem,
-            )
+    for out, flag, counts in ((down, 0, (least, most)), (up, 1, (most, least))):
+        as_lies = flags[flag : flag + 1, :] > 0.5
+        at = 0
+        for own, crossed, tall, count in (
+            (own_lead, lead, lines, counts[0]),
+            (own_ends, ends, 2 * LINE_RIM, counts[1]),
+        ):
+            here = 0 if out is down else 2 * LINE_RIM - count
+            there = 0 if out is down else tall - count
+            lying = own[here : here + count, :].astype(jnp.float32)
+            moved = crossed[there : there + count, :].astype(jnp.float32)
+            out[at : at + count, :] = jnp.where(as_lies, lying, moved).astype(jnp.bfloat16)
+            at += count
 
 
 def positions(place, cols, total_cols, at, span):
@@ -199,8 +184,8 @@
 
 
 def bands_kernel(
-    lines, cols, total_lines, total_cols, lag_floor, place, lag, offsets, weights, shifts, taps,
-    line_bands, col_bands, levers, basis, rows_basis, upper, chosen,
+    lines, cols, total_lines, total_cols, half_ring, lag_floor, place, lag, offsets, weights, shifts,
+    taps, line_bands, col_bands, levers, basis, rows_basis, upper, chosen, flags,
 ):
     rows = lines + 16
     period = 4 * MODES
@@ -233,6 +218,10 @@
     own = row_at + lax.broadcasted_iota(jnp.int32, (2 * MODES, count), 1)
     mode = lax.broadcasted_iota(jnp.int32, (2 * MODES, count), 0)
     chosen[...] = jnp.where(own == mode, 1.0, 0.0)
+    in_half = lax.rem(place[0], half_ring)
+    row = lax.broadcasted_iota(jnp.int32, flags.shape, 0)
+    wanted = jnp.where(row == 0, 0, half_ring - 1)
+    flags[...] = jnp.where(wanted == in_half, 1.0, 0.0)
     begin = place[0] * lines
     ahead = pl.multiple_of(lax.rem(begin + total_lines - TILE, total_lines), TILE)
     behind = pl.multiple_of(lax.rem(begin + lines, total_lines), TILE)
@@ -281,8 +270,12 @@
     lead, first_part, second_part, third_part = (*rest[:count], None, None, None)[:4]
     rest = rest[count:]
     if not fresh:
-        earlier, rest = rest[0], rest[2:]
-    parallax, pulled, sem, *scratch = rest
+        earlier, rest = rest[0], rest[1:]
+    if fresh:
+        parallax, pulled, sem, *scratch = rest
+    else:
+        kept, (pulled, *scratch) = rest[: len(jobs)], rest[len(jobs) :]
+        scratch[2::3] = kept
     rows = lines + 16
     half = lines // 2
     depth = half + 2 * LINE_RIM
@@ -363,11 +356,12 @@
                 weighted = boxed * lever[:, there]
                 for k in range(2):
                     pulls[k] = pulls[k] + weighted * levers[k : k + 1, there]
-        write = pltpu.make_async_copy(
-            result, parallax.at[s, :, pl.ds(first, width)], sem.at[n]
-        )
-        write.start()
-        writes.append(write)
+        if fresh:
+            write = pltpu.make_async_copy(
+                result, parallax.at[s, :, pl.ds(first, width)], sem.at[n]
+            )
+            write.start()
+            writes.append(write)
     if last:
         pulled[...] = jnp.zeros_like(pulled)
         for k in range(2):
@@ -378,6 +372,17 @@
             pulled[k] = pulls[k]
     for write in writes:
         write.wait()
+
+
+def store_kernel(jobs, *rest):
+    parallax, sem = rest[-2:]
+    copy_all(
+        [
+            (kept, parallax.at[s, :, pl.ds(first, width)])
+            for kept, (s, first, width) in zip(rest, jobs)
+        ],
+        sem,
+    )
 
 
 def final_kernel(lines, scale_pull, basis, rows_basis, upper, chosen, *rest):
@@ -414,15 +419,23 @@
     lag_floor = CAMERA_LAG // total_lines * total_lines + half_ring * lines
     rows = lines + 16
     whole = cols + 2 * TILE
-    low_z, high_z = pairs_of(cross_count, -1), pairs_of(cross_count, 1)
-    ring_down = [(i, (i - 1) % along_count) for i in range(along_count)]
-    ring_up = [(i, (i + 1) % along_count) for i in range(along_count)]
-    half_down, half_up = [], []
-    for i in range(along_count):
-        base = i // half_ring * half_ring
-        half_down.append((i, base + (i - base - 1) % half_ring))
-        half_up.append((i, base + (i - base + 1) % half_ring))
+    assert cross_count % 2 == 0 and half_ring % 2 == 0
+    even_along, even_cross = along_index % 2 == 0, cross_index % 2 == 0
     across = [(i, (i + half_ring) % along_count) for i in range(along_count)]
+
+    def swap(axis, pairs, even, to_before, to_behind):
+        count = lax.axis_size(axis)
+        inside = [(i, i ^ 1) for i in range(count)]
+        both = [*pairs, *((j, i) for i, j in pairs)]
+        near = lax.ppermute(jnp.where(even, to_behind, to_before), axis, inside)
+        far = lax.ppermute(jnp.where(even, to_before, to_behind), axis, both)
+        return jnp.where(even, far, near), jnp.where(even, near, far)
+
+    whole_ring = [(i, (i + 1) % along_count) for i in range(1, along_count, 2)]
+    half_rings = [
+        (i, i // half_ring * half_ring + (i + 1) % half_ring) for i in range(1, along_count, 2)
+    ]
+    line = [(i, i + 1) for i in range(1, cross_count - 1, 2)]
 
     def over(value):
         return lax.ppermute(value, "along", across)
@@ -453,12 +466,12 @@
     place = jnp.stack([along_index, cross_index, window_start[0]]).astype(jnp.int32)
 
     lead = over(forward)
-    (own_ends,) = mover(
+    own_lead, own_ends = mover(
         functools.partial(ends_kernel, lines),
         "ends",
-        ((2 * LINE_RIM, cols),),
-        (hbm(backward),),
-        2,
+        ((2 * LINE_RIM, cols), (2 * LINE_RIM, cols)),
+        (hbm(forward), hbm(backward)),
+        4,
     )
     ends = over(own_ends)
     cuts = (cols // 2, cols - lines - TILE)
@@ -474,13 +487,14 @@
     )
     first_part = over(first_part)
 
-    from_right = lax.ppermute(near_first, "cross", low_z)
-    from_left = lax.ppermute(near_last, "cross", high_z)
+    from_left, from_right = swap("cross", line, even_cross, near_first, near_last)
     depth = lines // 2 + 2 * LINE_RIM
     row_count = 4 * MODES // cross_count
     assert 2 * MODES % row_count == 0
     bands = pl.pallas_call(
-        functools.partial(bands_kernel, lines, cols, total_lines, total_cols, lag_floor),
+        functools.partial(
+            bands_kernel, lines, cols, total_lines, total_cols, half_ring, lag_floor
+        ),
         out_shape=(
             jax.ShapeDtypeStruct((2, rows, depth), bf16),
             jax.ShapeDtypeStruct((2, WIDE + 2 * EDGE, cols), bf16),
@@ -489,9 +503,10 @@
             jax.ShapeDtypeStruct((row_count, lines), f32),
             jax.ShapeDtypeStruct((8, lines), f32),
             jax.ShapeDtypeStruct((2 * MODES, row_count), f32),
+            jax.ShapeDtypeStruct((8, cols), f32),
         ),
         in_specs=[smem] + [vmem] * 5,
-        out_specs=(vmem,) * 7,
+        out_specs=(vmem,) * 8,
         compiler_params=limit,
         cost_estimate=pl.CostEstimate(
             flops=20 * 300 * cols, bytes_accessed=4 * 300 * cols, transcendentals=0
@@ -501,7 +516,7 @@
         place, lag_lines[None], hbm(band_offsets), hbm(along_weights), hbm(col_offsets),
         hbm(cross_weights),
     )
-    line_bands, col_bands, levers, basis, rows_basis, upper, chosen = bands
+    line_bands, col_bands, levers, basis, rows_basis, upper, chosen, flags = bands
     first_lines, last_lines = mover(
         functools.partial(nadir_lines_kernel, lines, cols),
         "nadir_lines",
@@ -509,19 +524,21 @@
         (hbm(nadir_view), from_left, from_right, line_bands),
         14,
     )
-    nadir_below = lax.ppermute(first_lines, "along", ring_down)
-    nadir_above = lax.ppermute(last_lines, "along", ring_up)
-
-    down, up = mover(
-        functools.partial(lines_kernel, lines, half_ring),
-        "lines",
-        ((3 * LINE_RIM // 2, cols), (3 * LINE_RIM // 2, cols)),
-        (place, hbm(forward), hbm(backward), lead, ends),
-        2,
-        1,
-    )
-    slab_below = lax.ppermute(down, "along", half_down)
-    slab_above = lax.ppermute(up, "along", half_up)
+    nadir_above, nadir_below = swap("along", whole_ring, even_along, first_lines, last_lines)
+
+    most_lines = 3 * LINE_RIM // 2
+    down, up = pl.pallas_call(
+        functools.partial(lines_kernel, lines),
+        out_shape=(jax.ShapeDtypeStruct((most_lines, cols), bf16),) * 2,
+        in_specs=[vmem] * 5,
+        out_specs=(vmem, vmem),
+        compiler_params=limit,
+        cost_estimate=pl.CostEstimate(
+            flops=0, bytes_accessed=16 * most_lines * cols, transcendentals=0
+        ),
+        name="lines",
+    )(flags, own_lead, own_ends, lead, ends)
+    slab_above, slab_below = swap("along", half_rings, even_along, down, up)
 
     second_part, third_part = pl.pallas_call(
         functools.partial(late_kernel, lines, cols, cuts),
@@ -564,11 +581,9 @@
             ends, *crossed,
         ]
         specs = [vmem] * len(operands)
-        aliases = {}
         if not fresh:
-            aliases = {len(operands) + 1: 0}
-            operands += [so_far[1], so_far[0]]
-            specs += [vmem, any_space]
+            operands.append(so_far)
+            specs.append(vmem)
         scratch = []
         for _, _, width in jobs:
             scratch += [
@@ -580,13 +595,16 @@
         return pl.pallas_call(
             functools.partial(slab_kernel, lines, cols, cuts, jobs, len(crossed), fresh, last),
             out_shape=(
-                pltpu.HBM((2, lines, cols), bf16),
+                *(
+                    (pltpu.HBM((2, lines, cols), bf16),)
+                    if fresh
+                    else (jax.ShapeDtypeStruct((lines, width), bf16) for _, _, width in jobs)
+                ),
                 jax.ShapeDtypeStruct((8, TILE) if last else (2, lines, TILE), f32),
             ),
             in_specs=specs,
-            out_specs=(any_space, vmem),
-            scratch_shapes=[pltpu.SemaphoreType.DMA((len(jobs),)), *scratch],
-            input_output_aliases=aliases,
+            out_specs=(any_space, vmem) if fresh else (vmem,) * (len(jobs) + 1),
+            scratch_shapes=[pltpu.SemaphoreType.DMA((len(jobs),)), *scratch] if fresh else scratch,
             compiler_params=limit,
             cost_estimate=pl.CostEstimate(
                 flops=2 * rows * (done + 256) * 900, bytes_accessed=20 * rows * done, transcendentals=0
@@ -594,15 +612,30 @@
             name=name,
         )(*operands)
 
-    so_far = run("inner", [(0, TILE, cols - 2 * TILE)], [lead], None, False)
-    jobs = [(1, 0, cuts[1] - TILE), (0, 0, TILE), (0, cols - TILE, TILE)]
-    so_far = run("second", jobs, [lead, first_part, second_part], so_far, False)
-    jobs = [(1, cuts[1] - TILE, cols - cuts[1] + TILE)]
+    split = cuts[0] - TILE
+    jobs = [(0, TILE, cols - 2 * TILE), (1, TILE, split - TILE)]
+    parallax, pulls = run("inner", jobs, [lead, first_part], None, False)
+    jobs = [(1, split, cuts[1] - TILE - split), (0, 0, TILE), (0, cols - TILE, TILE), (1, 0, TILE)]
+    *kept, pulls = run("second", jobs, [lead, first_part, second_part], pulls, False)
+    last_jobs = [(1, cuts[1] - TILE, cols - cuts[1] + TILE)]
     crossed = [lead, first_part, second_part, third_part]
-    parallax, pulled = run("third", jobs, crossed, so_far, True)
+    *last_kept, pulled = run("third", last_jobs, crossed, pulls, True)
+    kept, jobs = [*kept, *last_kept], jobs + last_jobs
+    parallax = pl.pallas_call(
+        functools.partial(store_kernel, jobs),
+        out_shape=pltpu.HBM((2, lines, cols), bf16),
+        in_specs=[vmem] * len(kept) + [any_space],
+        out_specs=any_space,
+        scratch_shapes=[pltpu.SemaphoreType.DMA((len(kept),))],
+        input_output_aliases={len(kept): 0},
+        compiler_params=limit,
+        cost_estimate=pl.CostEstimate(flops=0, bytes_accessed=2 * lines * cols, transcendentals=0),
+        name="store",
+    )(*kept, parallax)
 
     share = jnp.concatenate([sums, pulled], axis=1)
     shares = [share]
+    assert cross_count & (cross_count - 1) == 0
     for shift_by in range(1, cross_count):
         pairs = [(i, (i + shift_by) % cross_count) for i in range(cross_count)]
         shares.append(lax.ppermute(share, "cross", pairs))

time: 51.9 us -> 50.5 us (0.973)
  waiting for transfers between devices: 6.97 us -> 11 us
  starting transfers between devices: 22.6 us -> 19.1 us
  Pallas kernels: 20.3 us -> 18.4 us
    ppermute x5, waiting for transfers between devices: 3 us -> 7.29 us  [over(): return lax.ppermute(value, 'along', across)]
    ppermute x6, starting transfers between devices: 9.74 us -> 6.12 us  [the longest x3 4.33 us: swap(): far = lax.ppermute(jnp.where(even, to_before, to_behind), axis, both)]
    pallas_call x4 -> x3, Pallas kernels: 4.84 us -> 3.32 us  [mover(): pl.pallas_call(kernel, out_shape=tuple((jax.ShapeDtypeStruct(shape, bf16)...]
    pallas_call x3, Pallas kernels: 6.59 us -> 5.21 us  [run(): pl.pallas_call(functools.partial(slab_kernel, lines, cols, cuts, jobs, le...]
    pallas_call x0 -> x2, Pallas kernels: none -> 0.95 us  [the longest x1 0.87 us: local(): pl.pallas_call(functools.partial(store_kernel, jobs), out_shape=pltpu.HBM...]
    ppermute x3, waiting for transfers between devices: 2.35 us -> 1.45 us  [local(): shares.append(lax.ppermute(share, 'cross', pairs))]
    ppermute x6, waiting for transfers between devices: 1.62 us -> 2.23 us  [the longest x3 2.22 us: swap(): far = lax.ppermute(jnp.where(even, to_before, to_behind), axis, both)]
  transfers between devices with their start and end apart: 14 -> 14, of which waited for: 6 -> 6; matrix products, arithmetic and copies ran while one was open for 0% -> 0% of each run, Pallas kernels for 35% -> 33%
where the time goes in v5:
time: 50.5 us; the launch traced here: 50.1 us
  starting transfers between devices  19.1 us (38%)
  Pallas kernels  18.4 us (36%)
  waiting for transfers between devices  11 us (22%)
  between operations  1.5 us (3%)
    ppermute x5, waiting for transfers between devices, over(): return lax.ppermute(value, 'along', across)  7.29 us
    ppermute x5, starting transfers between devices, over(): return lax.ppermute(value, 'along', across)  7.16 us
    ppermute x3, starting transfers between devices, local(): shares.append(lax.ppermute(share, 'cross', pairs))  5.79 us
    pallas_call x3, Pallas kernels, run(): pl.pallas_call(functools.partial(slab_kernel, lines, cols, cuts, jobs, le...  5.21 us
    ppermute x3, starting transfers between devices, swap(): far = lax.ppermute(jnp.where(even, to_before, to_behind), axis, both)  4.33 us
    pallas_call x1, Pallas kernels, local(): pl.pallas_call(functools.partial(prep_kernel, lines, cols, total_cols), o...  3.57 us
    pallas_call x3, Pallas kernels, mover(): pl.pallas_call(kernel, out_shape=tuple((jax.ShapeDtypeStruct(shape, bf16)...  3.32 us
    pallas_call x1, Pallas kernels, local(): pl.pallas_call(functools.partial(bands_kernel, lines, cols, total_lines,...  3.3 us
  transfers between devices with their start and end apart: 14, of which 6 were waited for; matrix products, arithmetic and copies ran while one was open for 0% of the time, Pallas kernels for 33%

profile of v5, /device:TPU:0, one launch (start us, length us, event | category | flops | bytes accessed | tf_op | source)
XLA Modules:
  0.0 50.1 jit_solution(6242517559525488360)
XLA Ops:
  0.6 3.0 %collective-permute-start.4 = (bf16[256,1536]{1,0:T(8,128)(2,1)}, bf16[256,1536]{1,0:T(8,128)(2,1)S(1)}, u32[]{:S(2)}, u32[]{:S(2)}) collective-permute-start(bf16[256,1536]{1,0:T(8,128)(2,1)} %forward.3), channel_id=1, source_target_pairs={{0,16},{4,20},{8,24},{12,28},{16,0},{20,4},{24,8},{28,12},{1,17},{... | collective-permute-start | bytes 2359304 | tf_op jit(solution)/shard_map/ppermute | solution.py:441
  3.7 1.1 %ends.1 = (bf16[64,1536]{1,0:T(8,128)(2,1)S(1)}, bf16[64,1536]{1,0:T(8,128)(2,1)S(1)}) custom-call(bf16[256,1536]{1,0:T(8,128)(2,1)} %forward.3, bf16[256,1536]{1,0:T(8,128)(2,1)} %backward.5), custom_call_target="tpu_custom_call" | custom-call | bytes 786432 | tf_op jit(solution)/shard_map/ends/pallas_call | solution.py:453
  4.7 0.0 copy-start
  4.8 1.3 %cut.1 = (bf16[192,768]{1,0:T(8,128)(2,1)S(1)}, bf16[320,128]{1,0:T(8,128)(2,1)S(1)}, bf16[320,128]{1,0:T(8,128)(2,1)S(1)}) custom-call(bf16[256,1536]{1,0:T(8,128)(2,1)} %nadir.5, bf16[256,1536]{1,0:T(8,128)(2,1)} %forward.3, bf16[256,1536]{1,0:T(8,128)(2,1)} %backward.5, bf16[64,1536]{1,0:T(8,128)(2,1)S(1)} %get-tuple-element.38.ends.own_ends), custom_call_target="tpu_custom_call" | custom-call | bytes 917504 | tf_op jit(solution)/shard_map/cut/pallas_call | solution.py:453
  6.1 1.6 %collective-permute-start.1 = (bf16[320,128]{1,0:T(8,128)(2,1)S(1)}, bf16[320,128]{1,0:T(8,128)(2,1)S(1)}, u32[]{:S(2)}, u32[]{:S(2)}) collective-permute-start(bf16[320,128]{1,0:T(8,128)(2,1)S(1)} %get-tuple-element.79), channel_id=1, source_target_pairs={{0,1},{1,0},{2,3},{3,2},{4,5},{5,4},{6,7},{7,6},{8,9},{9,8},{10,11... | collective-permute-start | bytes 245768 | tf_op jit(solution)/shard_map/ppermute | solution.py:430
  7.7 0.7 %collective-permute-start = (bf16[320,128]{1,0:T(8,128)(2,1)S(1)}, bf16[320,128]{1,0:T(8,128)(2,1)S(1)}, u32[]{:S(2)}, u32[]{:S(2)}) collective-permute-start(bf16[320,128]{1,0:T(8,128)(2,1)S(1)} %get-tuple-element.80), channel_id=1, source_target_pairs={{1,2},{2,1},{5,6},{6,5},{9,10},{10,9},{13,14},{14,13},{17,18},{18,... | collective-permute-start | bytes 245768 | tf_op jit(solution)/shard_map/ppermute | solution.py:431
  9.0 0.1 pad_add_fusion.place
  9.1 0.0 copy-done
  9.1 3.3 %bands.1 = (bf16[2,272,192]{2,1,0:T(8,128)(2,1)S(1)}, bf16[2,288,1536]{2,1,0:T(8,128)(2,1)S(1)}, f32[8,1536]{1,0:T(8,128)S(1)}, f32[256,128]{1,0:T(8,128)S(1)}, ...) custom-call(s32[3]{0:T(128)S(1)} %pad_add_fusion.place, ...), custom_call_target="tpu_custom_call" | custom-call | flops 9216000 | bytes 1843200 | tf_op jit(solution)/shard_map/bands/pallas_call | solution.py:494
  12.4 0.0 collective-permute-done.1
  12.4 0.0 collective-permute-done
  12.5 1.0 %nadir_lines.1 = (bf16[16,2304]{1,0:T(8,128)(2,1)S(1)}, bf16[16,2304]{1,0:T(8,128)(2,1)S(1)}) custom-call(bf16[256,1536]{1,0:T(8,128)(2,1)} %nadir.5, bf16[320,128]{1,0:T(8,128)(2,1)S(1)} %get-tuple-element.78.from_left.left, bf16[320,128]{1,0:T(8,128)(2,1)S(1)} %get-tuple-element.77.from_right.right, bf16[2,272,192]{2,1,0:T(8,128)(2,1)S(1)} %get-tuple-element.41.bands.line_bands), custom_call_target="tpu_custom_call" | custom-call | bytes 294912 | tf_op jit(solution)/shard_map/nadir_lines/pallas_call | solution.py:453
  13.5 0.1 collective-permute-start.3
  13.6 1.5 %collective-permute-start.2 = (bf16[16,2304]{1,0:T(8,128)(2,1)S(1)}, bf16[16,2304]{1,0:T(8,128)(2,1)S(1)}, u32[]{:S(2)}, u32[]{:S(2)}) collective-permute-start(bf16[16,2304]{1,0:T(8,128)(2,1)S(1)} %get-tuple-element.84), channel_id=1, source_target_pairs={{4,8},{12,16},{20,24},{28,0},{8,4},{16,12},{24,20},{0,28},{5,9},{1... | collective-permute-start | bytes 221192 | tf_op jit(solution)/shard_map/ppermute | solution.py:431
  15.1 1.5 %collective-permute-start.5 = (bf16[64,1536]{1,0:T(8,128)(2,1)S(1)}, bf16[64,1536]{1,0:T(8,128)(2,1)S(1)}, u32[]{:S(2)}, u32[]{:S(2)}) collective-permute-start(bf16[64,1536]{1,0:T(8,128)(2,1)S(1)} %get-tuple-element.38.ends.own_ends), channel_id=1, source_target_pairs={{0,16},{4,20},{8,24},{12,28},{16,0},{20,4},{24,8},{28,12},{1,17},{... | collective-permute-start | bytes 589832 | tf_op jit(solution)/shard_map/ppermute | solution.py:441
  16.6 0.5 %collective-permute-start.8 = (bf16[192,768]{1,0:T(8,128)(2,1)S(1)}, bf16[192,768]{1,0:T(8,128)(2,1)S(1)}, u32[]{:S(2)}, u32[]{:S(2)}) collective-permute-start(bf16[192,768]{1,0:T(8,128)(2,1)S(1)} %get-tuple-element.55), channel_id=1, source_target_pairs={{0,16},{4,20},{8,24},{12,28},{16,0},{20,4},{24,8},{28,12},{1,17},{... | collective-permute-start | bytes 884744 | tf_op jit(solution)/shard_map/ppermute | solution.py:441
  17.1 0.0 collective-permute-done.3
  17.1 1.7 %collective-permute-done.2 = bf16[16,2304]{1,0:T(8,128)(2,1)S(1)} collective-permute-done((bf16[16,2304]{1,0:T(8,128)(2,1)S(1)}, bf16[16,2304]{1,0:T(8,128)(2,1)S(1)}, u32[]{:S(2)}, u32[]{:S(2)}) %collective-permute-start.2) | collective-permute-done | bytes 73760 | tf_op jit(solution)/shard_map/ppermute | solution.py:431
  18.9 1.1 %late_cut.1 = (bf16[256,384]{1,0:T(8,128)(2,1)S(1)}, bf16[192,384]{1,0:T(8,128)(2,1)S(1)}) custom-call(bf16[256,1536]{1,0:T(8,128)(2,1)} %backward.5, bf16[320,128]{1,0:T(8,128)(2,1)S(1)} %get-tuple-element.78.from_left.left, bf16[320,128]{1,0:T(8,128)(2,1)S(1)} %get-tuple-element.77.from_right.right, bf16[16,2304]{1,0:T(8,128)(2,1)S(1)} %get-tuple-element.82.above, ...), custom_call_target="tpu_custom_call" | custom-call | bytes 393216 | tf_op jit(solution)/shard_map/late_cut/pallas_call | solution.py:543
  20.0 0.2 collective-permute-start.9
  20.2 1.9 %collective-permute-start.10 = (bf16[192,384]{1,0:T(8,128)(2,1)S(1)}, bf16[192,384]{1,0:T(8,128)(2,1)S(1)}, u32[]{:S(2)}, u32[]{:S(2)}) collective-permute-start(bf16[192,384]{1,0:T(8,128)(2,1)S(1)} %get-tuple-element.62), channel_id=1, source_target_pairs={{0,16},{4,20},{8,24},{12,28},{16,0},{20,4},{24,8},{28,12},{1,17},{... | collective-permute-start | bytes 442376 | tf_op jit(solution)/shard_map/ppermute | solution.py:441
  22.1 5.2 %collective-permute-done.5.ends = bf16[64,1536]{1,0:T(8,128)(2,1)S(1)} collective-permute-done((bf16[64,1536]{1,0:T(8,128)(2,1)S(1)}, bf16[64,1536]{1,0:T(8,128)(2,1)S(1)}, u32[]{:S(2)}, u32[]{:S(2)}) %collective-permute-start.5) | collective-permute-done | bytes 196640 | tf_op jit(solution)/shard_map/ppermute | solution.py:441
  27.2 0.0 collective-permute-done.4.lead.rest_0_
  27.2 0.1 lines.1
  27.4 0.1 collective-permute-start.7
  27.4 2.1 %collective-permute-start.6 = (bf16[48,1536]{1,0:T(8,128)(2,1)S(1)}, bf16[48,1536]{1,0:T(8,128)(2,1)S(1)}, u32[]{:S(2)}, u32[]{:S(2)}) collective-permute-start(bf16[48,1536]{1,0:T(8,128)(2,1)S(1)} %get-tuple-element.76), channel_id=1, source_target_pairs={{4,8},{12,0},{20,24},{28,16},{8,4},{0,12},{24,20},{16,28},{5,9},{1... | collective-permute-start | bytes 442376 | tf_op jit(solution)/shard_map/ppermute | solution.py:431
  29.6 3.6 %prep.1 = (f32[272,1536]{1,0:T(8,128)S(1)}, bf16[272,1536]{1,0:T(8,128)(2,1)S(1)}, f32[256,1536]{1,0:T(8,128)S(1)}, f32[256,1536]{1,0:T(8,128)S(1)}, f32[8,256]{1,0:T(8,128)S(1)}) custom-call(s32[3]{0:T(128)S(1)} %pad_add_fusion.place, bf16[256,1536]{1,0:T(8,128)(2,1)} %nadir.5, bf16[320,128]{1,0:T(8,128)(2,1)S(1)} %get-tuple-element.78.from_left.left, ...), custom_call_target="tpu_custom_call" | custom-call | flops 427819008 | bytes 5013504 | tf_op jit(solution)/shard_map/prep/pallas_call | solution.py:558
  33.2 0.0 collective-permute-done.7
  33.2 0.5 collective-permute-done.6
  33.7 0.0 collective-permute-done.8.rest_1_
  33.7 2.9 %inner.1 = (bf16[2,256,1536]{2,1,0:T(8,128)(2,1)}, f32[2,256,128]{2,1,0:T(8,128)S(1)}) custom-call(f32[272,1536]{1,0:T(8,128)S(1)} %get-tuple-element.47.slopes, bf16[272,1536]{1,0:T(8,128)(2,1)S(1)} %get-tuple-element.48.center, f32[256,1536]{1,0:T(8,128)S(1)} %get-tuple-element.49.inverse, f32[256,1536]{1,0:T(8,128)S(1)} %get-tuple-element.50.lever, ...), custom_call_target="tpu_custom_call" | custom-call | flops 1002700800 | bytes 9748480 | tf_op jit(solution)/shard_map/inner/pallas_call | solution.py:595
  36.7 1.1 %collective-permute-done.9.rest_2_ = bf16[256,384]{1,0:T(8,128)(2,1)S(1)} collective-permute-done((bf16[256,384]{1,0:T(8,128)(2,1)S(1)}, bf16[256,384]{1,0:T(8,128)(2,1)S(1)}, u32[]{:S(2)}, u32[]{:S(2)}) %collective-permute-start.9) | collective-permute-done | bytes 196640 | tf_op jit(solution)/shard_map/ppermute | solution.py:441
  37.8 1.3 %second.1 = (bf16[256,384]{1,0:T(8,128)(2,1)S(1)}, bf16[256,128]{1,0:T(8,128)(2,1)S(1)}, bf16[256,128]{1,0:T(8,128)(2,1)S(1)}, bf16[256,128]{1,0:T(8,128)(2,1)S(1)}, f32[2,256,128]{2,1,0:T(8,128)S(1)}) custom-call(f32[272,1536]{1,0:T(8,128)S(1)} %get-tuple-element.47.slopes, bf16[272,1536]{1,0:T(8,128)(2,1)S(1)} %get-tuple-element.48.center, ...), custom_call_target="tpu_custom_call" | custom-call | flops 501350400 | bytes 4177920 | tf_op jit(solution)/shard_map/second/pallas_call | solution.py:595
  39.1 1.0 %collective-permute-done.10.rest_3_ = bf16[192,384]{1,0:T(8,128)(2,1)S(1)} collective-permute-done((bf16[192,384]{1,0:T(8,128)(2,1)S(1)}, bf16[192,384]{1,0:T(8,128)(2,1)S(1)}, u32[]{:S(2)}, u32[]{:S(2)}) %collective-permute-start.10) | collective-permute-done | bytes 147488 | tf_op jit(solution)/shard_map/ppermute | solution.py:441
  40.1 0.9 %third.1 = (bf16[256,512]{1,0:T(8,128)(2,1)S(1)}, f32[8,128]{1,0:T(8,128)S(1)}) custom-call(f32[272,1536]{1,0:T(8,128)S(1)} %get-tuple-element.47.slopes, bf16[272,1536]{1,0:T(8,128)(2,1)S(1)} %get-tuple-element.48.center, f32[256,1536]{1,0:T(8,128)S(1)} %get-tuple-element.49.inverse, f32[256,1536]{1,0:T(8,128)S(1)} %get-tuple-element.50.lever, ...), custom_call_target="tpu_custom_call" | custom-call | flops 376012800 | bytes 2785280 | tf_op jit(solution)/shard_map/third/pallas_call | solution.py:595
  41.1 1.8 %collective-permute-start.11 = (f32[8,384]{1,0:T(8,128)S(1)}, f32[8,384]{1,0:T(8,128)S(1)}, u32[]{:S(2)}, u32[]{:S(2)}) collective-permute-start(f32[8,384]{1,0:T(8,128)S(1)} %constant_dynamic-update-slice_fusion.rest_0_), channel_id=1, source_target_pairs={{0,1},{1,2},{2,3},{3,0},{4,5},{5,6},{6,7},{7,4},{8,9},{9,10},{10,1... | collective-permute-start | bytes 36872 | tf_op jit(solution)/shard_map/ppermute | solution.py:641
  42.9 2.6 %collective-permute-start.12 = (f32[8,384]{1,0:T(8,128)S(1)}, f32[8,384]{1,0:T(8,128)S(1)}, u32[]{:S(2)}, u32[]{:S(2)}) collective-permute-start(f32[8,384]{1,0:T(8,128)S(1)} %constant_dynamic-update-slice_fusion.rest_0_), channel_id=1, source_target_pairs={{0,2},{1,3},{2,0},{3,1},{4,6},{5,7},{6,4},{7,5},{8,10},{9,11},{10,... | collective-permute-start | bytes 36872 | tf_op jit(solution)/shard_map/ppermute | solution.py:641
  45.5 1.3 %collective-permute-start.13 = (f32[8,384]{1,0:T(8,128)S(1)}, f32[8,384]{1,0:T(8,128)S(1)}, u32[]{:S(2)}, u32[]{:S(2)}) collective-permute-start(f32[8,384]{1,0:T(8,128)S(1)} %constant_dynamic-update-slice_fusion.rest_0_), channel_id=1, source_target_pairs={{0,3},{1,0},{2,1},{3,2},{4,7},{5,4},{6,5},{7,6},{8,11},{9,8},{10,9... | collective-permute-start | bytes 36872 | tf_op jit(solution)/shard_map/ppermute | solution.py:641
  46.9 0.9 %store.1 = bf16[2,256,1536]{2,1,0:T(8,128)(2,1)} custom-call(bf16[256,384]{1,0:T(8,128)(2,1)S(1)} %get-tuple-element.58.rest_0_, bf16[256,128]{1,0:T(8,128)(2,1)S(1)} %get-tuple-element.59.rest_1_, bf16[256,128]{1,0:T(8,128)(2,1)S(1)} %get-tuple-element.60.rest_2_, bf16[256,128]{1,0:T(8,128)(2,1)S(1)} %get-tuple-element.61.rest_3_, ...), custom_call_target="tpu_custom_call", output_to_operand_aliasing={{}: (5, {})} | custom-call | bytes 786432 | tf_op jit(solution)/shard_map/store/pallas_call | solution.py:624
  47.7 0.0 collective-permute-done.11.rest_1_
  47.7 0.0 collective-permute-done.12.rest_2_
  47.8 1.4 %collective-permute-done.13.rest_3_ = f32[8,384]{1,0:T(8,128)S(1)} collective-permute-done((f32[8,384]{1,0:T(8,128)S(1)}, f32[8,384]{1,0:T(8,128)S(1)}, u32[]{:S(2)}, u32[]{:S(2)}) %collective-permute-start.13) | collective-permute-done | bytes 12320 | tf_op jit(solution)/shard_map/ppermute | solution.py:641
  49.2 0.9 %final.1 = (f32[1,64,256]{2,1,0:T(8,128)}, f32[1,64]{1,0:T(1,128)}) custom-call(f32[256,128]{1,0:T(8,128)S(1)} %get-tuple-element.53.basis, f32[64,256]{1,0:T(8,128)S(1)} %get-tuple-element.66.rows_basis, f32[8,256]{1,0:T(8,128)S(1)} %get-tuple-element.67.upper, f32[128,64]{1,0:T(8,128)S(1)} %get-tuple-element.68.chosen, ...), custom_call_target="tpu_custom_call" | custom-call | tf_op jit(solution)/shard_map/final/pallas_call | solution.py:643
  (8 shorter events, 0.1 us)
Async XLA Ops:
  0.6 26.6 %collective-permute-start.4 = (bf16[256,1536]{1,0:T(8,128)(2,1)}, bf16[256,1536]{1,0:T(8,128)(2,1)S(1)}, u32[]{:S(2)}, u32[]{:S(2)}) collective-permute-start(bf16[256,1536]{1,0:T(8,128)(2,1)} %forward.3), channel_id=1, source_target_pairs={{0,16},{4,20},{8,24},{12,28},{16,0},{20,4},{24,8},{28,12},{1,17},{... | collective-permute-start | bytes 2359304 | tf_op jit(solution)/shard_map/ppermute | solution.py:441
  4.7 4.4 %copy-start = (s32[2048]{0:T(1024)S(1)}, s32[2048]{0:T(1024)}, u32[]{:S(2)}) copy-start(s32[2048]{0:T(1024)} %param.16) | copy-start | bytes 24580
  6.1 6.4 %collective-permute-start.1 = (bf16[320,128]{1,0:T(8,128)(2,1)S(1)}, bf16[320,128]{1,0:T(8,128)(2,1)S(1)}, u32[]{:S(2)}, u32[]{:S(2)}) collective-permute-start(bf16[320,128]{1,0:T(8,128)(2,1)S(1)} %get-tuple-element.79), channel_id=1, source_target_pairs={{0,1},{1,0},{2,3},{3,2},{4,5},{5,4},{6,7},{7,6},{8,9},{9,8},{10,11... | collective-permute-start | bytes 245768 | tf_op jit(solution)/shard_map/ppermute | solution.py:430
  7.7 4.7 %collective-permute-start = (bf16[320,128]{1,0:T(8,128)(2,1)S(1)}, bf16[320,128]{1,0:T(8,128)(2,1)S(1)}, u32[]{:S(2)}, u32[]{:S(2)}) collective-permute-start(bf16[320,128]{1,0:T(8,128)(2,1)S(1)} %get-tuple-element.80), channel_id=1, source_target_pairs={{1,2},{2,1},{5,6},{6,5},{9,10},{10,9},{13,14},{14,13},{17,18},{18,... | collective-permute-start | bytes 245768 | tf_op jit(solution)/shard_map/ppermute | solution.py:431
  13.5 3.7 %collective-permute-start.3 = (bf16[16,2304]{1,0:T(8,128)(2,1)S(1)}, bf16[16,2304]{1,0:T(8,128)(2,1)S(1)}, u32[]{:S(2)}, u32[]{:S(2)}) collective-permute-start(bf16[16,2304]{1,0:T(8,128)(2,1)S(1)} %get-tuple-element.83), channel_id=1, source_target_pairs={{0,4},{4,0},{8,12},{12,8},{16,20},{20,16},{24,28},{28,24},{1,5},{5... | collective-permute-start | bytes 221192 | tf_op jit(solution)/shard_map/ppermute | solution.py:430
  13.6 5.3 %collective-permute-start.2 = (bf16[16,2304]{1,0:T(8,128)(2,1)S(1)}, bf16[16,2304]{1,0:T(8,128)(2,1)S(1)}, u32[]{:S(2)}, u32[]{:S(2)}) collective-permute-start(bf16[16,2304]{1,0:T(8,128)(2,1)S(1)} %get-tuple-element.84), channel_id=1, source_target_pairs={{4,8},{12,16},{20,24},{28,0},{8,4},{16,12},{24,20},{0,28},{5,9},{1... | collective-permute-start | bytes 221192 | tf_op jit(solution)/shard_map/ppermute | solution.py:431
  15.1 12.2 %collective-permute-start.5 = (bf16[64,1536]{1,0:T(8,128)(2,1)S(1)}, bf16[64,1536]{1,0:T(8,128)(2,1)S(1)}, u32[]{:S(2)}, u32[]{:S(2)}) collective-permute-start(bf16[64,1536]{1,0:T(8,128)(2,1)S(1)} %get-tuple-element.38.ends.own_ends), channel_id=1, source_target_pairs={{0,16},{4,20},{8,24},{12,28},{16,0},{20,4},{24,8},{28,12},{1,17},{... | collective-permute-start | bytes 589832 | tf_op jit(solution)/shard_map/ppermute | solution.py:441
  16.6 17.1 %collective-permute-start.8 = (bf16[192,768]{1,0:T(8,128)(2,1)S(1)}, bf16[192,768]{1,0:T(8,128)(2,1)S(1)}, u32[]{:S(2)}, u32[]{:S(2)}) collective-permute-start(bf16[192,768]{1,0:T(8,128)(2,1)S(1)} %get-tuple-element.55), channel_id=1, source_target_pairs={{0,16},{4,20},{8,24},{12,28},{16,0},{20,4},{24,8},{28,12},{1,17},{... | collective-permute-start | bytes 884744 | tf_op jit(solution)/shard_map/ppermute | solution.py:441
  20.0 17.8 %collective-permute-start.9 = (bf16[256,384]{1,0:T(8,128)(2,1)S(1)}, bf16[256,384]{1,0:T(8,128)(2,1)S(1)}, u32[]{:S(2)}, u32[]{:S(2)}) collective-permute-start(bf16[256,384]{1,0:T(8,128)(2,1)S(1)} %get-tuple-element.56), channel_id=1, source_target_pairs={{0,16},{4,20},{8,24},{12,28},{16,0},{20,4},{24,8},{28,12},{1,17},{... | collective-permute-start | bytes 589832 | tf_op jit(solution)/shard_map/ppermute | solution.py:441
  20.2 19.9 %collective-permute-start.10 = (bf16[192,384]{1,0:T(8,128)(2,1)S(1)}, bf16[192,384]{1,0:T(8,128)(2,1)S(1)}, u32[]{:S(2)}, u32[]{:S(2)}) collective-permute-start(bf16[192,384]{1,0:T(8,128)(2,1)S(1)} %get-tuple-element.62), channel_id=1, source_target_pairs={{0,16},{4,20},{8,24},{12,28},{16,0},{20,4},{24,8},{28,12},{1,17},{... | collective-permute-start | bytes 442376 | tf_op jit(solution)/shard_map/ppermute | solution.py:441
  27.4 5.8 %collective-permute-start.7 = (bf16[48,1536]{1,0:T(8,128)(2,1)S(1)}, bf16[48,1536]{1,0:T(8,128)(2,1)S(1)}, u32[]{:S(2)}, u32[]{:S(2)}) collective-permute-start(bf16[48,1536]{1,0:T(8,128)(2,1)S(1)} %get-tuple-element.75), channel_id=1, source_target_pairs={{0,4},{4,0},{8,12},{12,8},{16,20},{20,16},{24,28},{28,24},{1,5},{5... | collective-permute-start | bytes 442376 | tf_op jit(solution)/shard_map/ppermute | solution.py:430
  27.4 6.2 %collective-permute-start.6 = (bf16[48,1536]{1,0:T(8,128)(2,1)S(1)}, bf16[48,1536]{1,0:T(8,128)(2,1)S(1)}, u32[]{:S(2)}, u32[]{:S(2)}) collective-permute-start(bf16[48,1536]{1,0:T(8,128)(2,1)S(1)} %get-tuple-element.76), channel_id=1, source_target_pairs={{4,8},{12,0},{20,24},{28,16},{8,4},{0,12},{24,20},{16,28},{5,9},{1... | collective-permute-start | bytes 442376 | tf_op jit(solution)/shard_map/ppermute | solution.py:431
  41.1 6.7 %collective-permute-start.11 = (f32[8,384]{1,0:T(8,128)S(1)}, f32[8,384]{1,0:T(8,128)S(1)}, u32[]{:S(2)}, u32[]{:S(2)}) collective-permute-start(f32[8,384]{1,0:T(8,128)S(1)} %constant_dynamic-update-slice_fusion.rest_0_), channel_id=1, source_target_pairs={{0,1},{1,2},{2,3},{3,0},{4,5},{5,6},{6,7},{7,4},{8,9},{9,10},{10,1... | collective-permute-start | bytes 36872 | tf_op jit(solution)/shard_map/ppermute | solution.py:641
  42.9 4.8 %collective-permute-start.12 = (f32[8,384]{1,0:T(8,128)S(1)}, f32[8,384]{1,0:T(8,128)S(1)}, u32[]{:S(2)}, u32[]{:S(2)}) collective-permute-start(f32[8,384]{1,0:T(8,128)S(1)} %constant_dynamic-update-slice_fusion.rest_0_), channel_id=1, source_target_pairs={{0,2},{1,3},{2,0},{3,1},{4,6},{5,7},{6,4},{7,5},{8,10},{9,11},{10,... | collective-permute-start | bytes 36872 | tf_op jit(solution)/shard_map/ppermute | solution.py:641
  45.5 3.7 %collective-permute-start.13 = (f32[8,384]{1,0:T(8,128)S(1)}, f32[8,384]{1,0:T(8,128)S(1)}, u32[]{:S(2)}, u32[]{:S(2)}) collective-permute-start(f32[8,384]{1,0:T(8,128)S(1)} %constant_dynamic-update-slice_fusion.rest_0_), channel_id=1, source_target_pairs={{0,3},{1,0},{2,1},{3,2},{4,7},{5,4},{6,5},{7,6},{8,11},{9,8},{10,9... | collective-permute-start | bytes 36872 | tf_op jit(solution)/shard_map/ppermute | solution.py:641

commit v6 on v5

--- a/solution.py
+++ b/solution.py
@@ -17,6 +17,7 @@
 TILE = 128
 WIDE = 256
 EDGE = 16
+LESS = 8
 
 
 def box_sum(x, lines):
@@ -97,20 +98,24 @@
         (backward.at[body, pl.ds(cuts[1], cols - cuts[1])], third),
     ]
     lane = lax.broadcasted_iota(jnp.int32, (EDGE, TILE), 1)
+    kinds = []
     for k in range(4):
-        row = height + k * EDGE
         near = (from_left, from_right)[k // 2]
+        tiles = []
         for tile in range(lines // TILE):
             at = lines + (k % 2 * (lines // TILE) + tile) * EDGE
-            window = second.at[pl.ds(row, EDGE), pl.ds(tile * TILE, TILE)]
-            moves.append((near.at[pl.ds(at, EDGE), :], window))
+            tiles.append(near[at : at + EDGE, :].astype(jnp.float32))
         here = slice(whole + k * TILE, whole + (k + 1) * TILE)
         ahead = above[:, here].astype(jnp.float32)
         behind = below[:, here].astype(jnp.float32)
-        both = jnp.where(lane < TILE // 2, behind, ahead).astype(jnp.bfloat16)
-        second[row : row + EDGE, lines : lines + TILE] = both
+        tiles.append(jnp.where(lane < TILE // 2, behind, ahead))
+        kinds.append(jnp.concatenate(tiles, axis=1))
+    left = jnp.concatenate([kind[EDGE - LESS :] for kind in kinds[:2]], axis=0)
+    for n, block in enumerate((left, *kinds[2:])):
+        row = height + n * EDGE
+        second[row : row + EDGE, : lines + TILE] = block.astype(jnp.bfloat16)
     if width > lines + TILE:
-        second[height:, lines + TILE :] = jnp.zeros((4 * EDGE, width - lines - TILE), jnp.bfloat16)
+        second[height:, lines + TILE :] = jnp.zeros((3 * EDGE, width - lines - TILE), jnp.bfloat16)
     copy_all(moves, sem)
 
 
@@ -316,9 +321,11 @@
         for side in range(2):
             if (low < 0, high > cols)[side]:
                 at = 0 if side == 0 else width + TILE
-                row = height + (2 * side + s) * EDGE
+                row = height + (0 if side == 0 else (1 + s) * EDGE)
                 piece = second_part[row : row + EDGE, : lines + TILE].astype(jnp.float32)
-                gap = jnp.zeros((TILE - EDGE, lines + TILE), jnp.float32)
+                if side == 0:
+                    piece = piece[s * LESS : (s + 1) * LESS]
+                gap = jnp.zeros((TILE - piece.shape[0], lines + TILE), jnp.float32)
                 piece = jnp.concatenate([gap, piece] if side == 0 else [piece, gap], axis=0)
                 turned = piece.T.astype(jnp.bfloat16)
                 ext[LINE_RIM : LINE_RIM + lines, at : at + TILE] = turned[:lines]
@@ -392,16 +399,23 @@
         total = total + share[...]
     is_upper = upper[0:1, :] > 0.5
     sums = total[:, :lines]
-    precision = lax.Precision.HIGHEST
-    for n in range(2):
-        coef = jnp.where(is_upper, sums[n + 1 : n + 2], sums[n : n + 1])
-        gram[0, :, n * TILE : (n + 1) * TILE] = jnp.dot(
-            rows_basis[...] * coef, basis[...], precision=precision, preferred_element_type=jnp.float32
-        )
+    count = rows_basis.shape[0]
+    rows = [
+        rows_basis[...] * jnp.where(is_upper, sums[n + 1 : n + 2], sums[n : n + 1]) for n in range(2)
+    ]
+    both = jnp.dot(
+        jnp.concatenate(rows, axis=0),
+        basis[...],
+        precision=lax.Precision.HIGHEST,
+        preferred_element_type=jnp.float32,
+    )
+    gram[0, :, :TILE] = both[:count]
+    gram[0, :, TILE:] = both[count:]
     pull = jnp.where(is_upper[:, :TILE], total[1:2, lines:], total[0:1, lines:]) * scale_pull
-    rhs[...] = jnp.dot(
-        jnp.broadcast_to(pull, (8, TILE)), chosen[...], precision=precision, preferred_element_type=jnp.float32
-    )[0:1]
+    own = jnp.zeros((1, count), jnp.float32)
+    for at in range(0, TILE, count):
+        own = jnp.where(chosen[at : at + 1, 0:1] > 0.5, pull[:, at : at + count], own)
+    rhs[...] = own
 
 
 def local(
@@ -543,12 +557,12 @@
     second_part, third_part = pl.pallas_call(
         functools.partial(late_kernel, lines, cols, cuts),
         out_shape=(
-            jax.ShapeDtypeStruct((height + 4 * EDGE, cuts[1] - cuts[0]), bf16),
+            jax.ShapeDtypeStruct((height + 3 * EDGE, cuts[1] - cuts[0]), bf16),
             jax.ShapeDtypeStruct((height, cols - cuts[1]), bf16),
         ),
-        in_specs=[any_space, any_space, any_space, vmem, vmem],
+        in_specs=[any_space, vmem, vmem, vmem, vmem],
         out_specs=(vmem, vmem),
-        scratch_shapes=[pltpu.SemaphoreType.DMA((2 + 4 * lines // TILE,))],
+        scratch_shapes=[pltpu.SemaphoreType.DMA((2,))],
         compiler_params=limit,
         cost_estimate=pl.CostEstimate(flops=0, bytes_accessed=lines * cols, transcendentals=0),
         name="late_cut",

time: 50.5 us -> 50.2 us (level)
  no operation moved by 1% of the time
where the time goes in v6:
time: 50.2 us; the launch traced here: 49.9 us
  starting transfers between devices  19.1 us (38%)
  Pallas kernels  18.3 us (36%)
  waiting for transfers between devices  10.7 us (21%)
  between operations  1.5 us (3%)
    ppermute x5, starting transfers between devices, over(): return lax.ppermute(value, 'along', across)  7.16 us
    ppermute x5, waiting for transfers between devices, over(): return lax.ppermute(value, 'along', across)  7.07 us
    ppermute x3, starting transfers between devices, local(): shares.append(lax.ppermute(share, 'cross', pairs))  5.79 us
    pallas_call x3, Pallas kernels, run(): pl.pallas_call(functools.partial(slab_kernel, lines, cols, cuts, jobs, le...  5.27 us
    ppermute x3, starting transfers between devices, swap(): far = lax.ppermute(jnp.where(even, to_before, to_behind), axis, both)  4.33 us
    pallas_call x1, Pallas kernels, local(): pl.pallas_call(functools.partial(prep_kernel, lines, cols, total_cols), o...  3.58 us
    pallas_call x3, Pallas kernels, mover(): pl.pallas_call(kernel, out_shape=tuple((jax.ShapeDtypeStruct(shape, bf16)...  3.32 us
    pallas_call x1, Pallas kernels, local(): pl.pallas_call(functools.partial(bands_kernel, lines, cols, total_lines,...  3.3 us
  transfers between devices with their start and end apart: 14, of which 6 were waited for; matrix products, arithmetic and copies ran while one was open for 0% of the time, Pallas kernels for 33%

profile of v6, /device:TPU:0, one launch (start us, length us, event | category | flops | bytes accessed | tf_op | source)
XLA Modules:
  0.0 49.9 jit_solution(3060670526567796532)
XLA Ops:
  0.6 3.0 %collective-permute-start.4 = (bf16[256,1536]{1,0:T(8,128)(2,1)}, bf16[256,1536]{1,0:T(8,128)(2,1)S(1)}, u32[]{:S(2)}, u32[]{:S(2)}) collective-permute-start(bf16[256,1536]{1,0:T(8,128)(2,1)} %forward.3), channel_id=1, source_target_pairs={{0,16},{4,20},{8,24},{12,28},{16,0},{20,4},{24,8},{28,12},{1,17},{... | collective-permute-start | bytes 2359304 | tf_op jit(solution)/shard_map/ppermute | solution.py:455
  3.7 1.1 %ends.1 = (bf16[64,1536]{1,0:T(8,128)(2,1)S(1)}, bf16[64,1536]{1,0:T(8,128)(2,1)S(1)}) custom-call(bf16[256,1536]{1,0:T(8,128)(2,1)} %forward.3, bf16[256,1536]{1,0:T(8,128)(2,1)} %backward.5), custom_call_target="tpu_custom_call" | custom-call | bytes 786432 | tf_op jit(solution)/shard_map/ends/pallas_call | solution.py:467
  4.7 0.0 copy-start
  4.8 1.3 %cut.1 = (bf16[192,768]{1,0:T(8,128)(2,1)S(1)}, bf16[320,128]{1,0:T(8,128)(2,1)S(1)}, bf16[320,128]{1,0:T(8,128)(2,1)S(1)}) custom-call(bf16[256,1536]{1,0:T(8,128)(2,1)} %nadir.5, bf16[256,1536]{1,0:T(8,128)(2,1)} %forward.3, bf16[256,1536]{1,0:T(8,128)(2,1)} %backward.5, bf16[64,1536]{1,0:T(8,128)(2,1)S(1)} %get-tuple-element.38.ends.own_ends), custom_call_target="tpu_custom_call" | custom-call | bytes 917504 | tf_op jit(solution)/shard_map/cut/pallas_call | solution.py:467
  6.1 1.6 %collective-permute-start.1 = (bf16[320,128]{1,0:T(8,128)(2,1)S(1)}, bf16[320,128]{1,0:T(8,128)(2,1)S(1)}, u32[]{:S(2)}, u32[]{:S(2)}) collective-permute-start(bf16[320,128]{1,0:T(8,128)(2,1)S(1)} %get-tuple-element.79), channel_id=1, source_target_pairs={{0,1},{1,0},{2,3},{3,2},{4,5},{5,4},{6,7},{7,6},{8,9},{9,8},{10,11... | collective-permute-start | bytes 245768 | tf_op jit(solution)/shard_map/ppermute | solution.py:444
  7.7 0.7 %collective-permute-start = (bf16[320,128]{1,0:T(8,128)(2,1)S(1)}, bf16[320,128]{1,0:T(8,128)(2,1)S(1)}, u32[]{:S(2)}, u32[]{:S(2)}) collective-permute-start(bf16[320,128]{1,0:T(8,128)(2,1)S(1)} %get-tuple-element.80), channel_id=1, source_target_pairs={{1,2},{2,1},{5,6},{6,5},{9,10},{10,9},{13,14},{14,13},{17,18},{18,... | collective-permute-start | bytes 245768 | tf_op jit(solution)/shard_map/ppermute | solution.py:445
  9.0 0.1 pad_add_fusion.place
  9.1 0.0 copy-done
  9.1 3.3 %bands.1 = (bf16[2,272,192]{2,1,0:T(8,128)(2,1)S(1)}, bf16[2,288,1536]{2,1,0:T(8,128)(2,1)S(1)}, f32[8,1536]{1,0:T(8,128)S(1)}, f32[256,128]{1,0:T(8,128)S(1)}, ...) custom-call(s32[3]{0:T(128)S(1)} %pad_add_fusion.place, ...), custom_call_target="tpu_custom_call" | custom-call | flops 9216000 | bytes 1843200 | tf_op jit(solution)/shard_map/bands/pallas_call | solution.py:508
  12.4 0.0 collective-permute-done.1
  12.4 0.0 collective-permute-done
  12.5 1.0 %nadir_lines.1 = (bf16[16,2304]{1,0:T(8,128)(2,1)S(1)}, bf16[16,2304]{1,0:T(8,128)(2,1)S(1)}) custom-call(bf16[256,1536]{1,0:T(8,128)(2,1)} %nadir.5, bf16[320,128]{1,0:T(8,128)(2,1)S(1)} %get-tuple-element.78.from_left.left, bf16[320,128]{1,0:T(8,128)(2,1)S(1)} %get-tuple-element.77.from_right.right, bf16[2,272,192]{2,1,0:T(8,128)(2,1)S(1)} %get-tuple-element.41.bands.line_bands), custom_call_target="tpu_custom_call" | custom-call | bytes 294912 | tf_op jit(solution)/shard_map/nadir_lines/pallas_call | solution.py:467
  13.5 0.1 collective-permute-start.3
  13.6 1.5 %collective-permute-start.2 = (bf16[16,2304]{1,0:T(8,128)(2,1)S(1)}, bf16[16,2304]{1,0:T(8,128)(2,1)S(1)}, u32[]{:S(2)}, u32[]{:S(2)}) collective-permute-start(bf16[16,2304]{1,0:T(8,128)(2,1)S(1)} %get-tuple-element.84), channel_id=1, source_target_pairs={{4,8},{12,16},{20,24},{28,0},{8,4},{16,12},{24,20},{0,28},{5,9},{1... | collective-permute-start | bytes 221192 | tf_op jit(solution)/shard_map/ppermute | solution.py:445
  15.1 1.5 %collective-permute-start.5 = (bf16[64,1536]{1,0:T(8,128)(2,1)S(1)}, bf16[64,1536]{1,0:T(8,128)(2,1)S(1)}, u32[]{:S(2)}, u32[]{:S(2)}) collective-permute-start(bf16[64,1536]{1,0:T(8,128)(2,1)S(1)} %get-tuple-element.38.ends.own_ends), channel_id=1, source_target_pairs={{0,16},{4,20},{8,24},{12,28},{16,0},{20,4},{24,8},{28,12},{1,17},{... | collective-permute-start | bytes 589832 | tf_op jit(solution)/shard_map/ppermute | solution.py:455
  16.6 0.5 %collective-permute-start.8 = (bf16[192,768]{1,0:T(8,128)(2,1)S(1)}, bf16[192,768]{1,0:T(8,128)(2,1)S(1)}, u32[]{:S(2)}, u32[]{:S(2)}) collective-permute-start(bf16[192,768]{1,0:T(8,128)(2,1)S(1)} %get-tuple-element.55), channel_id=1, source_target_pairs={{0,16},{4,20},{8,24},{12,28},{16,0},{20,4},{24,8},{28,12},{1,17},{... | collective-permute-start | bytes 884744 | tf_op jit(solution)/shard_map/ppermute | solution.py:455
  17.1 0.0 collective-permute-done.3
  17.1 1.7 %collective-permute-done.2 = bf16[16,2304]{1,0:T(8,128)(2,1)S(1)} collective-permute-done((bf16[16,2304]{1,0:T(8,128)(2,1)S(1)}, bf16[16,2304]{1,0:T(8,128)(2,1)S(1)}, u32[]{:S(2)}, u32[]{:S(2)}) %collective-permute-start.2) | collective-permute-done | bytes 73760 | tf_op jit(solution)/shard_map/ppermute | solution.py:445
  18.9 1.0 %late_cut.1 = (bf16[240,384]{1,0:T(8,128)(2,1)S(1)}, bf16[192,384]{1,0:T(8,128)(2,1)S(1)}) custom-call(bf16[256,1536]{1,0:T(8,128)(2,1)} %backward.5, bf16[320,128]{1,0:T(8,128)(2,1)S(1)} %get-tuple-element.78.from_left.left, bf16[320,128]{1,0:T(8,128)(2,1)S(1)} %get-tuple-element.77.from_right.right, bf16[16,2304]{1,0:T(8,128)(2,1)S(1)} %get-tuple-element.82.above, ...), custom_call_target="tpu_custom_call" | custom-call | bytes 393216 | tf_op jit(solution)/shard_map/late_cut/pallas_call | solution.py:557
  19.9 0.2 collective-permute-start.9
  20.1 1.9 %collective-permute-start.10 = (bf16[192,384]{1,0:T(8,128)(2,1)S(1)}, bf16[192,384]{1,0:T(8,128)(2,1)S(1)}, u32[]{:S(2)}, u32[]{:S(2)}) collective-permute-start(bf16[192,384]{1,0:T(8,128)(2,1)S(1)} %get-tuple-element.62), channel_id=1, source_target_pairs={{0,16},{4,20},{8,24},{12,28},{16,0},{20,4},{24,8},{28,12},{1,17},{... | collective-permute-start | bytes 442376 | tf_op jit(solution)/shard_map/ppermute | solution.py:455
  22.0 5.3 %collective-permute-done.5.ends = bf16[64,1536]{1,0:T(8,128)(2,1)S(1)} collective-permute-done((bf16[64,1536]{1,0:T(8,128)(2,1)S(1)}, bf16[64,1536]{1,0:T(8,128)(2,1)S(1)}, u32[]{:S(2)}, u32[]{:S(2)}) %collective-permute-start.5) | collective-permute-done | bytes 196640 | tf_op jit(solution)/shard_map/ppermute | solution.py:455
  27.2 0.0 collective-permute-done.4.lead.rest_0_
  27.2 0.1 lines.1
  27.4 0.1 collective-permute-start.7
  27.4 2.1 %collective-permute-start.6 = (bf16[48,1536]{1,0:T(8,128)(2,1)S(1)}, bf16[48,1536]{1,0:T(8,128)(2,1)S(1)}, u32[]{:S(2)}, u32[]{:S(2)}) collective-permute-start(bf16[48,1536]{1,0:T(8,128)(2,1)S(1)} %get-tuple-element.76), channel_id=1, source_target_pairs={{4,8},{12,0},{20,24},{28,16},{8,4},{0,12},{24,20},{16,28},{5,9},{1... | collective-permute-start | bytes 442376 | tf_op jit(solution)/shard_map/ppermute | solution.py:445
  29.6 3.6 %prep.1 = (f32[272,1536]{1,0:T(8,128)S(1)}, bf16[272,1536]{1,0:T(8,128)(2,1)S(1)}, f32[256,1536]{1,0:T(8,128)S(1)}, f32[256,1536]{1,0:T(8,128)S(1)}, f32[8,256]{1,0:T(8,128)S(1)}) custom-call(s32[3]{0:T(128)S(1)} %pad_add_fusion.place, bf16[256,1536]{1,0:T(8,128)(2,1)} %nadir.5, bf16[320,128]{1,0:T(8,128)(2,1)S(1)} %get-tuple-element.78.from_left.left, ...), custom_call_target="tpu_custom_call" | custom-call | flops 427819008 | bytes 5013504 | tf_op jit(solution)/shard_map/prep/pallas_call | solution.py:572
  33.2 0.0 collective-permute-done.7
  33.2 0.5 %collective-permute-done.6 = bf16[48,1536]{1,0:T(8,128)(2,1)S(1)} collective-permute-done((bf16[48,1536]{1,0:T(8,128)(2,1)S(1)}, bf16[48,1536]{1,0:T(8,128)(2,1)S(1)}, u32[]{:S(2)}, u32[]{:S(2)}) %collective-permute-start.6) | collective-permute-done | bytes 147488 | tf_op jit(solution)/shard_map/ppermute | solution.py:445
  33.7 0.0 collective-permute-done.8.rest_1_
  33.7 3.0 %inner.1 = (bf16[2,256,1536]{2,1,0:T(8,128)(2,1)}, f32[2,256,128]{2,1,0:T(8,128)S(1)}) custom-call(f32[272,1536]{1,0:T(8,128)S(1)} %get-tuple-element.47.slopes, bf16[272,1536]{1,0:T(8,128)(2,1)S(1)} %get-tuple-element.48.center, f32[256,1536]{1,0:T(8,128)S(1)} %get-tuple-element.49.inverse, f32[256,1536]{1,0:T(8,128)S(1)} %get-tuple-element.50.lever, ...), custom_call_target="tpu_custom_call" | custom-call | flops 1002700800 | bytes 9748480 | tf_op jit(solution)/shard_map/inner/pallas_call | solution.py:609
  36.7 0.8 %collective-permute-done.9.rest_2_ = bf16[240,384]{1,0:T(8,128)(2,1)S(1)} collective-permute-done((bf16[240,384]{1,0:T(8,128)(2,1)S(1)}, bf16[240,384]{1,0:T(8,128)(2,1)S(1)}, u32[]{:S(2)}, u32[]{:S(2)}) %collective-permute-start.9) | collective-permute-done | bytes 184352 | tf_op jit(solution)/shard_map/ppermute | solution.py:455
  37.5 1.4 %second.1 = (bf16[256,384]{1,0:T(8,128)(2,1)S(1)}, bf16[256,128]{1,0:T(8,128)(2,1)S(1)}, bf16[256,128]{1,0:T(8,128)(2,1)S(1)}, bf16[256,128]{1,0:T(8,128)(2,1)S(1)}, f32[2,256,128]{2,1,0:T(8,128)S(1)}) custom-call(f32[272,1536]{1,0:T(8,128)S(1)} %get-tuple-element.47.slopes, bf16[272,1536]{1,0:T(8,128)(2,1)S(1)} %get-tuple-element.48.center, ...), custom_call_target="tpu_custom_call" | custom-call | flops 501350400 | bytes 4177920 | tf_op jit(solution)/shard_map/second/pallas_call | solution.py:609
  38.9 1.0 %collective-permute-done.10.rest_3_ = bf16[192,384]{1,0:T(8,128)(2,1)S(1)} collective-permute-done((bf16[192,384]{1,0:T(8,128)(2,1)S(1)}, bf16[192,384]{1,0:T(8,128)(2,1)S(1)}, u32[]{:S(2)}, u32[]{:S(2)}) %collective-permute-start.10) | collective-permute-done | bytes 147488 | tf_op jit(solution)/shard_map/ppermute | solution.py:455
  39.8 0.9 %third.1 = (bf16[256,512]{1,0:T(8,128)(2,1)S(1)}, f32[8,128]{1,0:T(8,128)S(1)}) custom-call(f32[272,1536]{1,0:T(8,128)S(1)} %get-tuple-element.47.slopes, bf16[272,1536]{1,0:T(8,128)(2,1)S(1)} %get-tuple-element.48.center, f32[256,1536]{1,0:T(8,128)S(1)} %get-tuple-element.49.inverse, f32[256,1536]{1,0:T(8,128)S(1)} %get-tuple-element.50.lever, ...), custom_call_target="tpu_custom_call" | custom-call | flops 376012800 | bytes 2785280 | tf_op jit(solution)/shard_map/third/pallas_call | solution.py:609
  40.8 1.9 %collective-permute-start.11 = (f32[8,384]{1,0:T(8,128)S(1)}, f32[8,384]{1,0:T(8,128)S(1)}, u32[]{:S(2)}, u32[]{:S(2)}) collective-permute-start(f32[8,384]{1,0:T(8,128)S(1)} %constant_dynamic-update-slice_fusion.rest_0_), channel_id=1, source_target_pairs={{0,1},{1,2},{2,3},{3,0},{4,5},{5,6},{6,7},{7,4},{8,9},{9,10},{10,1... | collective-permute-start | bytes 36872 | tf_op jit(solution)/shard_map/ppermute | solution.py:655
  42.7 2.6 %collective-permute-start.12 = (f32[8,384]{1,0:T(8,128)S(1)}, f32[8,384]{1,0:T(8,128)S(1)}, u32[]{:S(2)}, u32[]{:S(2)}) collective-permute-start(f32[8,384]{1,0:T(8,128)S(1)} %constant_dynamic-update-slice_fusion.rest_0_), channel_id=1, source_target_pairs={{0,2},{1,3},{2,0},{3,1},{4,6},{5,7},{6,4},{7,5},{8,10},{9,11},{10,... | collective-permute-start | bytes 36872 | tf_op jit(solution)/shard_map/ppermute | solution.py:655
  45.2 1.3 %collective-permute-start.13 = (f32[8,384]{1,0:T(8,128)S(1)}, f32[8,384]{1,0:T(8,128)S(1)}, u32[]{:S(2)}, u32[]{:S(2)}) collective-permute-start(f32[8,384]{1,0:T(8,128)S(1)} %constant_dynamic-update-slice_fusion.rest_0_), channel_id=1, source_target_pairs={{0,3},{1,0},{2,1},{3,2},{4,7},{5,4},{6,5},{7,6},{8,11},{9,8},{10,9... | collective-permute-start | bytes 36872 | tf_op jit(solution)/shard_map/ppermute | solution.py:655
  46.6 0.9 %store.1 = bf16[2,256,1536]{2,1,0:T(8,128)(2,1)} custom-call(bf16[256,384]{1,0:T(8,128)(2,1)S(1)} %get-tuple-element.58.rest_0_, bf16[256,128]{1,0:T(8,128)(2,1)S(1)} %get-tuple-element.59.rest_1_, bf16[256,128]{1,0:T(8,128)(2,1)S(1)} %get-tuple-element.60.rest_2_, bf16[256,128]{1,0:T(8,128)(2,1)S(1)} %get-tuple-element.61.rest_3_, ...), custom_call_target="tpu_custom_call", output_to_operand_aliasing={{}: (5, {})} | custom-call | bytes 786432 | tf_op jit(solution)/shard_map/store/pallas_call | solution.py:638
  47.5 0.0 collective-permute-done.11.rest_1_
  47.5 0.0 collective-permute-done.12.rest_2_
  47.5 1.4 %collective-permute-done.13.rest_3_ = f32[8,384]{1,0:T(8,128)S(1)} collective-permute-done((f32[8,384]{1,0:T(8,128)S(1)}, f32[8,384]{1,0:T(8,128)S(1)}, u32[]{:S(2)}, u32[]{:S(2)}) %collective-permute-start.13) | collective-permute-done | bytes 12320 | tf_op jit(solution)/shard_map/ppermute | solution.py:655
  48.9 0.9 %final.1 = (f32[1,64,256]{2,1,0:T(8,128)}, f32[1,64]{1,0:T(1,128)}) custom-call(f32[256,128]{1,0:T(8,128)S(1)} %get-tuple-element.53.basis, f32[64,256]{1,0:T(8,128)S(1)} %get-tuple-element.66.rows_basis, f32[8,256]{1,0:T(8,128)S(1)} %get-tuple-element.67.upper, f32[128,64]{1,0:T(8,128)S(1)} %get-tuple-element.68.chosen, ...), custom_call_target="tpu_custom_call" | custom-call | tf_op jit(solution)/shard_map/final/pallas_call | solution.py:657
  (8 shorter events, 0.1 us)
Async XLA Ops:
  0.6 26.6 %collective-permute-start.4 = (bf16[256,1536]{1,0:T(8,128)(2,1)}, bf16[256,1536]{1,0:T(8,128)(2,1)S(1)}, u32[]{:S(2)}, u32[]{:S(2)}) collective-permute-start(bf16[256,1536]{1,0:T(8,128)(2,1)} %forward.3), channel_id=1, source_target_pairs={{0,16},{4,20},{8,24},{12,28},{16,0},{20,4},{24,8},{28,12},{1,17},{... | collective-permute-start | bytes 2359304 | tf_op jit(solution)/shard_map/ppermute | solution.py:455
  4.7 4.4 %copy-start = (s32[2048]{0:T(1024)S(1)}, s32[2048]{0:T(1024)}, u32[]{:S(2)}) copy-start(s32[2048]{0:T(1024)} %param.16) | copy-start | bytes 24580
  6.1 6.4 %collective-permute-start.1 = (bf16[320,128]{1,0:T(8,128)(2,1)S(1)}, bf16[320,128]{1,0:T(8,128)(2,1)S(1)}, u32[]{:S(2)}, u32[]{:S(2)}) collective-permute-start(bf16[320,128]{1,0:T(8,128)(2,1)S(1)} %get-tuple-element.79), channel_id=1, source_target_pairs={{0,1},{1,0},{2,3},{3,2},{4,5},{5,4},{6,7},{7,6},{8,9},{9,8},{10,11... | collective-permute-start | bytes 245768 | tf_op jit(solution)/shard_map/ppermute | solution.py:444
  7.7 4.7 %collective-permute-start = (bf16[320,128]{1,0:T(8,128)(2,1)S(1)}, bf16[320,128]{1,0:T(8,128)(2,1)S(1)}, u32[]{:S(2)}, u32[]{:S(2)}) collective-permute-start(bf16[320,128]{1,0:T(8,128)(2,1)S(1)} %get-tuple-element.80), channel_id=1, source_target_pairs={{1,2},{2,1},{5,6},{6,5},{9,10},{10,9},{13,14},{14,13},{17,18},{18,... | collective-permute-start | bytes 245768 | tf_op jit(solution)/shard_map/ppermute | solution.py:445
  13.5 3.7 %collective-permute-start.3 = (bf16[16,2304]{1,0:T(8,128)(2,1)S(1)}, bf16[16,2304]{1,0:T(8,128)(2,1)S(1)}, u32[]{:S(2)}, u32[]{:S(2)}) collective-permute-start(bf16[16,2304]{1,0:T(8,128)(2,1)S(1)} %get-tuple-element.83), channel_id=1, source_target_pairs={{0,4},{4,0},{8,12},{12,8},{16,20},{20,16},{24,28},{28,24},{1,5},{5... | collective-permute-start | bytes 221192 | tf_op jit(solution)/shard_map/ppermute | solution.py:444
  13.6 5.3 %collective-permute-start.2 = (bf16[16,2304]{1,0:T(8,128)(2,1)S(1)}, bf16[16,2304]{1,0:T(8,128)(2,1)S(1)}, u32[]{:S(2)}, u32[]{:S(2)}) collective-permute-start(bf16[16,2304]{1,0:T(8,128)(2,1)S(1)} %get-tuple-element.84), channel_id=1, source_target_pairs={{4,8},{12,16},{20,24},{28,0},{8,4},{16,12},{24,20},{0,28},{5,9},{1... | collective-permute-start | bytes 221192 | tf_op jit(solution)/shard_map/ppermute | solution.py:445
  15.1 12.2 %collective-permute-start.5 = (bf16[64,1536]{1,0:T(8,128)(2,1)S(1)}, bf16[64,1536]{1,0:T(8,128)(2,1)S(1)}, u32[]{:S(2)}, u32[]{:S(2)}) collective-permute-start(bf16[64,1536]{1,0:T(8,128)(2,1)S(1)} %get-tuple-element.38.ends.own_ends), channel_id=1, source_target_pairs={{0,16},{4,20},{8,24},{12,28},{16,0},{20,4},{24,8},{28,12},{1,17},{... | collective-permute-start | bytes 589832 | tf_op jit(solution)/shard_map/ppermute | solution.py:455
  16.6 17.1 %collective-permute-start.8 = (bf16[192,768]{1,0:T(8,128)(2,1)S(1)}, bf16[192,768]{1,0:T(8,128)(2,1)S(1)}, u32[]{:S(2)}, u32[]{:S(2)}) collective-permute-start(bf16[192,768]{1,0:T(8,128)(2,1)S(1)} %get-tuple-element.55), channel_id=1, source_target_pairs={{0,16},{4,20},{8,24},{12,28},{16,0},{20,4},{24,8},{28,12},{1,17},{... | collective-permute-start | bytes 884744 | tf_op jit(solution)/shard_map/ppermute | solution.py:455
  19.9 17.6 %collective-permute-start.9 = (bf16[240,384]{1,0:T(8,128)(2,1)S(1)}, bf16[240,384]{1,0:T(8,128)(2,1)S(1)}, u32[]{:S(2)}, u32[]{:S(2)}) collective-permute-start(bf16[240,384]{1,0:T(8,128)(2,1)S(1)} %get-tuple-element.56), channel_id=1, source_target_pairs={{0,16},{4,20},{8,24},{12,28},{16,0},{20,4},{24,8},{28,12},{1,17},{... | collective-permute-start | bytes 552968 | tf_op jit(solution)/shard_map/ppermute | solution.py:455
  20.1 19.8 %collective-permute-start.10 = (bf16[192,384]{1,0:T(8,128)(2,1)S(1)}, bf16[192,384]{1,0:T(8,128)(2,1)S(1)}, u32[]{:S(2)}, u32[]{:S(2)}) collective-permute-start(bf16[192,384]{1,0:T(8,128)(2,1)S(1)} %get-tuple-element.62), channel_id=1, source_target_pairs={{0,16},{4,20},{8,24},{12,28},{16,0},{20,4},{24,8},{28,12},{1,17},{... | collective-permute-start | bytes 442376 | tf_op jit(solution)/shard_map/ppermute | solution.py:455
  27.4 5.8 %collective-permute-start.7 = (bf16[48,1536]{1,0:T(8,128)(2,1)S(1)}, bf16[48,1536]{1,0:T(8,128)(2,1)S(1)}, u32[]{:S(2)}, u32[]{:S(2)}) collective-permute-start(bf16[48,1536]{1,0:T(8,128)(2,1)S(1)} %get-tuple-element.75), channel_id=1, source_target_pairs={{0,4},{4,0},{8,12},{12,8},{16,20},{20,16},{24,28},{28,24},{1,5},{5... | collective-permute-start | bytes 442376 | tf_op jit(solution)/shard_map/ppermute | solution.py:444
  27.4 6.2 %collective-permute-start.6 = (bf16[48,1536]{1,0:T(8,128)(2,1)S(1)}, bf16[48,1536]{1,0:T(8,128)(2,1)S(1)}, u32[]{:S(2)}, u32[]{:S(2)}) collective-permute-start(bf16[48,1536]{1,0:T(8,128)(2,1)S(1)} %get-tuple-element.76), channel_id=1, source_target_pairs={{4,8},{12,0},{20,24},{28,16},{8,4},{0,12},{24,20},{16,28},{5,9},{1... | collective-permute-start | bytes 442376 | tf_op jit(solution)/shard_map/ppermute | solution.py:445
  40.8 6.7 %collective-permute-start.11 = (f32[8,384]{1,0:T(8,128)S(1)}, f32[8,384]{1,0:T(8,128)S(1)}, u32[]{:S(2)}, u32[]{:S(2)}) collective-permute-start(f32[8,384]{1,0:T(8,128)S(1)} %constant_dynamic-update-slice_fusion.rest_0_), channel_id=1, source_target_pairs={{0,1},{1,2},{2,3},{3,0},{4,5},{5,6},{6,7},{7,4},{8,9},{9,10},{10,1... | collective-permute-start | bytes 36872 | tf_op jit(solution)/shard_map/ppermute | solution.py:655
  42.7 4.8 %collective-permute-start.12 = (f32[8,384]{1,0:T(8,128)S(1)}, f32[8,384]{1,0:T(8,128)S(1)}, u32[]{:S(2)}, u32[]{:S(2)}) collective-permute-start(f32[8,384]{1,0:T(8,128)S(1)} %constant_dynamic-update-slice_fusion.rest_0_), channel_id=1, source_target_pairs={{0,2},{1,3},{2,0},{3,1},{4,6},{5,7},{6,4},{7,5},{8,10},{9,11},{10,... | collective-permute-start | bytes 36872 | tf_op jit(solution)/shard_map/ppermute | solution.py:655
  45.2 3.7 %collective-permute-start.13 = (f32[8,384]{1,0:T(8,128)S(1)}, f32[8,384]{1,0:T(8,128)S(1)}, u32[]{:S(2)}, u32[]{:S(2)}) collective-permute-start(f32[8,384]{1,0:T(8,128)S(1)} %constant_dynamic-update-slice_fusion.rest_0_), channel_id=1, source_target_pairs={{0,3},{1,0},{2,1},{3,2},{4,7},{5,4},{6,5},{7,6},{8,11},{9,8},{10,9... | collective-permute-start | bytes 36872 | tf_op jit(solution)/shard_map/ppermute | solution.py:655

commit v7 on v6

--- a/solution.py
+++ b/solution.py
@@ -70,20 +70,29 @@
     copy_all(moves, sem)
 
 
-def nadir_lines_kernel(lines, cols, nadir, from_left, from_right, bands, first, last, sem):
-    moves = []
-    whole = cols + 2 * TILE
-    for out, row, tile in ((first, 0, 0), (last, lines - NADIR_RIM, lines // TILE - 1)):
-        span = pl.ds(row, NADIR_RIM)
-        moves.append((from_left.at[span, :], out.at[:, pl.ds(0, TILE)]))
-        moves.append((nadir.at[span, :], out.at[:, pl.ds(TILE, cols)]))
-        moves.append((from_right.at[span, :], out.at[:, pl.ds(TILE + cols, TILE)]))
-        for n, near in enumerate((from_left, from_right)):
+def nadir_lines_kernel(
+    lines, cols, nadir, from_left, from_right, bands, first, last, stage, sem
+):
+    starts = (0, lines - NADIR_RIM)
+    copy_all(
+        [(nadir.at[pl.ds(row, NADIR_RIM), :], stage.at[n]) for n, row in enumerate(starts)], sem
+    )
+    fold = (cols + 2 * TILE) // 2
+    for n, (out, row) in enumerate(zip((first, last), starts)):
+        span = slice(row, row + NADIR_RIM)
+        long = jnp.concatenate([from_left[span, :], stage[n], from_right[span, :]], axis=1)
+        long = long.astype(jnp.float32)
+        long = long[:LESS] if n == 0 else long[NADIR_RIM - LESS :]
+        tile = n * (lines // TILE - 1)
+        parts = []
+        for near in (from_left, from_right):
             for s in range(2):
                 at = lines + (s * (lines // TILE) + tile) * EDGE
-                target = pl.ds(whole + (2 * n + s) * TILE, TILE)
-                moves.append((near.at[pl.ds(at, EDGE), :], out.at[:, target]))
-    copy_all(moves, sem)
+                parts.append(near[at : at + EDGE, :].astype(jnp.float32))
+        upper = [long[:, :fold], parts[0][EDGE - LESS :], parts[2][:LESS], parts[3][:LESS]]
+        lower = [long[:, fold:], parts[1][EDGE - LESS :], parts[2][LESS:], parts[3][LESS:]]
+        both = [jnp.concatenate(half, axis=1) for half in (upper, lower)]
+        out[...] = jnp.concatenate(both, axis=0).astype(jnp.bfloat16)
 
 
 def late_kernel(
@@ -97,21 +106,25 @@
         (backward.at[body, pl.ds(cuts[0], width)], second.at[pl.ds(0, height), :]),
         (backward.at[body, pl.ds(cuts[1], cols - cuts[1])], third),
     ]
+    fold = whole // 2
     lane = lax.broadcasted_iota(jnp.int32, (EDGE, TILE), 1)
-    kinds = []
-    for k in range(4):
-        near = (from_left, from_right)[k // 2]
+    blocks = []
+    for n in range(3):
+        here = slice(fold + n * TILE, fold + (n + 1) * TILE)
+        ahead, behind = (ref[:, here].astype(jnp.float32) for ref in (above, below))
         tiles = []
         for tile in range(lines // TILE):
-            at = lines + (k % 2 * (lines // TILE) + tile) * EDGE
-            tiles.append(near[at : at + EDGE, :].astype(jnp.float32))
-        here = slice(whole + k * TILE, whole + (k + 1) * TILE)
-        ahead = above[:, here].astype(jnp.float32)
-        behind = below[:, here].astype(jnp.float32)
+            at = lines + tile * EDGE
+            if n == 0:
+                pair = [at + EDGE - LESS, at + lines // TILE * EDGE + EDGE - LESS]
+                held = [from_left[k - LESS : k + LESS, :].astype(jnp.float32)[LESS:] for k in pair]
+                tiles.append(jnp.concatenate(held, axis=0))
+            else:
+                at += (n - 1) * (lines // TILE) * EDGE
+                tiles.append(from_right[at : at + EDGE, :].astype(jnp.float32))
         tiles.append(jnp.where(lane < TILE // 2, behind, ahead))
-        kinds.append(jnp.concatenate(tiles, axis=1))
-    left = jnp.concatenate([kind[EDGE - LESS :] for kind in kinds[:2]], axis=0)
-    for n, block in enumerate((left, *kinds[2:])):
+        blocks.append(jnp.concatenate(tiles, axis=1))
+    for n, block in enumerate(blocks):
         row = height + n * EDGE
         second[row : row + EDGE, : lines + TILE] = block.astype(jnp.bfloat16)
     if width > lines + TILE:
@@ -148,8 +161,14 @@
 ):
     tall = lines + 2 * NADIR_RIM
     rows = lines + 16
-    framed[0:NADIR_RIM, :] = above[:, 0 : cols + 2 * TILE]
-    framed[NADIR_RIM + lines : tall, :] = below[:, 0 : cols + 2 * TILE]
+    fold = (cols + 2 * TILE) // 2
+    blank = jnp.zeros((NADIR_RIM - LESS, 2 * fold), jnp.float32)
+    before, behind = (
+        jnp.concatenate([held[:LESS, :fold], held[LESS:, :fold]], axis=1)
+        for held in (above[...].astype(jnp.float32), below[...].astype(jnp.float32))
+    )
+    framed[0:NADIR_RIM, :] = jnp.concatenate([blank, before], axis=0).astype(jnp.bfloat16)
+    framed[NADIR_RIM + lines : tall, :] = jnp.concatenate([behind, blank], axis=0).astype(jnp.bfloat16)
     framed[NADIR_RIM : NADIR_RIM + lines, 0:TILE] = left[0:lines, :]
     framed[NADIR_RIM : NADIR_RIM + lines, TILE : TILE + cols] = nadir[...]
     framed[NADIR_RIM : NADIR_RIM + lines, TILE + cols :] = right[0:lines, :]
@@ -531,13 +550,19 @@
         hbm(cross_weights),
     )
     line_bands, col_bands, levers, basis, rows_basis, upper, chosen, flags = bands
-    first_lines, last_lines = mover(
+    folded = (NADIR_RIM, whole // 2 + 3 * TILE)
+    first_lines, last_lines = pl.pallas_call(
         functools.partial(nadir_lines_kernel, lines, cols),
-        "nadir_lines",
-        ((NADIR_RIM, whole + 4 * TILE), (NADIR_RIM, whole + 4 * TILE)),
-        (hbm(nadir_view), from_left, from_right, line_bands),
-        14,
-    )
+        out_shape=(jax.ShapeDtypeStruct(folded, bf16),) * 2,
+        in_specs=[any_space, vmem, vmem, any_space],
+        out_specs=(vmem, vmem),
+        scratch_shapes=[pltpu.VMEM((2, NADIR_RIM, cols), bf16), pltpu.SemaphoreType.DMA((2,))],
+        compiler_params=limit,
+        cost_estimate=pl.CostEstimate(
+            flops=0, bytes_accessed=16 * NADIR_RIM * cols, transcendentals=0
+        ),
+        name="nadir_lines",
+    )(hbm(nadir_view), from_left, from_right, line_bands)
     nadir_above, nadir_below = swap("along", whole_ring, even_along, first_lines, last_lines)
 
     most_lines = 3 * LINE_RIM // 2

time: 50.2 us -> 49.9 us (level)
    pallas_call x3 -> x2, Pallas kernels: 3.32 us -> 2.36 us  [mover(): pl.pallas_call(kernel, out_shape=tuple((jax.ShapeDtypeStruct(shape, bf16)...]
    pallas_call x0 -> x1, Pallas kernels: none -> 0.86 us  [local(): pl.pallas_call(functools.partial(nadir_lines_kernel, lines, cols), out_sh...]
    ppermute x3, waiting for transfers between devices: 2.22 us -> 1.47 us  [swap(): far = lax.ppermute(jnp.where(even, to_before, to_behind), axis, both)]
where the time goes in v7:
time: 49.9 us; the launch traced here: 49.5 us
  starting transfers between devices  19.1 us (38%)
  Pallas kernels  18.3 us (37%)
  waiting for transfers between devices  10.5 us (21%)
  between operations  1.5 us (3%)
    ppermute x5, waiting for transfers between devices, over(): return lax.ppermute(value, 'along', across)  7.53 us
    ppermute x5, starting transfers between devices, over(): return lax.ppermute(value, 'along', across)  7.16 us
    ppermute x3, starting transfers between devices, local(): shares.append(lax.ppermute(share, 'cross', pairs))  5.78 us
    pallas_call x3, Pallas kernels, run(): pl.pallas_call(functools.partial(slab_kernel, lines, cols, cuts, jobs, le...  5.27 us
    ppermute x3, starting transfers between devices, swap(): far = lax.ppermute(jnp.where(even, to_before, to_behind), axis, both)  4.33 us
    pallas_call x1, Pallas kernels, local(): pl.pallas_call(functools.partial(prep_kernel, lines, cols, total_cols), o...  3.62 us
    pallas_call x1, Pallas kernels, local(): pl.pallas_call(functools.partial(bands_kernel, lines, cols, total_lines,...  3.3 us
    pallas_call x2, Pallas kernels, mover(): pl.pallas_call(kernel, out_shape=tuple((jax.ShapeDtypeStruct(shape, bf16)...  2.36 us
  transfers between devices with their start and end apart: 14, of which 6 were waited for; matrix products, arithmetic and copies ran while one was open for 0% of the time, Pallas kernels for 33%

profile of v7, /device:TPU:0, one launch (start us, length us, event | category | flops | bytes accessed | tf_op | source)
XLA Modules:
  0.0 49.5 jit_solution(17398967845226048146)
XLA Ops:
  0.6 3.0 %collective-permute-start.4 = (bf16[256,1536]{1,0:T(8,128)(2,1)}, bf16[256,1536]{1,0:T(8,128)(2,1)S(1)}, u32[]{:S(2)}, u32[]{:S(2)}) collective-permute-start(bf16[256,1536]{1,0:T(8,128)(2,1)} %forward.3), channel_id=1, source_target_pairs={{0,16},{4,20},{8,24},{12,28},{16,0},{20,4},{24,8},{28,12},{1,17},{... | collective-permute-start | bytes 2359304 | tf_op jit(solution)/shard_map/ppermute | solution.py:474
  3.7 1.1 %ends.1 = (bf16[64,1536]{1,0:T(8,128)(2,1)S(1)}, bf16[64,1536]{1,0:T(8,128)(2,1)S(1)}) custom-call(bf16[256,1536]{1,0:T(8,128)(2,1)} %forward.3, bf16[256,1536]{1,0:T(8,128)(2,1)} %backward.5), custom_call_target="tpu_custom_call" | custom-call | bytes 786432 | tf_op jit(solution)/shard_map/ends/pallas_call | solution.py:486
  4.7 0.0 copy-start
  4.8 1.3 %cut.1 = (bf16[192,768]{1,0:T(8,128)(2,1)S(1)}, bf16[320,128]{1,0:T(8,128)(2,1)S(1)}, bf16[320,128]{1,0:T(8,128)(2,1)S(1)}) custom-call(bf16[256,1536]{1,0:T(8,128)(2,1)} %nadir.5, bf16[256,1536]{1,0:T(8,128)(2,1)} %forward.3, bf16[256,1536]{1,0:T(8,128)(2,1)} %backward.5, bf16[64,1536]{1,0:T(8,128)(2,1)S(1)} %get-tuple-element.38.ends.own_ends), custom_call_target="tpu_custom_call" | custom-call | bytes 917504 | tf_op jit(solution)/shard_map/cut/pallas_call | solution.py:486
  6.1 1.6 %collective-permute-start.1 = (bf16[320,128]{1,0:T(8,128)(2,1)S(1)}, bf16[320,128]{1,0:T(8,128)(2,1)S(1)}, u32[]{:S(2)}, u32[]{:S(2)}) collective-permute-start(bf16[320,128]{1,0:T(8,128)(2,1)S(1)} %get-tuple-element.79), channel_id=1, source_target_pairs={{0,1},{1,0},{2,3},{3,2},{4,5},{5,4},{6,7},{7,6},{8,9},{9,8},{10,11... | collective-permute-start | bytes 245768 | tf_op jit(solution)/shard_map/ppermute | solution.py:463
  7.7 0.7 %collective-permute-start = (bf16[320,128]{1,0:T(8,128)(2,1)S(1)}, bf16[320,128]{1,0:T(8,128)(2,1)S(1)}, u32[]{:S(2)}, u32[]{:S(2)}) collective-permute-start(bf16[320,128]{1,0:T(8,128)(2,1)S(1)} %get-tuple-element.80), channel_id=1, source_target_pairs={{1,2},{2,1},{5,6},{6,5},{9,10},{10,9},{13,14},{14,13},{17,18},{18,... | collective-permute-start | bytes 245768 | tf_op jit(solution)/shard_map/ppermute | solution.py:464
  9.0 0.1 pad_add_fusion.place
  9.1 0.0 copy-done
  9.1 3.3 %bands.1 = (bf16[2,272,192]{2,1,0:T(8,128)(2,1)S(1)}, bf16[2,288,1536]{2,1,0:T(8,128)(2,1)S(1)}, f32[8,1536]{1,0:T(8,128)S(1)}, f32[256,128]{1,0:T(8,128)S(1)}, ...) custom-call(s32[3]{0:T(128)S(1)} %pad_add_fusion.place, ...), custom_call_target="tpu_custom_call" | custom-call | flops 9216000 | bytes 1843200 | tf_op jit(solution)/shard_map/bands/pallas_call | solution.py:527
  12.4 0.0 collective-permute-done.1
  12.4 0.0 collective-permute-done
  12.5 0.9 %nadir_lines.1 = (bf16[16,1280]{1,0:T(8,128)(2,1)S(1)}, bf16[16,1280]{1,0:T(8,128)(2,1)S(1)}) custom-call(bf16[256,1536]{1,0:T(8,128)(2,1)} %nadir.5, bf16[320,128]{1,0:T(8,128)(2,1)S(1)} %get-tuple-element.78.from_left.left, bf16[320,128]{1,0:T(8,128)(2,1)S(1)} %get-tuple-element.77.from_right.right, bf16[2,272,192]{2,1,0:T(8,128)(2,1)S(1)} %get-tuple-element.41.bands.line_bands), custom_call_target="tpu_custom_call" | custom-call | bytes 393216 | tf_op jit(solution)/shard_map/nadir_lines/pallas_call | solution.py:554
  13.4 0.1 collective-permute-start.3
  13.4 1.5 %collective-permute-start.2 = (bf16[16,1280]{1,0:T(8,128)(2,1)S(1)}, bf16[16,1280]{1,0:T(8,128)(2,1)S(1)}, u32[]{:S(2)}, u32[]{:S(2)}) collective-permute-start(bf16[16,1280]{1,0:T(8,128)(2,1)S(1)} %get-tuple-element.84), channel_id=1, source_target_pairs={{4,8},{12,16},{20,24},{28,0},{8,4},{16,12},{24,20},{0,28},{5,9},{1... | collective-permute-start | bytes 122888 | tf_op jit(solution)/shard_map/ppermute | solution.py:464
  15.0 1.5 %collective-permute-start.5 = (bf16[64,1536]{1,0:T(8,128)(2,1)S(1)}, bf16[64,1536]{1,0:T(8,128)(2,1)S(1)}, u32[]{:S(2)}, u32[]{:S(2)}) collective-permute-start(bf16[64,1536]{1,0:T(8,128)(2,1)S(1)} %get-tuple-element.38.ends.own_ends), channel_id=1, source_target_pairs={{0,16},{4,20},{8,24},{12,28},{16,0},{20,4},{24,8},{28,12},{1,17},{... | collective-permute-start | bytes 589832 | tf_op jit(solution)/shard_map/ppermute | solution.py:474
  16.5 0.5 %collective-permute-start.8 = (bf16[192,768]{1,0:T(8,128)(2,1)S(1)}, bf16[192,768]{1,0:T(8,128)(2,1)S(1)}, u32[]{:S(2)}, u32[]{:S(2)}) collective-permute-start(bf16[192,768]{1,0:T(8,128)(2,1)S(1)} %get-tuple-element.55), channel_id=1, source_target_pairs={{0,16},{4,20},{8,24},{12,28},{16,0},{20,4},{24,8},{28,12},{1,17},{... | collective-permute-start | bytes 884744 | tf_op jit(solution)/shard_map/ppermute | solution.py:474
  17.0 0.0 collective-permute-done.3
  17.0 1.0 %collective-permute-done.2 = bf16[16,1280]{1,0:T(8,128)(2,1)S(1)} collective-permute-done((bf16[16,1280]{1,0:T(8,128)(2,1)S(1)}, bf16[16,1280]{1,0:T(8,128)(2,1)S(1)}, u32[]{:S(2)}, u32[]{:S(2)}) %collective-permute-start.2) | collective-permute-done | bytes 40992 | tf_op jit(solution)/shard_map/ppermute | solution.py:464
  18.1 1.0 %late_cut.1 = (bf16[240,384]{1,0:T(8,128)(2,1)S(1)}, bf16[192,384]{1,0:T(8,128)(2,1)S(1)}) custom-call(bf16[256,1536]{1,0:T(8,128)(2,1)} %backward.5, bf16[320,128]{1,0:T(8,128)(2,1)S(1)} %get-tuple-element.78.from_left.left, bf16[320,128]{1,0:T(8,128)(2,1)S(1)} %get-tuple-element.77.from_right.right, bf16[16,1280]{1,0:T(8,128)(2,1)S(1)} %get-tuple-element.82.above, ...), custom_call_target="tpu_custom_call" | custom-call | bytes 393216 | tf_op jit(solution)/shard_map/late_cut/pallas_call | solution.py:582
  19.1 0.6 %collective-permute-start.9 = (bf16[240,384]{1,0:T(8,128)(2,1)S(1)}, bf16[240,384]{1,0:T(8,128)(2,1)S(1)}, u32[]{:S(2)}, u32[]{:S(2)}) collective-permute-start(bf16[240,384]{1,0:T(8,128)(2,1)S(1)} %get-tuple-element.56), channel_id=1, source_target_pairs={{0,16},{4,20},{8,24},{12,28},{16,0},{20,4},{24,8},{28,12},{1,17},{... | collective-permute-start | bytes 552968 | tf_op jit(solution)/shard_map/ppermute | solution.py:474
  19.6 1.5 %collective-permute-start.10 = (bf16[192,384]{1,0:T(8,128)(2,1)S(1)}, bf16[192,384]{1,0:T(8,128)(2,1)S(1)}, u32[]{:S(2)}, u32[]{:S(2)}) collective-permute-start(bf16[192,384]{1,0:T(8,128)(2,1)S(1)} %get-tuple-element.62), channel_id=1, source_target_pairs={{0,16},{4,20},{8,24},{12,28},{16,0},{20,4},{24,8},{28,12},{1,17},{... | collective-permute-start | bytes 442376 | tf_op jit(solution)/shard_map/ppermute | solution.py:474
  21.2 5.7 %collective-permute-done.5.ends = bf16[64,1536]{1,0:T(8,128)(2,1)S(1)} collective-permute-done((bf16[64,1536]{1,0:T(8,128)(2,1)S(1)}, bf16[64,1536]{1,0:T(8,128)(2,1)S(1)}, u32[]{:S(2)}, u32[]{:S(2)}) %collective-permute-start.5) | collective-permute-done | bytes 196640 | tf_op jit(solution)/shard_map/ppermute | solution.py:474
  26.9 0.0 collective-permute-done.4.lead.rest_0_
  26.9 0.1 lines.1
  27.0 0.1 collective-permute-start.7
  27.1 2.1 %collective-permute-start.6 = (bf16[48,1536]{1,0:T(8,128)(2,1)S(1)}, bf16[48,1536]{1,0:T(8,128)(2,1)S(1)}, u32[]{:S(2)}, u32[]{:S(2)}) collective-permute-start(bf16[48,1536]{1,0:T(8,128)(2,1)S(1)} %get-tuple-element.76), channel_id=1, source_target_pairs={{4,8},{12,0},{20,24},{28,16},{8,4},{0,12},{24,20},{16,28},{5,9},{1... | collective-permute-start | bytes 442376 | tf_op jit(solution)/shard_map/ppermute | solution.py:464
  29.2 3.6 %prep.1 = (f32[272,1536]{1,0:T(8,128)S(1)}, bf16[272,1536]{1,0:T(8,128)(2,1)S(1)}, f32[256,1536]{1,0:T(8,128)S(1)}, f32[256,1536]{1,0:T(8,128)S(1)}, f32[8,256]{1,0:T(8,128)S(1)}) custom-call(s32[3]{0:T(128)S(1)} %pad_add_fusion.place, bf16[256,1536]{1,0:T(8,128)(2,1)} %nadir.5, bf16[320,128]{1,0:T(8,128)(2,1)S(1)} %get-tuple-element.78.from_left.left, ...), custom_call_target="tpu_custom_call" | custom-call | flops 427819008 | bytes 5013504 | tf_op jit(solution)/shard_map/prep/pallas_call | solution.py:597
  32.9 0.0 collective-permute-done.7
  32.9 0.5 collective-permute-done.6
  33.4 0.0 collective-permute-done.8.rest_1_
  33.4 3.0 %inner.1 = (bf16[2,256,1536]{2,1,0:T(8,128)(2,1)}, f32[2,256,128]{2,1,0:T(8,128)S(1)}) custom-call(f32[272,1536]{1,0:T(8,128)S(1)} %get-tuple-element.47.slopes, bf16[272,1536]{1,0:T(8,128)(2,1)S(1)} %get-tuple-element.48.center, f32[256,1536]{1,0:T(8,128)S(1)} %get-tuple-element.49.inverse, f32[256,1536]{1,0:T(8,128)S(1)} %get-tuple-element.50.lever, ...), custom_call_target="tpu_custom_call" | custom-call | flops 1002700800 | bytes 9748480 | tf_op jit(solution)/shard_map/inner/pallas_call | solution.py:634
  36.3 0.8 %collective-permute-done.9.rest_2_ = bf16[240,384]{1,0:T(8,128)(2,1)S(1)} collective-permute-done((bf16[240,384]{1,0:T(8,128)(2,1)S(1)}, bf16[240,384]{1,0:T(8,128)(2,1)S(1)}, u32[]{:S(2)}, u32[]{:S(2)}) %collective-permute-start.9) | collective-permute-done | bytes 184352 | tf_op jit(solution)/shard_map/ppermute | solution.py:474
  37.2 1.4 %second.1 = (bf16[256,384]{1,0:T(8,128)(2,1)S(1)}, bf16[256,128]{1,0:T(8,128)(2,1)S(1)}, bf16[256,128]{1,0:T(8,128)(2,1)S(1)}, bf16[256,128]{1,0:T(8,128)(2,1)S(1)}, f32[2,256,128]{2,1,0:T(8,128)S(1)}) custom-call(f32[272,1536]{1,0:T(8,128)S(1)} %get-tuple-element.47.slopes, bf16[272,1536]{1,0:T(8,128)(2,1)S(1)} %get-tuple-element.48.center, ...), custom_call_target="tpu_custom_call" | custom-call | flops 501350400 | bytes 4177920 | tf_op jit(solution)/shard_map/second/pallas_call | solution.py:634
  38.5 1.0 %collective-permute-done.10.rest_3_ = bf16[192,384]{1,0:T(8,128)(2,1)S(1)} collective-permute-done((bf16[192,384]{1,0:T(8,128)(2,1)S(1)}, bf16[192,384]{1,0:T(8,128)(2,1)S(1)}, u32[]{:S(2)}, u32[]{:S(2)}) %collective-permute-start.10) | collective-permute-done | bytes 147488 | tf_op jit(solution)/shard_map/ppermute | solution.py:474
  39.5 1.0 %third.1 = (bf16[256,512]{1,0:T(8,128)(2,1)S(1)}, f32[8,128]{1,0:T(8,128)S(1)}) custom-call(f32[272,1536]{1,0:T(8,128)S(1)} %get-tuple-element.47.slopes, bf16[272,1536]{1,0:T(8,128)(2,1)S(1)} %get-tuple-element.48.center, f32[256,1536]{1,0:T(8,128)S(1)} %get-tuple-element.49.inverse, f32[256,1536]{1,0:T(8,128)S(1)} %get-tuple-element.50.lever, ...), custom_call_target="tpu_custom_call" | custom-call | flops 376012800 | bytes 2785280 | tf_op jit(solution)/shard_map/third/pallas_call | solution.py:634
  40.5 1.8 %collective-permute-start.11 = (f32[8,384]{1,0:T(8,128)S(1)}, f32[8,384]{1,0:T(8,128)S(1)}, u32[]{:S(2)}, u32[]{:S(2)}) collective-permute-start(f32[8,384]{1,0:T(8,128)S(1)} %constant_dynamic-update-slice_fusion.rest_0_), channel_id=1, source_target_pairs={{0,1},{1,2},{2,3},{3,0},{4,5},{5,6},{6,7},{7,4},{8,9},{9,10},{10,1... | collective-permute-start | bytes 36872 | tf_op jit(solution)/shard_map/ppermute | solution.py:680
  42.3 2.6 %collective-permute-start.12 = (f32[8,384]{1,0:T(8,128)S(1)}, f32[8,384]{1,0:T(8,128)S(1)}, u32[]{:S(2)}, u32[]{:S(2)}) collective-permute-start(f32[8,384]{1,0:T(8,128)S(1)} %constant_dynamic-update-slice_fusion.rest_0_), channel_id=1, source_target_pairs={{0,2},{1,3},{2,0},{3,1},{4,6},{5,7},{6,4},{7,5},{8,10},{9,11},{10,... | collective-permute-start | bytes 36872 | tf_op jit(solution)/shard_map/ppermute | solution.py:680
  44.9 1.4 %collective-permute-start.13 = (f32[8,384]{1,0:T(8,128)S(1)}, f32[8,384]{1,0:T(8,128)S(1)}, u32[]{:S(2)}, u32[]{:S(2)}) collective-permute-start(f32[8,384]{1,0:T(8,128)S(1)} %constant_dynamic-update-slice_fusion.rest_0_), channel_id=1, source_target_pairs={{0,3},{1,0},{2,1},{3,2},{4,7},{5,4},{6,5},{7,6},{8,11},{9,8},{10,9... | collective-permute-start | bytes 36872 | tf_op jit(solution)/shard_map/ppermute | solution.py:680
  46.3 0.9 %store.1 = bf16[2,256,1536]{2,1,0:T(8,128)(2,1)} custom-call(bf16[256,384]{1,0:T(8,128)(2,1)S(1)} %get-tuple-element.58.rest_0_, bf16[256,128]{1,0:T(8,128)(2,1)S(1)} %get-tuple-element.59.rest_1_, bf16[256,128]{1,0:T(8,128)(2,1)S(1)} %get-tuple-element.60.rest_2_, bf16[256,128]{1,0:T(8,128)(2,1)S(1)} %get-tuple-element.61.rest_3_, ...), custom_call_target="tpu_custom_call", output_to_operand_aliasing={{}: (5, {})} | custom-call | bytes 786432 | tf_op jit(solution)/shard_map/store/pallas_call | solution.py:663
  47.1 0.0 collective-permute-done.11.rest_1_
  47.1 0.0 collective-permute-done.12.rest_2_
  47.2 1.4 %collective-permute-done.13.rest_3_ = f32[8,384]{1,0:T(8,128)S(1)} collective-permute-done((f32[8,384]{1,0:T(8,128)S(1)}, f32[8,384]{1,0:T(8,128)S(1)}, u32[]{:S(2)}, u32[]{:S(2)}) %collective-permute-start.13) | collective-permute-done | bytes 12320 | tf_op jit(solution)/shard_map/ppermute | solution.py:680
  48.6 0.9 %final.1 = (f32[1,64,256]{2,1,0:T(8,128)}, f32[1,64]{1,0:T(1,128)}) custom-call(f32[256,128]{1,0:T(8,128)S(1)} %get-tuple-element.53.basis, f32[64,256]{1,0:T(8,128)S(1)} %get-tuple-element.66.rows_basis, f32[8,256]{1,0:T(8,128)S(1)} %get-tuple-element.67.upper, f32[128,64]{1,0:T(8,128)S(1)} %get-tuple-element.68.chosen, ...), custom_call_target="tpu_custom_call" | custom-call | tf_op jit(solution)/shard_map/final/pallas_call | solution.py:682
  (8 shorter events, 0.1 us)
Async XLA Ops:
  0.6 26.3 %collective-permute-start.4 = (bf16[256,1536]{1,0:T(8,128)(2,1)}, bf16[256,1536]{1,0:T(8,128)(2,1)S(1)}, u32[]{:S(2)}, u32[]{:S(2)}) collective-permute-start(bf16[256,1536]{1,0:T(8,128)(2,1)} %forward.3), channel_id=1, source_target_pairs={{0,16},{4,20},{8,24},{12,28},{16,0},{20,4},{24,8},{28,12},{1,17},{... | collective-permute-start | bytes 2359304 | tf_op jit(solution)/shard_map/ppermute | solution.py:474
  4.7 4.4 %copy-start = (s32[2048]{0:T(1024)S(1)}, s32[2048]{0:T(1024)}, u32[]{:S(2)}) copy-start(s32[2048]{0:T(1024)} %param.16) | copy-start | bytes 24580
  6.1 6.4 %collective-permute-start.1 = (bf16[320,128]{1,0:T(8,128)(2,1)S(1)}, bf16[320,128]{1,0:T(8,128)(2,1)S(1)}, u32[]{:S(2)}, u32[]{:S(2)}) collective-permute-start(bf16[320,128]{1,0:T(8,128)(2,1)S(1)} %get-tuple-element.79), channel_id=1, source_target_pairs={{0,1},{1,0},{2,3},{3,2},{4,5},{5,4},{6,7},{7,6},{8,9},{9,8},{10,11... | collective-permute-start | bytes 245768 | tf_op jit(solution)/shard_map/ppermute | solution.py:463
  7.7 4.7 %collective-permute-start = (bf16[320,128]{1,0:T(8,128)(2,1)S(1)}, bf16[320,128]{1,0:T(8,128)(2,1)S(1)}, u32[]{:S(2)}, u32[]{:S(2)}) collective-permute-start(bf16[320,128]{1,0:T(8,128)(2,1)S(1)} %get-tuple-element.80), channel_id=1, source_target_pairs={{1,2},{2,1},{5,6},{6,5},{9,10},{10,9},{13,14},{14,13},{17,18},{18,... | collective-permute-start | bytes 245768 | tf_op jit(solution)/shard_map/ppermute | solution.py:464
  13.4 3.7 %collective-permute-start.3 = (bf16[16,1280]{1,0:T(8,128)(2,1)S(1)}, bf16[16,1280]{1,0:T(8,128)(2,1)S(1)}, u32[]{:S(2)}, u32[]{:S(2)}) collective-permute-start(bf16[16,1280]{1,0:T(8,128)(2,1)S(1)} %get-tuple-element.83), channel_id=1, source_target_pairs={{0,4},{4,0},{8,12},{12,8},{16,20},{20,16},{24,28},{28,24},{1,5},{5... | collective-permute-start | bytes 122888 | tf_op jit(solution)/shard_map/ppermute | solution.py:463
  13.4 4.6 %collective-permute-start.2 = (bf16[16,1280]{1,0:T(8,128)(2,1)S(1)}, bf16[16,1280]{1,0:T(8,128)(2,1)S(1)}, u32[]{:S(2)}, u32[]{:S(2)}) collective-permute-start(bf16[16,1280]{1,0:T(8,128)(2,1)S(1)} %get-tuple-element.84), channel_id=1, source_target_pairs={{4,8},{12,16},{20,24},{28,0},{8,4},{16,12},{24,20},{0,28},{5,9},{1... | collective-permute-start | bytes 122888 | tf_op jit(solution)/shard_map/ppermute | solution.py:464
  15.0 11.9 %collective-permute-start.5 = (bf16[64,1536]{1,0:T(8,128)(2,1)S(1)}, bf16[64,1536]{1,0:T(8,128)(2,1)S(1)}, u32[]{:S(2)}, u32[]{:S(2)}) collective-permute-start(bf16[64,1536]{1,0:T(8,128)(2,1)S(1)} %get-tuple-element.38.ends.own_ends), channel_id=1, source_target_pairs={{0,16},{4,20},{8,24},{12,28},{16,0},{20,4},{24,8},{28,12},{1,17},{... | collective-permute-start | bytes 589832 | tf_op jit(solution)/shard_map/ppermute | solution.py:474
  16.5 16.8 %collective-permute-start.8 = (bf16[192,768]{1,0:T(8,128)(2,1)S(1)}, bf16[192,768]{1,0:T(8,128)(2,1)S(1)}, u32[]{:S(2)}, u32[]{:S(2)}) collective-permute-start(bf16[192,768]{1,0:T(8,128)(2,1)S(1)} %get-tuple-element.55), channel_id=1, source_target_pairs={{0,16},{4,20},{8,24},{12,28},{16,0},{20,4},{24,8},{28,12},{1,17},{... | collective-permute-start | bytes 884744 | tf_op jit(solution)/shard_map/ppermute | solution.py:474
  19.1 18.1 %collective-permute-start.9 = (bf16[240,384]{1,0:T(8,128)(2,1)S(1)}, bf16[240,384]{1,0:T(8,128)(2,1)S(1)}, u32[]{:S(2)}, u32[]{:S(2)}) collective-permute-start(bf16[240,384]{1,0:T(8,128)(2,1)S(1)} %get-tuple-element.56), channel_id=1, source_target_pairs={{0,16},{4,20},{8,24},{12,28},{16,0},{20,4},{24,8},{28,12},{1,17},{... | collective-permute-start | bytes 552968 | tf_op jit(solution)/shard_map/ppermute | solution.py:474
  19.6 19.9 %collective-permute-start.10 = (bf16[192,384]{1,0:T(8,128)(2,1)S(1)}, bf16[192,384]{1,0:T(8,128)(2,1)S(1)}, u32[]{:S(2)}, u32[]{:S(2)}) collective-permute-start(bf16[192,384]{1,0:T(8,128)(2,1)S(1)} %get-tuple-element.62), channel_id=1, source_target_pairs={{0,16},{4,20},{8,24},{12,28},{16,0},{20,4},{24,8},{28,12},{1,17},{... | collective-permute-start | bytes 442376 | tf_op jit(solution)/shard_map/ppermute | solution.py:474
  27.0 5.8 %collective-permute-start.7 = (bf16[48,1536]{1,0:T(8,128)(2,1)S(1)}, bf16[48,1536]{1,0:T(8,128)(2,1)S(1)}, u32[]{:S(2)}, u32[]{:S(2)}) collective-permute-start(bf16[48,1536]{1,0:T(8,128)(2,1)S(1)} %get-tuple-element.75), channel_id=1, source_target_pairs={{0,4},{4,0},{8,12},{12,8},{16,20},{20,16},{24,28},{28,24},{1,5},{5... | collective-permute-start | bytes 442376 | tf_op jit(solution)/shard_map/ppermute | solution.py:463
  27.1 6.2 %collective-permute-start.6 = (bf16[48,1536]{1,0:T(8,128)(2,1)S(1)}, bf16[48,1536]{1,0:T(8,128)(2,1)S(1)}, u32[]{:S(2)}, u32[]{:S(2)}) collective-permute-start(bf16[48,1536]{1,0:T(8,128)(2,1)S(1)} %get-tuple-element.76), channel_id=1, source_target_pairs={{4,8},{12,0},{20,24},{28,16},{8,4},{0,12},{24,20},{16,28},{5,9},{1... | collective-permute-start | bytes 442376 | tf_op jit(solution)/shard_map/ppermute | solution.py:464
  40.5 6.7 %collective-permute-start.11 = (f32[8,384]{1,0:T(8,128)S(1)}, f32[8,384]{1,0:T(8,128)S(1)}, u32[]{:S(2)}, u32[]{:S(2)}) collective-permute-start(f32[8,384]{1,0:T(8,128)S(1)} %constant_dynamic-update-slice_fusion.rest_0_), channel_id=1, source_target_pairs={{0,1},{1,2},{2,3},{3,0},{4,5},{5,6},{6,7},{7,4},{8,9},{9,10},{10,1... | collective-permute-start | bytes 36872 | tf_op jit(solution)/shard_map/ppermute | solution.py:680
  42.3 4.8 %collective-permute-start.12 = (f32[8,384]{1,0:T(8,128)S(1)}, f32[8,384]{1,0:T(8,128)S(1)}, u32[]{:S(2)}, u32[]{:S(2)}) collective-permute-start(f32[8,384]{1,0:T(8,128)S(1)} %constant_dynamic-update-slice_fusion.rest_0_), channel_id=1, source_target_pairs={{0,2},{1,3},{2,0},{3,1},{4,6},{5,7},{6,4},{7,5},{8,10},{9,11},{10,... | collective-permute-start | bytes 36872 | tf_op jit(solution)/shard_map/ppermute | solution.py:680
  44.9 3.7 %collective-permute-start.13 = (f32[8,384]{1,0:T(8,128)S(1)}, f32[8,384]{1,0:T(8,128)S(1)}, u32[]{:S(2)}, u32[]{:S(2)}) collective-permute-start(f32[8,384]{1,0:T(8,128)S(1)} %constant_dynamic-update-slice_fusion.rest_0_), channel_id=1, source_target_pairs={{0,3},{1,0},{2,1},{3,2},{4,7},{5,4},{6,5},{7,6},{8,11},{9,8},{10,9... | collective-permute-start | bytes 36872 | tf_op jit(solution)/shard_map/ppermute | solution.py:680
